TPU v7x, 256 devices: a whole 4x4x8 slice. The times are simulated.
256 devices in a mesh: dp: 4 (over y), fsdp: 64 (over z, x, core).
Axes of the slice: x: 4, y: 4, z: 8, core: 2. Of those that a mesh axis runs over, the one named last changes fastest.
Arguments:
- inputs: bfloat16 [90112, 8192], P(('dp', 'fsdp')), may hold values from -6 to 6
- frozen: bfloat16 [8192, 512], P('fsdp'), may hold values from -0.0625 to 0.0625
- cotangent: bfloat16 [90112, 512], P(('dp', 'fsdp')), may hold values from -48 to 48
- delta_slots: bfloat16 [128, 128, 128], P('fsdp'), may hold values from -0.1796875 to 0.1796875
- slot_tile: int32 [128], P('fsdp'), may hold values from -1 to 255, as said below
- token_count: int32 [256], P(('dp', 'fsdp')), may hold values from 1 to 352, as said below
Outputs:
- projected: bfloat16 [90112, 512], P(('dp', 'fsdp'))
- input_grad: bfloat16 [90112, 8192], P(('dp', 'fsdp'))
- delta_grad: float32 [128, 128, 128], P('fsdp')
Inputs may be any that keep to these rules, and one draw needn't show every extreme that they name: `slot_tile`: slot s belongs to fsdp index s // 2; an index owns its live blocks in its first slots and empty slots hold -1; live tile numbers are distinct; some index has all 2 slots live and some index has none. `token_count`: some device has all 352 rows valid.
All inputs are finite; a program needn't handle non-finite values.
Results may differ from a plain program's by a relative error of at most 0.0046.
Values may be sent and summed in bfloat16 or wider, within the bound.
No kernel may reach another device: no remote copies, remote signals or barrier semaphores. Data moves between devices by JAX's collectives and lax.ppermute only.
A program may use at most 192 MiB of HBM per device.

v0:
```python
import jax
import jax.numpy as jnp
from jax import lax
from jax.sharding import PartitionSpec as P


def per_device(inputs, frozen, cotangent, delta_slots, slot_tile, token_count):
    block_size = delta_slots.shape[1]
    tokens_here = inputs.shape[0]
    model_width = inputs.shape[1]
    heads_width = cotangent.shape[1]
    col_tiles = heads_width // block_size
    row_tiles = model_width // block_size
    row_ids = jnp.arange(tokens_here, dtype=jnp.int32)
    valid_rows = (row_ids < token_count[0])[:, None]
    masked = jnp.where(valid_rows, cotangent, jnp.zeros_like(cotangent))
    token_total = lax.psum(token_count[0].astype(jnp.float32), ("dp", "fsdp"))
    all_deltas, all_tiles = (
        lax.all_gather(delta_slots, "fsdp", axis=0, tiled=True),
        lax.all_gather(slot_tile, "fsdp", axis=0, tiled=True),
    )
    tile_count = row_tiles * col_tiles
    slot_target = jnp.where(all_tiles >= 0, all_tiles, tile_count)
    placed = (
        jnp.zeros((tile_count + 1, block_size, block_size), jnp.bfloat16)
        .at[slot_target]
        .add(all_deltas)[:tile_count]
    )
    delta_dense = (
        placed.reshape(row_tiles, col_tiles, block_size, block_size)
        .transpose(0, 2, 1, 3)
        .reshape(model_width, heads_width)
    )
    contract_cols = (((1,), (1,)), ((), ()))
    effective = (
        lax.all_gather(frozen, "fsdp", axis=0, tiled=True).astype(jnp.float32)
        + delta_dense.astype(jnp.float32)
    ).astype(jnp.bfloat16)
    forward = jnp.dot(inputs, effective, preferred_element_type=jnp.float32)
    backward = lax.dot_general(
        masked, effective, contract_cols, preferred_element_type=jnp.float32
    ).astype(jnp.bfloat16)
    grad_in = backward
    forward, grad_in = (forward, grad_in)
    projected = jnp.where(valid_rows, forward, jnp.zeros_like(forward)).astype(jnp.bfloat16)
    tile_index = jnp.where(all_tiles >= 0, all_tiles, 0)
    x_tiles = jnp.take(
        inputs.reshape(tokens_here, row_tiles, block_size), tile_index // col_tiles, axis=1
    )
    g_tiles = jnp.take(
        masked.reshape(tokens_here, col_tiles, block_size), tile_index % col_tiles, axis=1
    )
    partial_grad = jnp.einsum("tsa,tsb->sab", x_tiles, g_tiles, preferred_element_type=jnp.float32)
    partial_grad = partial_grad * (all_tiles >= 0).astype(jnp.float32)[:, None, None]
    owned_grad = lax.psum_scatter(partial_grad, "fsdp", scatter_dimension=0, tiled=True)
    owned_grad = lax.psum(owned_grad, "dp")
    return (projected, grad_in, owned_grad / token_total)


def solution(mesh):
    in_specs = (
        P(("dp", "fsdp"), None),
        P("fsdp", None),
        P(("dp", "fsdp"), None),
        P("fsdp", None, None),
        P("fsdp"),
        P(("dp", "fsdp")),
    )
    out_specs = (P(("dp", "fsdp"), None), P(("dp", "fsdp"), None), P("fsdp", None, None))
    return jax.shard_map(
        per_device, mesh=mesh, in_specs=in_specs, out_specs=out_specs, check_vma=False
    )
```

profile of v0, /device:TPU:10, one launch (start us, length us, event | category | flops | bytes accessed | tf_op | source)
XLA Modules:
  0.0 483.8 jit_solution(1868448471370399990)
XLA Ops:
  7.2 0.0 reduce-scatter.2.cloned.1.call-start
  7.2 1.3 dynamic-slice
  9.2 0.9 dynamic-update-slice
  10.0 22.5 %all-reduce = s32[128]{0:T(128)S(1)} all-reduce(s32[128]{0:T(128)S(1)} %dynamic-update-slice), channel_id=1, replica_groups=mesh['dp'=4,'fsdp'=64] {'fsdp'}, use_global_device_ids=true, to_apply=%add | all-reduce | flops 128 | bytes 1024
  33.3 6.2 %copy_bitcast_fusion = bf16[352,64,128]{2,0,1:T(8,128)(2,1)} fusion(bf16[352,8192]{1,0:T(8,128)(2,1)} %param.6), kind=kLoop, calls=%fused_computation.14 | loop fusion | bytes 11534336 | tf_op jit(solution)/shard_map/reshape | solution.py:48
  39.4 0.1 copy_bitcast_fusion.1
  39.6 7.9 %gather_fusion.1 = bf16[128,352,128]{2,1,0:T(8,128)(2,1)} fusion(bf16[352,4,128]{2,0,1:T(8,128)(2,1)S(1)} %copy_bitcast_fusion.1, s32[1024]{0:T(1024)S(1)} %pad_clamp_fusion), kind=kCustom, calls=%fused_computation.1 | custom fusion | bytes 23069184 | tf_op jit(solution)/shard_map/jit(_take)/gather | solution.py:50
  47.4 10.4 %gather_fusion = bf16[128,352,128]{2,1,0:T(8,128)(2,1)} fusion(bf16[352,64,128]{2,0,1:T(8,128)(2,1)} %copy_bitcast_fusion, s32[1024]{0:T(1024)S(1)} %pad_clamp_fusion.1), kind=kCustom, calls=%fused_computation | custom fusion | bytes 23069184 | tf_op jit(solution)/shard_map/jit(_take)/gather | solution.py:47
  57.8 12.4 %broadcast_multiply_fusion = f32[128,128,128]{2,1,0:T(8,128)} fusion(f32[128]{0:T(128)S(1)} %get-tuple-element.8, bf16[128,352,128]{2,1,0:T(8,128)(2,1)} %gather_fusion.1, pred[128]{0:T(512)(128)(4,1)S(1)} %get-tuple-element.6, bf16[128,352,128]{2,1,0:T(8,128)(2,1)} %gather_fusion, pred[128]{0:T(512)(128)(4,1)S(1)} %get-tuple-element.3), kind=kOutput, calls=%fused_computation.16 | convolution fusion | flops 1490026496 | bytes 31458048 | tf_op jit(solution)/shard_map/tsa,tsb->sab/dot_general | solution.py:53
  70.2 0.0 all-gather.5.cloned.1.call-start
  70.3 0.7 all-gather.5.cloned.1.call-update
  71.0 146.5 %reduce-scatter.2.cloned.1.call-done = f32[2,128,128]{2,1,0:T(8,128)} async-done(((f32[128,128,128]{2,1,0:T(8,128)}), f32[2,128,128]{2,1,0:T(8,128)}) %reduce-scatter.2.cloned.1.call-update) | async-done | bytes 131088 | tf_op jit(solution)/shard_map/reduce_scatter | solution.py:55
  217.6 0.8 copy.13
  218.4 73.5 %psum.15 = f32[]{:T(128)} all-reduce(f32[]{:T(128)S(6)} %convert_element_type.43), channel_id=1, replica_groups=mesh['dp'=4,'fsdp'=64] {'dp','fsdp'}, use_global_device_ids=true, to_apply=%region_3.4 | all-reduce | flops 1 | bytes 8 | tf_op jit(solution)/shard_map/psum | solution.py:17
  291.9 5.8 %all-gather.5.cloned.1.call-done = bf16[128,128,128]{2,1,0:T(8,128)(2,1)} async-done(((bf16[2,128,128]{2,1,0:T(8,128)(2,1)}), bf16[128,128,128]{2,1,0:T(8,128)(2,1)}) %all-gather.5.cloned.1.call-update) | async-done | bytes 4194320 | tf_op jit(solution)/shard_map/all_gather | solution.py:19
  297.6 5.4 %broadcast_in_dim.58 = bf16[257,128,128]{2,1,0:T(8,128)(2,1)} broadcast(bf16[]{:T(256)} %constant.53.clone.1), dimensions={} | broadcast | bytes 8421378 | tf_op jit(solution)/shard_map/broadcast_in_dim | solution.py:25
  303.0 26.6 %scatter_fusion = bf16[257,128,128]{2,1,0:T(8,128)(2,1)} fusion(bf16[257,128,128]{2,1,0:T(8,128)(2,1)} %broadcast_in_dim.58, s32[128]{0:T(128)S(1)} %compare_select_fusion.2, bf16[128,128,128]{2,1,0:T(8,128)(2,1)} %all-gather.5.cloned.1.call-done), kind=kCustom, calls=%fused_computation.2 | custom fusion | flops 2097152 | bytes 12583424 | tf_op jit(solution)/shard_map/scatter-add | solution.py:27
  329.6 10.4 %slice.8 = bf16[256,128,128]{2,1,0:T(8,128)(2,1)} slice(bf16[257,128,128]{2,1,0:T(8,128)(2,1)} %scatter_fusion), slice={[0:256], [0:128], [0:128]} | slice | bytes 16777216 | tf_op jit(solution)/shard_map/slice | solution.py:25
  340.0 11.2 %convert_bitcast_fusion = f32[64,128,4,128]{3,1,2,0:T(8,128)} fusion(bf16[64,4,128,128]{3,2,1,0:T(8,128)(2,1)} %bitcast.43), kind=kLoop, calls=%fused_computation.5 | loop fusion | flops 4194304 | bytes 25165824 | tf_op jit(solution)/shard_map/convert_element_type | solution.py:37
  351.2 16.7 %copy.14 = f32[64,128,4,128]{1,0,3,2:T(8,128)} copy(f32[64,128,4,128]{3,1,2,0:T(8,128)} %convert_bitcast_fusion) | data formatting | bytes 33554432 | tf_op jit(solution)/shard_map/convert_element_type | solution.py:37
  368.0 2.2 broadcast_divide_fusion
  370.2 64.1 %all-gather.3.cloned.1.call-done = bf16[8192,512]{0,1:T(8,128)(2,1)} async-done(((bf16[128,512]{0,1:T(8,128)(2,1)}), bf16[8192,512]{0,1:T(8,128)(2,1)}) %all-gather.3.cloned.1.call-update) | async-done | bytes 8388624 | tf_op jit(solution)/shard_map/all_gather | solution.py:36
  434.3 21.5 %convolution_convert_fusion = bf16[352,8192]{1,0:T(8,128)(2,1)} fusion(bf16[352,512]{1,0:T(8,128)(2,1)S(1)} %copy-done, pred[352]{0:T(512)(128)(4,1)S(1)} %iota_compare_fusion, f32[64,8,64,128]{3,2,1,0:T(8,128)} %bitcast.41, bf16[8192,512]{0,1:T(8,128)(2,1)} %all-gather.3.cloned.1.call-done), kind=kOutput, calls=%fused_computation.13 | convolution fusion | flops 2968436736 | bytes 31293792 | tf_op jit(solution)/shard_map/dot_general | solution.py:40
  455.8 21.0 %fusion.14 = bf16[352,512]{1,0:T(8,128)(2,1)} fusion(bf16[352,8192]{1,0:T(8,128)(2,1)} %param.6, pred[352]{0:T(512)(128)(4,1)S(1)} %iota_compare_fusion, f32[64,8,64,128]{3,2,1,0:T(8,128)} %bitcast.42, bf16[8192,512]{0,1:T(8,128)(2,1)} %all-gather.3.cloned.1.call-done), kind=kOutput, calls=%fused_computation.19 | convolution fusion | flops 2965733376 | bytes 31293792 | tf_op jit(solution)/shard_map/dot_general | solution.py:39
  (17 shorter events, 0.2 us)
Async XLA Ops:
  7.2 32.2 %copy-start = (bf16[352,512]{1,0:T(8,128)(2,1)S(1)}, bf16[352,512]{1,0:T(8,128)(2,1)}, u32[]{:S(2)}) copy-start(bf16[352,512]{1,0:T(8,128)(2,1)} %param.8) | copy-start | bytes 1081348
  7.2 210.4 %reduce-scatter.2.cloned.1.call-start = ((), (), s32[]{:S(2)}) async-start(), calls=%async_computation.3 | async-start | bytes 8519680 | tf_op jit(solution)/shard_map/reduce_scatter | solution.py:55
  70.2 147.4 %copy-start.1 = (bf16[128,512]{1,0:T(8,128)(2,1)S(1)}, bf16[128,512]{1,0:T(8,128)(2,1)}, u32[]{:S(2)}) copy-start(bf16[128,512]{1,0:T(8,128)(2,1)} %param.7) | copy-start | bytes 393220
  70.2 227.4 %all-gather.5.cloned.1.call-start = ((), (), s32[]{:S(2)}) async-start(), calls=%async_computation.2 | async-start | bytes 4259840 | tf_op jit(solution)/shard_map/all_gather | solution.py:19
  71.0 297.0 %all-reduce.3.cloned.1.call-start = ((), (), s32[]{:S(2)}) async-start(), calls=%async_computation.4 | async-start | bytes 262144 | tf_op jit(solution)/shard_map/psum | solution.py:56
  217.6 216.8 %all-gather.3.cloned.1.call-start = ((), (), s32[]{:S(2)}) async-start(), calls=%async_computation.1 | async-start | bytes 8519680 | tf_op jit(solution)/shard_map/all_gather | solution.py:36
Sparse Core Ops, SparseCore 0:
  70.3 147.1 reduce-scatter.1
  220.7 76.9 all-gather.4
  300.1 43.5 all-reduce.2
  346.7 87.5 all-gather.2
where the time goes:
time: 492 us; the launch traced here: 484 us
  waiting for transfers between devices  217 us (44%)
  blocking collectives  95.9 us (19%)
  local copies, waits for them, and re-layouts  59.8 us (12%)
  matrix products  54.8 us (11%)
  other arithmetic  40.2 us (8%)
  between operations  15.6 us (3%)
    reduce_scatter x1, waiting for transfers between devices, per_device(): lax.psum_scatter(partial_grad, 'fsdp', scatter_dimension=0, tiled=True)  147 us
    psum x1, blocking collectives, per_device(): token_total = lax.psum(token_count[0].astype(jnp.float32), ('dp', 'fsdp'))  73.5 us
    all_gather x1, waiting for transfers between devices, per_device(): lax.all_gather(frozen, 'fsdp', axis=0, tiled=True).astype(jnp.float32)  64.1 us
    scatter-add x1, other arithmetic, per_device(): placed = jnp.zeros((tile_count + 1, block_size, block_size), jnp.bfloat16...  26.6 us
    unnamed x1, blocking collectives  22.5 us
    dot_general x1, matrix products, per_device(): lax.dot_general(masked, effective, contract_cols, preferred_element_type=...  21.5 us
    dot_general x1, matrix products, per_device(): forward = jnp.dot(inputs, effective, preferred_element_type=jnp.float32)  21 us
    convert_element_type x1, local copies, waits for them, and re-layouts, per_device(): delta_dense.astype(jnp.float32)  16.7 us
  transfers between devices with their start and end apart: 4, of which 3 were waited for; matrix products, arithmetic and copies ran while one was open for 15% of the time, Pallas kernels for 0%

commit v1 on v0

v1 whole, which is shorter than its diff:
```python
import functools

import jax
import jax.numpy as jnp
from jax import lax
from jax.experimental import pallas as pl
from jax.experimental.pallas import tpu as pltpu
from jax.sharding import PartitionSpec as P

NZ, NX, NC, NY = 8, 4, 2, 4
BF16, F32 = jnp.bfloat16, jnp.float32
EVEN = (2, 0, -2, 4)
FROM_UP = (3, 1)
FROM_DOWN = (-1, -3)


def fetch(v, dz=0, dx=0, dc=0):
    pairs = []
    for z in range(NZ):
        for x in range(NX):
            for c in range(NC):
                src = ((z + dz) % NZ * NX + (x + dx) % NX) * NC + (c ^ dc)
                pairs.append((src, (z * NX + x) * NC + c))
    return lax.ppermute(v, "fsdp", pairs)


def fetch_y(v, dy):
    return lax.ppermute(v, "dp", [((y + dy) % NY, y) for y in range(NY)])


def params(mib):
    return pltpu.CompilerParams(vmem_limit_bytes=mib * 2**20)


def grad_blocks(ids, pos, x_ref, m_ref, c_rel, emit):
    block = 128
    y, z, x, c = pos[0], pos[1], pos[2], pos[3]
    core = (c + c_rel) % 2

    def one(i, carry):
        xr, zr, k = i // (NZ * 2), (i // 2) % NZ, i % 2
        owner = ((z + zr) % NZ * NX + (x + xr) % NX) * NC + core
        tile = ids[owner * 2 + k]
        live = tile >= 0
        safe = jnp.maximum(tile, 0)
        row = zr * 64 + k * 32

        @pl.when(live)
        def _():
            xt = x_ref[:, pl.ds(pl.multiple_of(safe // 4 * block, block), block)]
            mt = m_ref[:, pl.ds(pl.multiple_of(safe % 4 * block, block), block)]
            part = lax.dot_general(xt, mt, (((0,), (0,)), ((), ())), preferred_element_type=F32)
            for q in range(NY):
                emit((q + NY - y) % NY, xr, pl.multiple_of(row, 32), part[q * 32 : q * 32 + 32])

        @pl.when(jnp.logical_not(live))
        def _():
            for q in range(NY):
                emit(q, xr, pl.multiple_of(row, 32), jnp.zeros((32, block), F32))

        return carry

    lax.fori_loop(0, NX * NZ * 2, one, 0, unroll=2)


def mask_rows(cot_ref, count, m_ref):
    rows = lax.broadcasted_iota(jnp.int32, cot_ref.shape, 0)
    g = cot_ref[...]
    m_ref[...] = jnp.where(rows < count, g, jnp.zeros_like(g))


def grads_away_kernel(ids, pos, x_ref, cot_ref, out_ref, m_ref):
    mask_rows(cot_ref, pos[4], m_ref)

    def emit(q, xr, row, v):
        out_ref[q, xr, pl.ds(row, 32), :] = v.astype(BF16)

    grad_blocks(ids, pos, x_ref, m_ref, 1, emit)


def grads_home_kernel(ids, pos, x_ref, cot_ref, r_ref, h0, h1, h2, h3, m_ref, t_ref):
    mask_rows(cot_ref, pos[4], m_ref)

    def emit(q, xr, row, v):
        t_ref[q, xr, pl.ds(row, 32), :] = v

    grad_blocks(ids, pos, x_ref, m_ref, 0, emit)
    for q, h in enumerate((h0, h1, h2, h3)):
        for xr in range(NX):
            h[xr] = (t_ref[q, xr] + r_ref[q, xr].astype(F32)).astype(h.dtype)


def vmem(n):
    return [pl.BlockSpec(memory_space=pltpu.VMEM)] * n


def smem(n):
    return [pl.BlockSpec(memory_space=pltpu.SMEM)] * n


def grads_away(ids, pos, x, cot):
    return pl.pallas_call(
        grads_away_kernel,
        out_shape=jax.ShapeDtypeStruct((NY, NX, 512, 128), BF16),
        in_specs=smem(2) + vmem(2),
        out_specs=vmem(1)[0],
        scratch_shapes=[pltpu.VMEM(cot.shape, BF16)],
        compiler_params=params(40),
        cost_estimate=pl.CostEstimate(flops=1_500_000_000, bytes_accessed=8_000_000, transcendentals=0),
        name="grads_away",
    )(ids, pos, x, cot)


def grads_home(ids, pos, x, cot, r):
    return pl.pallas_call(
        grads_home_kernel,
        out_shape=[jax.ShapeDtypeStruct((NX, 512, 128), d) for d in (F32, BF16, BF16, BF16)],
        in_specs=smem(2) + vmem(3),
        out_specs=vmem(4),
        scratch_shapes=[pltpu.VMEM(cot.shape, BF16), pltpu.VMEM((NY, NX, 512, 128), F32)],
        compiler_params=params(48),
        cost_estimate=pl.CostEstimate(flops=1_500_000_000, bytes_accessed=10_000_000, transcendentals=0),
        name="grads_home",
    )(ids, pos, x, cot, r)


def sum_y_kernel(a, b, c, d, j0, j1, j2, j3):
    for xr, j in enumerate((j0, j1, j2, j3)):
        s = a[xr] + b[xr].astype(F32) + c[xr].astype(F32) + d[xr].astype(F32)
        j[...] = s.astype(j.dtype)


def sum_y(*parts):
    return pl.pallas_call(
        sum_y_kernel,
        out_shape=[jax.ShapeDtypeStruct((512, 128), d) for d in (F32, BF16, BF16, BF16)],
        in_specs=vmem(4),
        out_specs=vmem(4),
        name="sum_y",
    )(*parts)


def sum_x_kernel(a, b, c, d, *outs):
    for zr, o in enumerate(outs):
        rows = slice(zr * 64, zr * 64 + 64)
        o[...] = a[rows, :] + b[rows, :].astype(F32) + c[rows, :].astype(F32) + d[rows, :].astype(F32)


def sum_x(*parts):
    return pl.pallas_call(
        sum_x_kernel,
        out_shape=[jax.ShapeDtypeStruct((64, 128), F32)] * NZ,
        in_specs=vmem(4),
        out_specs=vmem(NZ),
        name="sum_x",
    )(*parts)


def sum_z_kernel(ids, *refs):
    out = refs[-1]
    total = refs[0][...]
    for r in refs[1:-1]:
        total = total + r[...]
    out[0:64, :] = total
    out[64:72, :] = jnp.full((8, 128), ids[128].astype(F32), F32)


def sum_z(ids, *parts):
    return pl.pallas_call(
        sum_z_kernel,
        out_shape=jax.ShapeDtypeStruct((72, 128), F32),
        in_specs=smem(1) + vmem(NZ),
        out_specs=vmem(1)[0],
        name="sum_z",
    )(ids, *parts)


def finish_kernel(pos, v0, v1, v2, v3, out):
    y = pos[0]
    total = (v0[64:65, :] + v1[64:65, :]) + (v2[64:65, :] + v3[64:65, :])
    for j, v in enumerate((v0, v1, v2, v3)):
        q = (y + j) % NY
        for k in range(2):
            out[k, pl.ds(pl.multiple_of(q * 32, 32), 32), :] = v[k * 32 : k * 32 + 32, :] / total


def finish(pos, *parts):
    return pl.pallas_call(
        finish_kernel,
        out_shape=jax.ShapeDtypeStruct((2, 128, 128), F32),
        in_specs=smem(1) + vmem(4),
        out_specs=vmem(1)[0],
        name="finish",
    )(pos, *parts)


def products_kernel(chunk, ids, pos, x_ref, cot_ref, *refs):
    pieces, (proj_ref, grad_ref, w_ref, d_ref, m_ref, acc_ref, wsem, dsem) = refs[:20], refs[20:]
    step = pl.program_id(0)
    block = 128

    @pl.when(step == 0)
    def _():
        z, x, c = pos[1], pos[2], pos[3]
        copies = []

        def owner(dz, dx, dc):
            return ((z + dz + NZ) % NZ * NX + (x + dx) % NX) * NC + (c + dc) % 2

        def put_w(src, tile):
            rows = pl.ds(pl.multiple_of(tile * block, block), block)
            copies.append(pltpu.make_async_copy(src, w_ref.at[rows, :], wsem.at[len(copies)]))

        for dc in range(2):
            a, zp, zm = pieces[dc * 10 : dc * 10 + 4], pieces[dc * 10 + 4], pieces[dc * 10 + 5]
            for dx in range(NX):
                for i, dz in enumerate(EVEN):
                    put_w(a[dx].at[i], owner(dz, dx, dc))
                for i, dz in enumerate(FROM_UP):
                    put_w(zp.at[dx, i], owner(dz, dx, dc))
                for i, dz in enumerate(FROM_DOWN):
                    put_w(zm.at[dx, i], owner(dz, dx, dc))
        n = 0
        for dc in range(2):
            cs = pieces[dc * 10 + 6 : dc * 10 + 10]
            for dx in range(NX):
                for i, dz in enumerate(EVEN + FROM_UP + FROM_DOWN):
                    slots = pl.ds(owner(dz, dx, dc) * 2, 2)
                    copies.append(pltpu.make_async_copy(cs[dx].at[i], d_ref.at[slots], dsem.at[n]))
                    n += 1
        for copy in copies:
            copy.start()
        mask_rows(cot_ref, pos[4], m_ref)
        acc_ref[...] = jnp.zeros_like(acc_ref)
        for copy in copies:
            copy.wait()

        def add(s, carry):
            tile = ids[s]

            @pl.when(tile >= 0)
            def _():
                at = (
                    pl.ds(pl.multiple_of(tile // 4 * block, block), block),
                    pl.ds(pl.multiple_of(tile % 4 * block, block), block),
                )
                w_ref[at] = (w_ref[at].astype(F32) + d_ref[s].astype(F32)).astype(BF16)

            return carry

        lax.fori_loop(0, 128, add, 0)

    w = w_ref[pl.ds(pl.multiple_of(step * chunk, chunk), chunk), :]
    acc_ref[...] += jnp.dot(x_ref[...], w, preferred_element_type=F32)
    grad_ref[...] = lax.dot_general(
        m_ref[...], w, (((1,), (1,)), ((), ())), preferred_element_type=F32
    ).astype(BF16)

    @pl.when(step == pl.num_programs(0) - 1)
    def _():
        acc = acc_ref[...]
        rows = lax.broadcasted_iota(jnp.int32, acc.shape, 0)
        proj_ref[...] = jnp.where(rows < pos[4], acc, jnp.zeros_like(acc)).astype(BF16)


def products(ids, pos, x, cot, pieces):
    tokens, width = x.shape
    heads = cot.shape[1]
    chunk = 512
    return pl.pallas_call(
        functools.partial(products_kernel, chunk),
        grid=(width // chunk,),
        out_shape=[jax.ShapeDtypeStruct((tokens, heads), BF16), jax.ShapeDtypeStruct((tokens, width), BF16)],
        in_specs=smem(2)
        + [
            pl.BlockSpec((tokens, chunk), lambda i: (0, i)),
            pl.BlockSpec((tokens, heads), lambda i: (0, 0)),
        ]
        + [pl.BlockSpec(memory_space=pl.ANY)] * 20,
        out_specs=[
            pl.BlockSpec((tokens, heads), lambda i: (0, 0)),
            pl.BlockSpec((tokens, chunk), lambda i: (0, i)),
        ],
        scratch_shapes=[
            pltpu.VMEM((width, heads), BF16),
            pltpu.VMEM((128, 128, 128), BF16),
            pltpu.VMEM((tokens, heads), BF16),
            pltpu.VMEM((tokens, heads), F32),
            pltpu.SemaphoreType.DMA((64,)),
            pltpu.SemaphoreType.DMA((64,)),
        ],
        compiler_params=params(32),
        cost_estimate=pl.CostEstimate(flops=6_000_000_000, bytes_accessed=25_000_000, transcendentals=0),
        name="products",
    )(ids, pos, x, cot, *pieces)


def per_device(inputs, frozen, cotangent, delta_slots, slot_tile, token_count):
    f = lax.axis_index("fsdp")
    y = lax.axis_index("dp")
    here = jnp.zeros((256,), jnp.int32)
    here = lax.dynamic_update_slice(here, slot_tile, (2 * f,))
    here = lax.dynamic_update_slice(here, token_count, (128,))

    even = [fetch(frozen, dz=d) if d else frozen for d in EVEN]
    deven = [fetch(delta_slots, dz=d) if d else delta_slots for d in EVEN]
    ids = lax.psum(here, "fsdp")
    pos = jnp.stack([y, f // 8, f // 2 % 4, f % 2, token_count[0]]).astype(jnp.int32)

    away = grads_away(ids, pos, inputs, cotangent)
    back = fetch(away, dc=1)

    a0 = jnp.stack(even)
    a = [a0] + [fetch(a0, dx=d) for d in (1, 2, 3)]
    b0 = jnp.stack(deven)
    up, down = fetch(b0[0:2], dz=1), fetch(b0[1:3], dz=-1)

    h = grads_home(ids, pos, inputs, cotangent, back)
    got = [h[0], fetch_y(h[3], 1), fetch_y(h[2], 2), fetch_y(h[1], -1)]

    c0 = jnp.concatenate([b0, up, down])
    c = [c0] + [fetch(c0, dx=d) for d in (1, 2, 3)]
    zp = fetch(jnp.stack([v[0:2] for v in a]), dz=1)
    zm = fetch(jnp.stack([v[1:3] for v in a]), dz=-1)

    j = sum_y(*got)
    got = [j[0], fetch(j[3], dx=1), fetch(j[2], dx=2), fetch(j[1], dx=-1)]
    t = sum_x(*got)
    q = sum_z(ids, t[0], *[fetch(t[8 - d], dz=d) for d in range(1, 8)])
    owned = finish(pos, q, *[fetch_y(q, d) for d in (1, 2, 3)])

    mine = [*a, zp, zm, *c]
    pieces = mine + [fetch(v, dc=1) for v in mine]
    projected, grad_in = products(ids, pos, inputs, cotangent, pieces)
    return projected, grad_in, owned


def solution(mesh):
    in_specs = (
        P(("dp", "fsdp"), None),
        P("fsdp", None),
        P(("dp", "fsdp"), None),
        P("fsdp", None, None),
        P("fsdp"),
        P(("dp", "fsdp")),
    )
    out_specs = (P(("dp", "fsdp"), None), P(("dp", "fsdp"), None), P("fsdp", None, None))
    return jax.shard_map(per_device, mesh=mesh, in_specs=in_specs, out_specs=out_specs, check_vma=False)
```

time: 492 us -> 224 us (0.46)
  the two profiles are of different devices: /device:TPU:10 before, /device:TPU:1 now
where the time goes in v1:
time: 224 us; the launch traced here: 222 us
  starting transfers between devices  83.1 us (37%)
  Pallas kernels  55.1 us (25%)
  waiting for transfers between devices  52.9 us (24%)
  blocking collectives  15.6 us (7%)
  local copies, waits for them, and re-layouts  11.5 us (5%)
  other arithmetic  2.34 us (1%)
    ppermute x37, starting transfers between devices, fetch(): return lax.ppermute(v, 'fsdp', pairs)  73.4 us
    ppermute x37, waiting for transfers between devices, fetch(): return lax.ppermute(v, 'fsdp', pairs)  31.2 us
    pallas_call x1, Pallas kernels, products(): pl.pallas_call(functools.partial(products_kernel, chunk), grid=(width //...  23.3 us
    ppermute x6, waiting for transfers between devices, fetch_y(): return lax.ppermute(v, 'dp', [((y + dy) % NY, y) for y in range(NY)])  21.8 us
    psum x1, blocking collectives, per_device(): ids = lax.psum(here, 'fsdp')  15.6 us
    pallas_call x1, Pallas kernels, grads_home(): pl.pallas_call(grads_home_kernel, out_shape=[jax.ShapeDtypeStruct((NX, 51...  12.9 us
    pallas_call x1, Pallas kernels, grads_away(): pl.pallas_call(grads_away_kernel, out_shape=jax.ShapeDtypeStruct((NY, NX,...  11.5 us
    unnamed x39, local copies, waits for them, and re-layouts  10.4 us
  transfers between devices with their start and end apart: 43, of which 10 were waited for; matrix products, arithmetic and copies ran while one was open for 2% of the time, Pallas kernels for 24%

profile of v1, /device:TPU:1, one launch (start us, length us, event | category | flops | bytes accessed | tf_op | source)
XLA Modules:
  0.0 222.0 jit_solution(14709748727054487580)
XLA Ops:
  0.6 6.9 %collective-permute-start.8 = (bf16[2,128,128]{2,1,0:T(8,128)(2,1)}, bf16[2,128,128]{2,1,0:T(8,128)(2,1)S(1)}, u32[]{:S(2)}, u32[]{:S(2)}) collective-permute-start(bf16[2,128,128]{2,1,0:T(8,128)(2,1)} %param.9), channel_id=1, source_target_pairs={{16,0},{17,1},{18,2},{19,3},{20,4},{21,5},{22,6},{23,7},{24,8},{25... | collective-permute-start | bytes 196616 | tf_op jit(solution)/shard_map/ppermute | solution.py:24
  12.1 4.4 %collective-permute-start.2 = (bf16[128,512]{1,0:T(8,128)(2,1)}, bf16[128,512]{1,0:T(8,128)(2,1)S(1)}, u32[]{:S(2)}, u32[]{:S(2)}) collective-permute-start(bf16[128,512]{1,0:T(8,128)(2,1)} %param.7), channel_id=1, source_target_pairs={{32,0},{33,1},{34,2},{35,3},{36,4},{37,5},{38,6},{39,7},{40,8},{41... | collective-permute-start | bytes 393224 | tf_op jit(solution)/shard_map/ppermute | solution.py:24
  18.1 15.6 %psum.7.ids = s32[256]{0:T(256)S(1)} all-reduce(s32[256]{0:T(256)S(1)} %constant_dynamic-update-slice_fusion.5), channel_id=1, replica_groups=mesh['dp'=4,'fsdp'=64] {'fsdp'}, use_global_device_ids=true, to_apply=%region_0.0 | all-reduce | flops 256 | bytes 2048 | tf_op jit(solution)/shard_map/psum | solution.py:307
  33.7 2.6 %copy-done = bf16[352,8192]{1,0:T(8,128)(2,1)S(1)} copy-done((bf16[352,8192]{1,0:T(8,128)(2,1)S(1)}, bf16[352,8192]{1,0:T(8,128)(2,1)}, u32[]{:S(2)}) %copy-start) | copy-done | bytes 5767192
  37.3 11.5 %grads_away.1 = bf16[4,4,512,128]{3,2,1,0:T(8,128)(2,1)S(1)} custom-call(s32[256]{0:T(256)S(1)} %psum.7.ids, s32[5]{0:T(128)S(1)} %stack.85.pos, bf16[352,8192]{1,0:T(8,128)(2,1)S(1)} %copy-done, bf16[352,512]{1,0:T(8,128)(2,1)S(1)} %copy-done.2), custom_call_target="tpu_custom_call" | custom-call | flops 1500000000 | bytes 8000000 | tf_op jit(solution)/shard_map/grads_away/pallas_call | solution.py:102
  48.8 3.2 %collective-permute-start.26 = (bf16[4,4,512,128]{3,2,1,0:T(8,128)(2,1)S(1)}, bf16[4,4,512,128]{3,2,1,0:T(8,128)(2,1)S(1)}, u32[]{:S(2)}, u32[]{:S(2)}) collective-permute-start(bf16[4,4,512,128]{3,2,1,0:T(8,128)(2,1)S(1)} %grads_away.1), channel_id=1, source_target_pairs={{1,0},{0,1},{3,2},{2,3},{5,4},{4,5},{7,6},{6,7},{9,8},{8,9},{11,10... | collective-permute-start | bytes 6291464 | tf_op jit(solution)/shard_map/ppermute | solution.py:24
  56.5 4.5 %collective-permute-done.1 = bf16[128,512]{1,0:T(8,128)(2,1)S(1)} collective-permute-done((bf16[128,512]{1,0:T(8,128)(2,1)S(1)}, bf16[128,512]{1,0:T(8,128)(2,1)S(1)}, u32[]{:S(2)}, u32[]{:S(2)}) %collective-permute-start.1) | collective-permute-done | bytes 131104 | tf_op jit(solution)/shard_map/ppermute | solution.py:24
  63.2 2.7 %collective-permute-start.16 = (bf16[4,128,512]{2,1,0:T(8,128)(2,1)S(1)}, bf16[4,128,512]{2,1,0:T(8,128)(2,1)S(1)}, u32[]{:S(2)}, u32[]{:S(2)}) collective-permute-start(bf16[4,128,512]{2,1,0:T(8,128)(2,1)S(1)} %pad_maximum_fusion.2.refs_0_), channel_id=1, source_target_pairs={{1,0},{0,1},{3,2},{2,3},{5,4},{4,5},{7,6},{6,7},{9,8},{8,9},{11,10... | collective-permute-start | bytes 1572872 | tf_op jit(solution)/shard_map/ppermute | solution.py:24
  67.3 9.1 %collective-permute-done.5.refs_3_ = bf16[4,128,512]{2,1,0:T(8,128)(2,1)S(1)} collective-permute-done((bf16[4,128,512]{2,1,0:T(8,128)(2,1)S(1)}, bf16[4,128,512]{2,1,0:T(8,128)(2,1)S(1)}, u32[]{:S(2)}, u32[]{:S(2)}) %collective-permute-start.5) | collective-permute-done | bytes 524320 | tf_op jit(solution)/shard_map/ppermute | solution.py:24
  76.4 11.5 %collective-permute-start.22 = (bf16[8,2,128,128]{3,2,1,0:T(8,128)(2,1)S(1)}, bf16[8,2,128,128]{3,2,1,0:T(8,128)(2,1)S(1)}, u32[]{:S(2)}, u32[]{:S(2)}) collective-permute-start(bf16[8,2,128,128]{3,2,1,0:T(8,128)(2,1)S(1)} %constant_dynamic-update-slice_fusion.refs_6_), channel_id=1, source_target_pairs={{1,0},{0,1},{3,2},{2,3},{5,4},{4,5},{7,6},{6,7},{9,8},{8,9},{11,10... | collective-permute-start | bytes 1572872 | tf_op jit(solution)/shard_map/ppermute | solution.py:24
  89.2 2.7 %collective-permute-start.6 = (bf16[4,2,128,512]{3,2,1,0:T(8,128)(2,1)}, bf16[4,2,128,512]{3,2,1,0:T(8,128)(2,1)}, u32[]{:S(2)}, u32[]{:S(2)}) collective-permute-start(bf16[4,2,128,512]{3,2,1,0:T(8,128)(2,1)} %pad_maximum_fusion), channel_id=1, source_target_pairs={{8,0},{9,1},{10,2},{11,3},{12,4},{13,5},{14,6},{15,7},{16,8},{17,9... | collective-permute-start | bytes 3145736 | tf_op jit(solution)/shard_map/ppermute | solution.py:24
  91.9 12.9 %grads_home.1 = (f32[4,512,128]{2,1,0:T(8,128)S(1)}, bf16[4,512,128]{2,1,0:T(8,128)(2,1)S(1)}, bf16[4,512,128]{2,1,0:T(8,128)(2,1)S(1)}, bf16[4,512,128]{2,1,0:T(8,128)(2,1)S(1)}) custom-call(s32[256]{0:T(256)S(1)} %psum.7.ids, s32[5]{0:T(128)S(1)} %stack.85.pos, bf16[352,8192]{1,0:T(8,128)(2,1)} %x_ref.5, bf16[352,512]{1,0:T(8,128)(2,1)S(1)} %copy-done.3, ...), custom_call_target="tpu_custom_call" | custom-call | flops 1500000000 | bytes 10000000 | tf_op jit(solution)/shard_map/grads_home/pallas_call | solution.py:115
  105.7 2.7 %collective-permute-start.27 = (bf16[4,512,128]{2,1,0:T(8,128)(2,1)S(1)}, bf16[4,512,128]{2,1,0:T(8,128)(2,1)S(1)}, u32[]{:S(2)}, u32[]{:S(2)}) collective-permute-start(bf16[4,512,128]{2,1,0:T(8,128)(2,1)S(1)} %get-tuple-element.24), channel_id=1, source_target_pairs={{64,0},{128,64},{192,128},{0,192},{65,1},{129,65},{193,129},{1,193... | collective-permute-start | bytes 1572872 | tf_op jit(solution)/shard_map/ppermute | solution.py:28
  111.4 7.4 %collective-permute-done.27.b = bf16[4,512,128]{2,1,0:T(8,128)(2,1)S(1)} collective-permute-done((bf16[4,512,128]{2,1,0:T(8,128)(2,1)S(1)}, bf16[4,512,128]{2,1,0:T(8,128)(2,1)S(1)}, u32[]{:S(2)}, u32[]{:S(2)}) %collective-permute-start.27) | collective-permute-done | bytes 524320 | tf_op jit(solution)/shard_map/ppermute | solution.py:28
  122.7 12.5 %collective-permute-done.29.d = bf16[4,512,128]{2,1,0:T(8,128)(2,1)S(1)} collective-permute-done((bf16[4,512,128]{2,1,0:T(8,128)(2,1)S(1)}, bf16[4,512,128]{2,1,0:T(8,128)(2,1)S(1)}, u32[]{:S(2)}, u32[]{:S(2)}) %collective-permute-start.29) | collective-permute-done | bytes 524320 | tf_op jit(solution)/shard_map/ppermute | solution.py:28
  137.7 2.6 %sum_y.1 = (f32[512,128]{1,0:T(8,128)}, bf16[512,128]{1,0:T(8,128)(2,1)}, bf16[512,128]{1,0:T(8,128)(2,1)}, bf16[512,128]{1,0:T(8,128)(2,1)}) custom-call(f32[4,512,128]{2,1,0:T(8,128)} %copy-done.4, bf16[4,512,128]{2,1,0:T(8,128)(2,1)} %copy-done.10, bf16[4,512,128]{2,1,0:T(8,128)(2,1)} %copy-done.11, bf16[4,512,128]{2,1,0:T(8,128)(2,1)} %copy-done.12), custom_call_target="tpu_custom_call" | custom-call | tf_op jit(solution)/shard_map/sum_y/pallas_call | solution.py:134
  141.1 13.3 %collective-permute-done.13.refs_7_ = bf16[8,2,128,128]{3,2,1,0:T(8,128)(2,1)} collective-permute-done((bf16[8,2,128,128]{3,2,1,0:T(8,128)(2,1)S(1)}, bf16[8,2,128,128]{3,2,1,0:T(8,128)(2,1)}, u32[]{:S(2)}, u32[]{:S(2)}) %collective-permute-start.13) | collective-permute-done | bytes 524320 | tf_op jit(solution)/shard_map/ppermute | solution.py:24
  154.4 2.8 %collective-permute-start.19 = (bf16[4,128,512]{2,1,0:T(8,128)(2,1)S(1)}, bf16[4,128,512]{2,1,0:T(8,128)(2,1)}, u32[]{:S(2)}, u32[]{:S(2)}) collective-permute-start(bf16[4,128,512]{2,1,0:T(8,128)(2,1)S(1)} %collective-permute-done.5.refs_3_), channel_id=1, source_target_pairs={{1,0},{0,1},{3,2},{2,3},{5,4},{4,5},{7,6},{6,7},{9,8},{8,9},{11,10... | collective-permute-start | bytes 1572872 | tf_op jit(solution)/shard_map/ppermute | solution.py:24
  160.8 2.9 %collective-permute-start.21 = (bf16[4,2,128,512]{3,2,1,0:T(8,128)(2,1)}, bf16[4,2,128,512]{3,2,1,0:T(8,128)(2,1)}, u32[]{:S(2)}, u32[]{:S(2)}) collective-permute-start(bf16[4,2,128,512]{3,2,1,0:T(8,128)(2,1)} %collective-permute-done.7.refs_5_), channel_id=1, source_target_pairs={{1,0},{0,1},{3,2},{2,3},{5,4},{4,5},{7,6},{6,7},{9,8},{8,9},{11,10... | collective-permute-start | bytes 3145736 | tf_op jit(solution)/shard_map/ppermute | solution.py:24
  166.3 3.4 %collective-permute-start.35 = (f32[64,128]{1,0:T(8,128)}, f32[64,128]{1,0:T(8,128)}, u32[]{:S(2)}, u32[]{:S(2)}) collective-permute-start(f32[64,128]{1,0:T(8,128)} %get-tuple-element.34), channel_id=1, source_target_pairs={{24,0},{25,1},{26,2},{27,3},{28,4},{29,5},{30,6},{31,7},{32,8},{33... | collective-permute-start | bytes 98312 | tf_op jit(solution)/shard_map/ppermute | solution.py:24
  173.4 2.7 %collective-permute-start.38 = (f32[64,128]{1,0:T(8,128)}, f32[64,128]{1,0:T(8,128)}, u32[]{:S(2)}, u32[]{:S(2)}) collective-permute-start(f32[64,128]{1,0:T(8,128)} %get-tuple-element.37), channel_id=1, source_target_pairs={{48,0},{49,1},{50,2},{51,3},{52,4},{53,5},{54,6},{55,7},{56,8},{57... | collective-permute-start | bytes 98312 | tf_op jit(solution)/shard_map/ppermute | solution.py:24
  186.2 3.4 %collective-permute-start.42 = (f32[72,128]{1,0:T(8,128)}, f32[72,128]{1,0:T(8,128)S(1)}, u32[]{:S(2)}, u32[]{:S(2)}) collective-permute-start(f32[72,128]{1,0:T(8,128)} %sum_z.1.v0), channel_id=1, source_target_pairs={{192,0},{0,64},{64,128},{128,192},{193,1},{1,65},{65,129},{129,193... | collective-permute-start | bytes 110600 | tf_op jit(solution)/shard_map/ppermute | solution.py:28
  192.2 2.6 %copy-done.1 = bf16[352,8192]{1,0:T(8,128)(2,1)S(1)} copy-done((bf16[352,8192]{1,0:T(8,128)(2,1)S(1)}, bf16[352,8192]{1,0:T(8,128)(2,1)}, u32[]{:S(2)}) %copy-start.1) | copy-done | bytes 5767192
  196.5 23.3 %products.1 = (bf16[352,512]{1,0:T(8,128)(2,1)}, bf16[352,8192]{1,0:T(8,128)(2,1)}) custom-call(s32[256]{0:T(256)S(1)} %copy-done.6, s32[5]{0:T(128)S(1)} %stack.85.pos, bf16[352,8192]{1,0:T(8,128)(2,1)S(1)} %copy-done.1, bf16[352,512]{1,0:T(8,128)(2,1)S(1)} %copy-done.3, bf16[4,128,512]{2,1,0:T(8,128)(2,1)S(1)} %pad_maximum_fusion.2.refs_0_, ...), custom_call_target="tpu_custom_call" | custom-call | flops 6000000000 | bytes 25000000 | tf_op jit(solution)/shard_map/products/pallas_call | solution.py:270
  (122 shorter events, 53.1 us)
Async XLA Ops:
  0.6 48.2 %collective-permute-start.8 = (bf16[2,128,128]{2,1,0:T(8,128)(2,1)}, bf16[2,128,128]{2,1,0:T(8,128)(2,1)S(1)}, u32[]{:S(2)}, u32[]{:S(2)}) collective-permute-start(bf16[2,128,128]{2,1,0:T(8,128)(2,1)} %param.9), channel_id=1, source_target_pairs={{16,0},{17,1},{18,2},{19,3},{20,4},{21,5},{22,6},{23,7},{24,8},{25... | collective-permute-start | bytes 196616 | tf_op jit(solution)/shard_map/ppermute | solution.py:24
  7.6 53.7 %collective-permute-start.10 = (bf16[2,128,128]{2,1,0:T(8,128)(2,1)}, bf16[2,128,128]{2,1,0:T(8,128)(2,1)S(1)}, u32[]{:S(2)}, u32[]{:S(2)}) collective-permute-start(bf16[2,128,128]{2,1,0:T(8,128)(2,1)} %param.9), channel_id=1, source_target_pairs={{32,0},{33,1},{34,2},{35,3},{36,4},{37,5},{38,6},{39,7},{40,8},{41... | collective-permute-start | bytes 196616 | tf_op jit(solution)/shard_map/ppermute | solution.py:24
  8.6 43.5 %collective-permute-start.9 = (bf16[2,128,128]{2,1,0:T(8,128)(2,1)}, bf16[2,128,128]{2,1,0:T(8,128)(2,1)S(1)}, u32[]{:S(2)}, u32[]{:S(2)}) collective-permute-start(bf16[2,128,128]{2,1,0:T(8,128)(2,1)} %param.9), channel_id=1, source_target_pairs={{48,0},{49,1},{50,2},{51,3},{52,4},{53,5},{54,6},{55,7},{56,8},{57... | collective-permute-start | bytes 196616 | tf_op jit(solution)/shard_map/ppermute | solution.py:24
  10.8 42.9 %collective-permute-start = (bf16[128,512]{1,0:T(8,128)(2,1)}, bf16[128,512]{1,0:T(8,128)(2,1)S(1)}, u32[]{:S(2)}, u32[]{:S(2)}) collective-permute-start(bf16[128,512]{1,0:T(8,128)(2,1)} %param.7), channel_id=1, source_target_pairs={{16,0},{17,1},{18,2},{19,3},{20,4},{21,5},{22,6},{23,7},{24,8},{25... | collective-permute-start | bytes 393224 | tf_op jit(solution)/shard_map/ppermute | solution.py:24
  12.1 41.9 %collective-permute-start.2 = (bf16[128,512]{1,0:T(8,128)(2,1)}, bf16[128,512]{1,0:T(8,128)(2,1)S(1)}, u32[]{:S(2)}, u32[]{:S(2)}) collective-permute-start(bf16[128,512]{1,0:T(8,128)(2,1)} %param.7), channel_id=1, source_target_pairs={{32,0},{33,1},{34,2},{35,3},{36,4},{37,5},{38,6},{39,7},{40,8},{41... | collective-permute-start | bytes 393224 | tf_op jit(solution)/shard_map/ppermute | solution.py:24
  48.8 43.0 %collective-permute-start.26 = (bf16[4,4,512,128]{3,2,1,0:T(8,128)(2,1)S(1)}, bf16[4,4,512,128]{3,2,1,0:T(8,128)(2,1)S(1)}, u32[]{:S(2)}, u32[]{:S(2)}) collective-permute-start(bf16[4,4,512,128]{3,2,1,0:T(8,128)(2,1)S(1)} %grads_away.1), channel_id=1, source_target_pairs={{1,0},{0,1},{3,2},{2,3},{5,4},{4,5},{7,6},{6,7},{9,8},{8,9},{11,10... | collective-permute-start | bytes 6291464 | tf_op jit(solution)/shard_map/ppermute | solution.py:24
  61.1 15.3 %collective-permute-start.5 = (bf16[4,128,512]{2,1,0:T(8,128)(2,1)S(1)}, bf16[4,128,512]{2,1,0:T(8,128)(2,1)S(1)}, u32[]{:S(2)}, u32[]{:S(2)}) collective-permute-start(bf16[4,128,512]{2,1,0:T(8,128)(2,1)S(1)} %pad_maximum_fusion.2.refs_0_), channel_id=1, source_target_pairs={{6,0},{7,1},{0,2},{1,3},{2,4},{3,5},{4,6},{5,7},{14,8},{15,9},{8,1... | collective-permute-start | bytes 1572872 | tf_op jit(solution)/shard_map/ppermute | solution.py:24
  61.3 26.7 %collective-permute-start.4 = (bf16[4,128,512]{2,1,0:T(8,128)(2,1)S(1)}, bf16[4,128,512]{2,1,0:T(8,128)(2,1)S(1)}, u32[]{:S(2)}, u32[]{:S(2)}) collective-permute-start(bf16[4,128,512]{2,1,0:T(8,128)(2,1)S(1)} %pad_maximum_fusion.2.refs_0_), channel_id=1, source_target_pairs={{4,0},{5,1},{6,2},{7,3},{0,4},{1,5},{2,6},{3,7},{12,8},{13,9},{14,... | collective-permute-start | bytes 1572872 | tf_op jit(solution)/shard_map/ppermute | solution.py:24
  63.2 45.6 %collective-permute-start.16 = (bf16[4,128,512]{2,1,0:T(8,128)(2,1)S(1)}, bf16[4,128,512]{2,1,0:T(8,128)(2,1)S(1)}, u32[]{:S(2)}, u32[]{:S(2)}) collective-permute-start(bf16[4,128,512]{2,1,0:T(8,128)(2,1)S(1)} %pad_maximum_fusion.2.refs_0_), channel_id=1, source_target_pairs={{1,0},{0,1},{3,2},{2,3},{5,4},{4,5},{7,6},{6,7},{9,8},{8,9},{11,10... | collective-permute-start | bytes 1572872 | tf_op jit(solution)/shard_map/ppermute | solution.py:24
  65.9 22.1 %collective-permute-start.3 = (bf16[4,128,512]{2,1,0:T(8,128)(2,1)S(1)}, bf16[4,128,512]{2,1,0:T(8,128)(2,1)S(1)}, u32[]{:S(2)}, u32[]{:S(2)}) collective-permute-start(bf16[4,128,512]{2,1,0:T(8,128)(2,1)S(1)} %pad_maximum_fusion.2.refs_0_), channel_id=1, source_target_pairs={{2,0},{3,1},{4,2},{5,3},{6,4},{7,5},{0,6},{1,7},{10,8},{11,9},{12,... | collective-permute-start | bytes 1572872 | tf_op jit(solution)/shard_map/ppermute | solution.py:24
  76.4 34.2 %collective-permute-start.22 = (bf16[8,2,128,128]{3,2,1,0:T(8,128)(2,1)S(1)}, bf16[8,2,128,128]{3,2,1,0:T(8,128)(2,1)S(1)}, u32[]{:S(2)}, u32[]{:S(2)}) collective-permute-start(bf16[8,2,128,128]{3,2,1,0:T(8,128)(2,1)S(1)} %constant_dynamic-update-slice_fusion.refs_6_), channel_id=1, source_target_pairs={{1,0},{0,1},{3,2},{2,3},{5,4},{4,5},{7,6},{6,7},{9,8},{8,9},{11,10... | collective-permute-start | bytes 1572872 | tf_op jit(solution)/shard_map/ppermute | solution.py:24
  89.2 65.2 %collective-permute-start.6 = (bf16[4,2,128,512]{3,2,1,0:T(8,128)(2,1)}, bf16[4,2,128,512]{3,2,1,0:T(8,128)(2,1)}, u32[]{:S(2)}, u32[]{:S(2)}) collective-permute-start(bf16[4,2,128,512]{3,2,1,0:T(8,128)(2,1)} %pad_maximum_fusion), channel_id=1, source_target_pairs={{8,0},{9,1},{10,2},{11,3},{12,4},{13,5},{14,6},{15,7},{16,8},{17,9... | collective-permute-start | bytes 3145736 | tf_op jit(solution)/shard_map/ppermute | solution.py:24
  108.8 26.3 %collective-permute-start.29 = (bf16[4,512,128]{2,1,0:T(8,128)(2,1)S(1)}, bf16[4,512,128]{2,1,0:T(8,128)(2,1)S(1)}, u32[]{:S(2)}, u32[]{:S(2)}) collective-permute-start(bf16[4,512,128]{2,1,0:T(8,128)(2,1)S(1)} %get-tuple-element.26), channel_id=1, source_target_pairs={{192,0},{0,64},{64,128},{128,192},{193,1},{1,65},{65,129},{129,193... | collective-permute-start | bytes 1572872 | tf_op jit(solution)/shard_map/ppermute | solution.py:28
  111.4 45.8 %collective-permute-start.7 = (bf16[4,2,128,512]{3,2,1,0:T(8,128)(2,1)}, bf16[4,2,128,512]{3,2,1,0:T(8,128)(2,1)}, u32[]{:S(2)}, u32[]{:S(2)}) collective-permute-start(bf16[4,2,128,512]{3,2,1,0:T(8,128)(2,1)} %pad_maximum_fusion.1), channel_id=1, source_target_pairs={{56,0},{57,1},{58,2},{59,3},{60,4},{61,5},{62,6},{63,7},{0,8},{1,9... | collective-permute-start | bytes 3145736 | tf_op jit(solution)/shard_map/ppermute | solution.py:24
  118.8 21.5 %collective-permute-start.15 = (bf16[8,2,128,128]{3,2,1,0:T(8,128)(2,1)S(1)}, bf16[8,2,128,128]{3,2,1,0:T(8,128)(2,1)}, u32[]{:S(2)}, u32[]{:S(2)}) collective-permute-start(bf16[8,2,128,128]{3,2,1,0:T(8,128)(2,1)S(1)} %constant_dynamic-update-slice_fusion.refs_6_), channel_id=1, source_target_pairs={{6,0},{7,1},{0,2},{1,3},{2,4},{3,5},{4,6},{5,7},{14,8},{15,9},{8,1... | collective-permute-start | bytes 1572872 | tf_op jit(solution)/shard_map/ppermute | solution.py:24
  121.2 19.8 %collective-permute-start.14 = (bf16[8,2,128,128]{3,2,1,0:T(8,128)(2,1)S(1)}, bf16[8,2,128,128]{3,2,1,0:T(8,128)(2,1)}, u32[]{:S(2)}, u32[]{:S(2)}) collective-permute-start(bf16[8,2,128,128]{3,2,1,0:T(8,128)(2,1)S(1)} %constant_dynamic-update-slice_fusion.refs_6_), channel_id=1, source_target_pairs={{4,0},{5,1},{6,2},{7,3},{0,4},{1,5},{2,6},{3,7},{12,8},{13,9},{14,... | collective-permute-start | bytes 1572872 | tf_op jit(solution)/shard_map/ppermute | solution.py:24
  135.1 19.3 %collective-permute-start.13 = (bf16[8,2,128,128]{3,2,1,0:T(8,128)(2,1)S(1)}, bf16[8,2,128,128]{3,2,1,0:T(8,128)(2,1)}, u32[]{:S(2)}, u32[]{:S(2)}) collective-permute-start(bf16[8,2,128,128]{3,2,1,0:T(8,128)(2,1)S(1)} %constant_dynamic-update-slice_fusion.refs_6_), channel_id=1, source_target_pairs={{2,0},{3,1},{4,2},{5,3},{6,4},{7,5},{0,6},{1,7},{10,8},{11,9},{12,... | collective-permute-start | bytes 1572872 | tf_op jit(solution)/shard_map/ppermute | solution.py:24
  140.2 17.2 %collective-permute-start.30 = (bf16[512,128]{1,0:T(8,128)(2,1)}, bf16[512,128]{1,0:T(8,128)(2,1)}, u32[]{:S(2)}, u32[]{:S(2)}) collective-permute-start(bf16[512,128]{1,0:T(8,128)(2,1)} %get-tuple-element.28), channel_id=1, source_target_pairs={{2,0},{3,1},{4,2},{5,3},{6,4},{7,5},{0,6},{1,7},{10,8},{11,9},{12,... | collective-permute-start | bytes 393224 | tf_op jit(solution)/shard_map/ppermute | solution.py:24
  141.1 18.6 %collective-permute-start.31 = (bf16[512,128]{1,0:T(8,128)(2,1)}, bf16[512,128]{1,0:T(8,128)(2,1)}, u32[]{:S(2)}, u32[]{:S(2)}) collective-permute-start(bf16[512,128]{1,0:T(8,128)(2,1)} %get-tuple-element.29), channel_id=1, source_target_pairs={{4,0},{5,1},{6,2},{7,3},{0,4},{1,5},{2,6},{3,7},{12,8},{13,9},{14,... | collective-permute-start | bytes 393224 | tf_op jit(solution)/shard_map/ppermute | solution.py:24
  159.7 32.5 %collective-permute-start.20 = (bf16[4,2,128,512]{3,2,1,0:T(8,128)(2,1)}, bf16[4,2,128,512]{3,2,1,0:T(8,128)(2,1)}, u32[]{:S(2)}, u32[]{:S(2)}) collective-permute-start(bf16[4,2,128,512]{3,2,1,0:T(8,128)(2,1)} %collective-permute-done.6.refs_4_), channel_id=1, source_target_pairs={{1,0},{0,1},{3,2},{2,3},{5,4},{4,5},{7,6},{6,7},{9,8},{8,9},{11,10... | collective-permute-start | bytes 3145736 | tf_op jit(solution)/shard_map/ppermute | solution.py:24
  160.8 31.4 %collective-permute-start.21 = (bf16[4,2,128,512]{3,2,1,0:T(8,128)(2,1)}, bf16[4,2,128,512]{3,2,1,0:T(8,128)(2,1)}, u32[]{:S(2)}, u32[]{:S(2)}) collective-permute-start(bf16[4,2,128,512]{3,2,1,0:T(8,128)(2,1)} %collective-permute-done.7.refs_5_), channel_id=1, source_target_pairs={{1,0},{0,1},{3,2},{2,3},{5,4},{4,5},{7,6},{6,7},{9,8},{8,9},{11,10... | collective-permute-start | bytes 3145736 | tf_op jit(solution)/shard_map/ppermute | solution.py:24
  186.2 33.6 %collective-permute-start.42 = (f32[72,128]{1,0:T(8,128)}, f32[72,128]{1,0:T(8,128)S(1)}, u32[]{:S(2)}, u32[]{:S(2)}) collective-permute-start(f32[72,128]{1,0:T(8,128)} %sum_z.1.v0), channel_id=1, source_target_pairs={{192,0},{0,64},{64,128},{128,192},{193,1},{1,65},{65,129},{129,193... | collective-permute-start | bytes 110600 | tf_op jit(solution)/shard_map/ppermute | solution.py:28
  189.7 30.2 %collective-permute-start.41 = (f32[72,128]{1,0:T(8,128)}, f32[72,128]{1,0:T(8,128)}, u32[]{:S(2)}, u32[]{:S(2)}) collective-permute-start(f32[72,128]{1,0:T(8,128)} %sum_z.1.v0), channel_id=1, source_target_pairs={{128,0},{192,64},{0,128},{64,192},{129,1},{193,65},{1,129},{65,193... | collective-permute-start | bytes 110600 | tf_op jit(solution)/shard_map/ppermute | solution.py:28
  191.5 28.4 %collective-permute-start.40 = (f32[72,128]{1,0:T(8,128)}, f32[72,128]{1,0:T(8,128)}, u32[]{:S(2)}, u32[]{:S(2)}) collective-permute-start(f32[72,128]{1,0:T(8,128)} %sum_z.1.v0), channel_id=1, source_target_pairs={{64,0},{128,64},{192,128},{0,192},{65,1},{129,65},{193,129},{1,193... | collective-permute-start | bytes 110600 | tf_op jit(solution)/shard_map/ppermute | solution.py:28
  (36 other events, 543.7 us)

commit v2 on v0

v2 whole, which is shorter than its diff:
```python
import functools

import jax
import jax.numpy as jnp
from jax import lax
from jax.experimental import pallas as pl
from jax.experimental.pallas import tpu as pltpu
from jax.sharding import PartitionSpec as P

NZ, NX, NC, NY = 8, 4, 2, 4
BF16, F32 = jnp.bfloat16, jnp.float32
OWNERS = NZ * NX


def fetch(v, offset):
    pairs = []
    for y in range(NY):
        for z in range(NZ):
            for x in range(NX):
                for c in range(NC):
                    dy, dz, dx, dc = offset(c)
                    near = (((y + dy) % NY * NZ + (z + dz) % NZ) * NX + (x + dx) % NX) * NC + (c ^ dc)
                    pairs.append((near, ((y * NZ + z) * NX + x) * NC + c))
    return lax.ppermute(v, ("dp", "fsdp"), pairs)


def exchange(sent, offset):
    n = len(sent)
    signed = lambda j: j - n if j > n // 2 else j
    return [fetch(sent[n - j], lambda c, j=j: offset(c, signed(j))) for j in range(1, n)]


def other_core(v):
    return fetch(v, lambda c: (0, 0, 0, 1))


def y_or_x(c, d):
    return (d, 0, 0, 0) if c == 0 else (0, 0, d, 0)


def x_or_y(c, d):
    return y_or_x(1 - c, d)


def along_z(c, d):
    return (0, d, 0, 0)


def params(mib):
    return pltpu.CompilerParams(vmem_limit_bytes=mib * 2**20)


def vmem(n):
    return [pl.BlockSpec(memory_space=pltpu.VMEM)] * n


def smem(n):
    return [pl.BlockSpec(memory_space=pltpu.SMEM)] * n


def grad_blocks(ids, core, x_ref, mt_ref, emit):
    block = 128

    def one(i, carry):
        tile = ids[((i // 2 % NZ * NX + i // (2 * NZ)) * NC + core) * 2 + i % 2]
        safe = jnp.maximum(tile, 0)
        xt = x_ref[:, pl.ds(pl.multiple_of(safe // 4 * block, block), block)]
        mt = mt_ref[pl.ds(pl.multiple_of(safe % 4 * block, block), block), :]
        part = jnp.dot(mt, xt, preferred_element_type=F32)
        emit(i, jnp.where(tile >= 0, part, jnp.zeros_like(part)))
        return carry

    lax.fori_loop(0, OWNERS * 2, one, 0, unroll=4)


def grads_away_kernel(ids, pos, x_ref, cot_ref, out_ref, mt_ref):
    rows = lax.broadcasted_iota(jnp.int32, cot_ref.shape, 0)
    g = cot_ref[...]
    mt_ref[...] = jnp.where(rows < pos[4], g, jnp.zeros_like(g)).T

    def emit(i, v):
        out_ref[i] = v.astype(BF16)

    grad_blocks(ids, 1 - pos[3], x_ref, mt_ref, emit)


def grads_home_kernel(ids, pos, x_ref, mt_ref, r_ref, h0, h1, h2, h3, t_ref):
    def emit(i, v):
        t_ref[i] = v + r_ref[i].astype(F32)

    grad_blocks(ids, pos[3], x_ref, mt_ref, emit)
    @pl.when(pos[3] == 0)
    def _():
        for j, h in enumerate((h0, h1, h2, h3)):
            q = (pos[0] + j) % NY
            h[...] = t_ref[:, pl.ds(pl.multiple_of(q * 32, 32), 32), :].astype(h.dtype)

    @pl.when(pos[3] == 1)
    def _():
        for j, h in enumerate((h0, h1, h2, h3)):
            x = (pos[2] + j) % NX
            h[...] = t_ref[pl.ds(x * 16, 16)].reshape(OWNERS * 2, 32, 128).astype(h.dtype)


def grads_away(ids, pos, x, cot):
    return pl.pallas_call(
        grads_away_kernel,
        out_shape=[
            jax.ShapeDtypeStruct((OWNERS * 2, 128, 128), BF16),
            jax.ShapeDtypeStruct(cot.shape[::-1], BF16),
        ],
        in_specs=smem(2) + vmem(2),
        out_specs=vmem(2),
        compiler_params=params(32),
        cost_estimate=pl.CostEstimate(flops=3_000_000_000, bytes_accessed=8_000_000, transcendentals=0),
        name="grads_away",
    )(ids, pos, x, cot)


def grads_home(ids, pos, x, mt, r):
    return pl.pallas_call(
        grads_home_kernel,
        out_shape=[jax.ShapeDtypeStruct((OWNERS * 2, 32, 128), d) for d in (F32, BF16, BF16, BF16)],
        in_specs=smem(2) + vmem(3),
        out_specs=vmem(4),
        scratch_shapes=[pltpu.VMEM((OWNERS * 2, 128, 128), F32)],
        compiler_params=params(32),
        cost_estimate=pl.CostEstimate(flops=3_000_000_000, bytes_accessed=10_000_000, transcendentals=0),
        name="grads_home",
    )(ids, pos, x, mt, r)


def sum_first_kernel(pos, a, b, c, d, j0, j1, j2, j3, t_ref):
    t_ref[...] = a[...] + b[...].astype(F32) + c[...].astype(F32) + d[...].astype(F32)

    @pl.when(pos[3] == 0)
    def _():
        for j, o in enumerate((j0, j1, j2, j3)):
            x = (pos[2] + j) % NX
            o[...] = t_ref[pl.ds(x * 16, 16)].astype(o.dtype)

    @pl.when(pos[3] == 1)
    def _():
        for j, o in enumerate((j0, j1, j2, j3)):
            q = (pos[0] + j) % NY
            for i in range(16):
                o[i] = t_ref[i * 4 + q].astype(o.dtype)


def sum_first(pos, *parts):
    return pl.pallas_call(
        sum_first_kernel,
        out_shape=[jax.ShapeDtypeStruct((16, 32, 128), d) for d in (F32, BF16, BF16, BF16)],
        in_specs=smem(1) + vmem(4),
        out_specs=vmem(4),
        scratch_shapes=[pltpu.VMEM(parts[0].shape, F32)],
        compiler_params=params(16),
        name="sum_first",
    )(pos, *parts)


def sum_second_kernel(pos, a, b, c, d, *refs):
    outs, t_ref = refs[:-1], refs[-1]
    t_ref[...] = a[...] + b[...].astype(F32) + c[...].astype(F32) + d[...].astype(F32)
    for j, o in enumerate(outs):
        z = (pos[1] + j) % NZ
        o[...] = t_ref[pl.ds(z * 2, 2)]


def sum_second(pos, *parts):
    return pl.pallas_call(
        sum_second_kernel,
        out_shape=[jax.ShapeDtypeStruct((2, 32, 128), F32)] * NZ,
        in_specs=smem(1) + vmem(4),
        out_specs=vmem(NZ),
        scratch_shapes=[pltpu.VMEM(parts[0].shape, F32)],
        compiler_params=params(16),
        name="sum_second",
    )(pos, *parts)


def sum_third_kernel(ids, *refs):
    out = refs[-1]
    total = refs[0][...]
    for r in refs[1:-1]:
        total = total + r[...]
    out[0:64, :] = total.reshape(64, 128)
    out[64:72, :] = jnp.full((8, 128), ids[128].astype(F32), F32)


def sum_third(ids, *parts):
    return pl.pallas_call(
        sum_third_kernel,
        out_shape=jax.ShapeDtypeStruct((72, 128), F32),
        in_specs=smem(1) + vmem(NZ),
        out_specs=vmem(1)[0],
        name="sum_third",
    )(ids, *parts)


def finish_kernel(pos, v0, v1, v2, v3, out, t_ref):
    total = (v0[64:65, :] + v1[64:65, :]) + (v2[64:65, :] + v3[64:65, :])
    for j, v in enumerate((v0, v1, v2, v3)):
        q = (pos[0] + j) % NY
        for k in range(2):
            t_ref[k, pl.ds(pl.multiple_of(q * 32, 32), 32), :] = v[k * 32 : k * 32 + 32, :] / total
    for k in range(2):
        out[k] = t_ref[k].T


def finish(pos, *parts):
    return pl.pallas_call(
        finish_kernel,
        out_shape=jax.ShapeDtypeStruct((2, 128, 128), F32),
        in_specs=smem(1) + vmem(4),
        out_specs=vmem(1)[0],
        scratch_shapes=[pltpu.VMEM((2, 128, 128), F32)],
        name="finish",
    )(pos, *parts)


def pack_kernel(frozen_ref, delta_ref, out):
    out[0:128, :] = frozen_ref[...]
    for k in range(2):
        for half in range(2):
            col = (2 * k + half) * 128
            out[128:192, col : col + 128] = delta_ref[k, half * 64 : half * 64 + 64, :]


def pack(frozen, delta_slots):
    return pl.pallas_call(
        pack_kernel,
        out_shape=jax.ShapeDtypeStruct((192, 512), BF16),
        in_specs=vmem(2),
        out_specs=vmem(1)[0],
        name="pack",
    )(frozen, delta_slots)


TILES_A_STEP = 4


def products_kernel(inverse, pos, x_ref, cot_ref, w_ref, all_ref, proj_ref, grad_ref, d_ref, m_ref, acc_ref, e_ref, sem):
    step = pl.program_id(0)
    block = 128
    rows = lax.broadcasted_iota(jnp.int32, acc_ref.shape, 0)

    @pl.when(step == 0)
    def _():
        copy = pltpu.make_async_copy(all_ref.at[:, 128:192, :], d_ref, sem)
        copy.start()
        g = cot_ref[...]
        m_ref[...] = jnp.where(rows < pos[4], g, jnp.zeros_like(g))
        acc_ref[...] = jnp.zeros_like(acc_ref)
        copy.wait()

    for j in range(TILES_A_STEP):
        for col in range(4):
            slot = inverse[(step * TILES_A_STEP + j) * 4 + col]
            safe = jnp.maximum(slot, 0)
            for half in range(2):
                lanes = pl.ds(pl.multiple_of((safe % 2 * 2 + half) * block, block), block)
                d = d_ref[safe // 2, :, lanes].astype(F32)
                d = jnp.where(slot >= 0, d, jnp.zeros_like(d))
                at = slice(half * 64, half * 64 + 64), slice(col * block, col * block + block)
                w = w_ref[j, at[0], at[1]].astype(F32)
                e_ref[j * block + half * 64 : j * block + half * 64 + 64, at[1]] = (w + d).astype(BF16)

    w = e_ref[...]
    acc_ref[...] += jnp.dot(x_ref[...], w, preferred_element_type=F32)
    grad_ref[...] = lax.dot_general(
        m_ref[...], w, (((1,), (1,)), ((), ())), preferred_element_type=F32
    ).astype(BF16)

    @pl.when(step == pl.num_programs(0) - 1)
    def _():
        acc = acc_ref[...]
        proj_ref[...] = jnp.where(rows < pos[4], acc, jnp.zeros_like(acc)).astype(BF16)


def products(inverse, pos, x, cot, gathered):
    tokens, width = x.shape
    heads = cot.shape[1]
    chunk = TILES_A_STEP * 128
    return pl.pallas_call(
        products_kernel,
        grid=(width // chunk,),
        out_shape=[jax.ShapeDtypeStruct((tokens, heads), BF16), jax.ShapeDtypeStruct((tokens, width), BF16)],
        in_specs=smem(2)
        + [
            pl.BlockSpec((tokens, chunk), lambda i: (0, i)),
            pl.BlockSpec((tokens, heads), lambda i: (0, 0)),
            pl.BlockSpec((TILES_A_STEP, 128, heads), lambda i: (i, 0, 0)),
            pl.BlockSpec(memory_space=pl.ANY),
        ],
        out_specs=[
            pl.BlockSpec((tokens, heads), lambda i: (0, 0)),
            pl.BlockSpec((tokens, chunk), lambda i: (0, i)),
        ],
        scratch_shapes=[
            pltpu.VMEM((64, 64, heads), BF16),
            pltpu.VMEM((tokens, heads), BF16),
            pltpu.VMEM((tokens, heads), F32),
            pltpu.VMEM((chunk, heads), BF16),
            pltpu.SemaphoreType.DMA,
        ],
        compiler_params=params(60),
        cost_estimate=pl.CostEstimate(flops=6_000_000_000, bytes_accessed=25_000_000, transcendentals=0),
        name="products",
    )(inverse, pos, x, cot, gathered, gathered)


def per_device(inputs, frozen, cotangent, delta_slots, slot_tile, token_count):
    f = lax.axis_index("fsdp")
    y = lax.axis_index("dp")
    gathered = lax.all_gather(pack(frozen, delta_slots), "fsdp", axis=0)
    here = jnp.zeros((256,), jnp.int32)
    here = lax.dynamic_update_slice(here, slot_tile, (2 * f,))
    here = lax.dynamic_update_slice(here, token_count, (128,))
    ids = lax.psum(here, "fsdp")
    pos = jnp.stack([y, f // 8, f // 2 % 4, f % 2, token_count[0]]).astype(jnp.int32)

    away, mt = grads_away(ids, pos, inputs, cotangent)
    h = grads_home(ids, pos, inputs, mt, other_core(away))
    j = sum_first(pos, h[0], *exchange(h, y_or_x))
    t = sum_second(pos, j[0], *exchange(j, x_or_y))
    q = sum_third(ids, t[0], *exchange(t, along_z))
    owned = finish(pos, q, *[fetch(q, lambda c, d=d: (d, 0, 0, 0)) for d in (1, 2, 3)])

    slots = jnp.arange(128, dtype=jnp.int32)
    tiles = jnp.arange(256, dtype=jnp.int32)
    inverse = jnp.max(jnp.where(ids[None, :128] == tiles[:, None], slots[None, :], -1), axis=1)
    projected, grad_in = products(inverse, pos, inputs, cotangent, gathered)
    return projected, grad_in, owned


def solution(mesh):
    in_specs = (
        P(("dp", "fsdp"), None),
        P("fsdp", None),
        P(("dp", "fsdp"), None),
        P("fsdp", None, None),
        P("fsdp"),
        P(("dp", "fsdp")),
    )
    out_specs = (P(("dp", "fsdp"), None), P(("dp", "fsdp"), None), P("fsdp", None, None))
    return jax.shard_map(per_device, mesh=mesh, in_specs=in_specs, out_specs=out_specs, check_vma=False)
```

time: 492 us -> 147 us (0.30); the launches traced: 484 us -> 146 us
  waiting for transfers between devices: 217 us -> 35.7 us
  blocking collectives: 95.9 us -> 22.6 us
  matrix products: 54.8 us -> 0 us
  local copies, waits for them, and re-layouts: 59.8 us -> 6.43 us
  other arithmetic: 40.2 us -> 0.65 us
  Pallas kernels: 0 us -> 38.6 us
  starting transfers between devices: 0.16 us -> 27 us
    reduce_scatter x1 -> x0, waiting for transfers between devices: 147 us -> none  [per_device(): lax.psum_scatter(partial_grad, 'fsdp', scatter_dimension=0, tiled=True)]
    all_gather x2 -> x1, waiting for transfers between devices: 69.9 us -> 0.01 us  [per_device(): gathered = lax.all_gather(pack(frozen, delta_slots), 'fsdp', axis=0)]
    dot_general x3 -> x0, matrix products: 54.8 us -> none  [the longest x1 21.5 us: per_device(): lax.dot_general(masked, effective, contract_cols, preferred_element_type=...]
    psum x1, blocking collectives: 73.5 us -> 22.6 us  [per_device(): ids = lax.psum(here, 'fsdp')]
    pallas_call x0 -> x8, Pallas kernels: none -> 38.6 us  [the longest x1 20.1 us: products(): pl.pallas_call(products_kernel, grid=(width // chunk,), out_shape=[jax.Sh...]
    ppermute x0 -> x17, waiting for transfers between devices: none -> 35.7 us  [fetch(): return lax.ppermute(v, ('dp', 'fsdp'), pairs)]
    ppermute x0 -> x17, starting transfers between devices: none -> 27 us  [fetch(): return lax.ppermute(v, ('dp', 'fsdp'), pairs)]
    scatter-add x1 -> x0, other arithmetic: 26.6 us -> none  [per_device(): placed = jnp.zeros((tile_count + 1, block_size, block_size), jnp.bfloat16...]
  transfers between devices with their start and end apart: 4 -> 18, of which waited for: 3 -> 13; matrix products, arithmetic and copies ran while one was open for 15% -> 1% of each run, Pallas kernels for 0% -> 12%
where the time goes in v2:
time: 147 us; the launch traced here: 146 us
  Pallas kernels  38.6 us (26%)
  waiting for transfers between devices  35.7 us (24%)
  starting transfers between devices  27 us (18%)
  blocking collectives  22.6 us (15%)
  between operations  14.9 us (10%)
  local copies, waits for them, and re-layouts  6.43 us (4%)
    ppermute x17, waiting for transfers between devices, fetch(): return lax.ppermute(v, ('dp', 'fsdp'), pairs)  35.7 us
    ppermute x17, starting transfers between devices, fetch(): return lax.ppermute(v, ('dp', 'fsdp'), pairs)  27 us
    psum x1, blocking collectives, per_device(): ids = lax.psum(here, 'fsdp')  22.6 us
    pallas_call x1, Pallas kernels, products(): pl.pallas_call(products_kernel, grid=(width // chunk,), out_shape=[jax.Sh...  20.1 us
    pallas_call x1, Pallas kernels, grads_home(): pl.pallas_call(grads_home_kernel, out_shape=[jax.ShapeDtypeStruct((OWNERS...  6.18 us
    pallas_call x1, Pallas kernels, grads_away(): pl.pallas_call(grads_away_kernel, out_shape=[jax.ShapeDtypeStruct((OWNERS...  6.12 us
    unnamed x30, local copies, waits for them, and re-layouts  5.46 us
  transfers between devices with their start and end apart: 18, of which 13 were waited for; matrix products, arithmetic and copies ran while one was open for 1% of the time, Pallas kernels for 12%

profile of v2, /device:TPU:10, one launch (start us, length us, event | category | flops | bytes accessed | tf_op | source)
XLA Modules:
  0.0 145.9 jit_solution(18277728558063679164)
XLA Ops:
  7.2 1.6 %pack.1 = bf16[192,512]{1,0:T(8,128)(2,1)} custom-call(bf16[128,512]{1,0:T(8,128)(2,1)} %frozen_ref.1, bf16[2,128,128]{2,1,0:T(8,128)(2,1)} %delta_ref.1), custom_call_target="tpu_custom_call" | custom-call | tf_op jit(solution)/shard_map/pack/pallas_call | solution.py:231
  10.5 22.6 %psum.7.ids = s32[256]{0:T(256)S(1)} all-reduce(s32[256]{0:T(256)S(1)} %constant_dynamic-update-slice_fusion), channel_id=1, replica_groups=mesh['dp'=4,'fsdp'=64] {'fsdp'}, use_global_device_ids=true, to_apply=%region_0.0 | all-reduce | flops 256 | bytes 2048 | tf_op jit(solution)/shard_map/psum | solution.py:320
  33.1 2.6 %copy-done = bf16[352,8192]{1,0:T(8,128)(2,1)S(1)} copy-done((bf16[352,8192]{1,0:T(8,128)(2,1)S(1)}, bf16[352,8192]{1,0:T(8,128)(2,1)}, u32[]{:S(2)}) %copy-start) | copy-done | bytes 5767192
  36.7 6.1 %grads_away.1 = (bf16[64,128,128]{2,1,0:T(8,128)(2,1)S(1)}, bf16[512,352]{1,0:T(8,128)(2,1)S(1)}) custom-call(s32[256]{0:T(256)S(1)} %psum.7.ids, s32[5]{0:T(128)S(1)} %stack.19.pos, bf16[352,8192]{1,0:T(8,128)(2,1)S(1)} %copy-done, bf16[352,512]{1,0:T(8,128)(2,1)S(1)} %copy-done.1), custom_call_target="tpu_custom_call" | custom-call | flops 3000000000 | bytes 8000000 | tf_op jit(solution)/shard_map/grads_away/pallas_call | solution.py:106
  42.9 4.1 %collective-permute-done.r_ref = bf16[64,128,128]{2,1,0:T(8,128)(2,1)S(1)} collective-permute-done((bf16[64,128,128]{2,1,0:T(8,128)(2,1)S(1)}, bf16[64,128,128]{2,1,0:T(8,128)(2,1)S(1)}, u32[]{:S(2)}, u32[]{:S(2)}) %collective-permute-start) | collective-permute-done | bytes 2097184 | tf_op jit(solution)/shard_map/ppermute | solution.py:24
  47.1 6.2 %grads_home.1 = (f32[64,32,128]{2,1,0:T(8,128)S(1)}, bf16[64,32,128]{2,1,0:T(8,128)(2,1)S(1)}, bf16[64,32,128]{2,1,0:T(8,128)(2,1)S(1)}, bf16[64,32,128]{2,1,0:T(8,128)(2,1)S(1)}) custom-call(s32[256]{0:T(256)S(1)} %psum.7.ids, s32[5]{0:T(128)S(1)} %stack.19.pos, bf16[352,8192]{1,0:T(8,128)(2,1)S(1)} %copy-done, ...), custom_call_target="tpu_custom_call" | custom-call | flops 3000000000 | bytes 10000000 | tf_op jit(solution)/shard_map/grads_home/pallas_call | solution.py:121
  53.8 2.6 %collective-permute-start.2 = (bf16[64,32,128]{2,1,0:T(8,128)(2,1)S(1)}, bf16[64,32,128]{2,1,0:T(8,128)(2,1)S(1)}, u32[]{:S(2)}, u32[]{:S(2)}) collective-permute-start(bf16[64,32,128]{2,1,0:T(8,128)(2,1)S(1)} %get-tuple-element.29), channel_id=1, source_target_pairs={{128,0},{5,1},{130,2},{7,3},{132,4},{1,5},{134,6},{3,7},{136,8},{1... | collective-permute-start | bytes 1572872 | tf_op jit(solution)/shard_map/ppermute | solution.py:24
  56.4 1.9 %collective-permute-start.3 = (bf16[64,32,128]{2,1,0:T(8,128)(2,1)S(1)}, bf16[64,32,128]{2,1,0:T(8,128)(2,1)S(1)}, u32[]{:S(2)}, u32[]{:S(2)}) collective-permute-start(bf16[64,32,128]{2,1,0:T(8,128)(2,1)S(1)} %get-tuple-element.30), channel_id=1, source_target_pairs={{192,0},{7,1},{194,2},{1,3},{196,4},{3,5},{198,6},{5,7},{200,8},{1... | collective-permute-start | bytes 1572872 | tf_op jit(solution)/shard_map/ppermute | solution.py:24
  58.3 4.3 %collective-permute-done.1.b = bf16[64,32,128]{2,1,0:T(8,128)(2,1)S(1)} collective-permute-done((bf16[64,32,128]{2,1,0:T(8,128)(2,1)S(1)}, bf16[64,32,128]{2,1,0:T(8,128)(2,1)S(1)}, u32[]{:S(2)}, u32[]{:S(2)}) %collective-permute-start.1) | collective-permute-done | bytes 524320 | tf_op jit(solution)/shard_map/ppermute | solution.py:24
  62.5 6.6 %collective-permute-done.2.c = bf16[64,32,128]{2,1,0:T(8,128)(2,1)S(1)} collective-permute-done((bf16[64,32,128]{2,1,0:T(8,128)(2,1)S(1)}, bf16[64,32,128]{2,1,0:T(8,128)(2,1)S(1)}, u32[]{:S(2)}, u32[]{:S(2)}) %collective-permute-start.2) | collective-permute-done | bytes 524320 | tf_op jit(solution)/shard_map/ppermute | solution.py:24
  71.1 1.8 %collective-permute-start.4 = (bf16[16,32,128]{2,1,0:T(8,128)(2,1)S(1)}, bf16[16,32,128]{2,1,0:T(8,128)(2,1)S(1)}, u32[]{:S(2)}, u32[]{:S(2)}) collective-permute-start(bf16[16,32,128]{2,1,0:T(8,128)(2,1)S(1)} %get-tuple-element.32), channel_id=1, source_target_pairs={{2,0},{65,1},{4,2},{67,3},{6,4},{69,5},{0,6},{71,7},{10,8},{73,9},... | collective-permute-start | bytes 393224 | tf_op jit(solution)/shard_map/ppermute | solution.py:24
  73.2 2.1 %collective-permute-start.6 = (bf16[16,32,128]{2,1,0:T(8,128)(2,1)S(1)}, bf16[16,32,128]{2,1,0:T(8,128)(2,1)S(1)}, u32[]{:S(2)}, u32[]{:S(2)}) collective-permute-start(bf16[16,32,128]{2,1,0:T(8,128)(2,1)S(1)} %get-tuple-element.34), channel_id=1, source_target_pairs={{6,0},{193,1},{0,2},{195,3},{2,4},{197,5},{4,6},{199,7},{14,8},{20... | collective-permute-start | bytes 393224 | tf_op jit(solution)/shard_map/ppermute | solution.py:24
  75.2 3.7 %collective-permute-done.4.b = bf16[16,32,128]{2,1,0:T(8,128)(2,1)S(1)} collective-permute-done((bf16[16,32,128]{2,1,0:T(8,128)(2,1)S(1)}, bf16[16,32,128]{2,1,0:T(8,128)(2,1)S(1)}, u32[]{:S(2)}, u32[]{:S(2)}) %collective-permute-start.4) | collective-permute-done | bytes 131104 | tf_op jit(solution)/shard_map/ppermute | solution.py:24
  78.9 4.2 %collective-permute-done.5.c = bf16[16,32,128]{2,1,0:T(8,128)(2,1)S(1)} collective-permute-done((bf16[16,32,128]{2,1,0:T(8,128)(2,1)S(1)}, bf16[16,32,128]{2,1,0:T(8,128)(2,1)S(1)}, u32[]{:S(2)}, u32[]{:S(2)}) %collective-permute-start.5) | collective-permute-done | bytes 131104 | tf_op jit(solution)/shard_map/ppermute | solution.py:24
  83.1 2.1 %collective-permute-done.6.d = bf16[16,32,128]{2,1,0:T(8,128)(2,1)S(1)} collective-permute-done((bf16[16,32,128]{2,1,0:T(8,128)(2,1)S(1)}, bf16[16,32,128]{2,1,0:T(8,128)(2,1)S(1)}, u32[]{:S(2)}, u32[]{:S(2)}) %collective-permute-start.6) | collective-permute-done | bytes 131104 | tf_op jit(solution)/shard_map/ppermute | solution.py:24
  87.0 5.0 %collective-permute-start.9 = (f32[2,32,128]{2,1,0:T(8,128)S(1)}, f32[2,32,128]{2,1,0:T(8,128)S(1)}, u32[]{:S(2)}, u32[]{:S(2)}) collective-permute-start(f32[2,32,128]{2,1,0:T(8,128)S(1)} %get-tuple-element.38), channel_id=1, source_target_pairs={{24,0},{25,1},{26,2},{27,3},{28,4},{29,5},{30,6},{31,7},{32,8},{33... | collective-permute-start | bytes 98312 | tf_op jit(solution)/shard_map/ppermute | solution.py:24
  93.0 3.3 %collective-permute-start.11 = (f32[2,32,128]{2,1,0:T(8,128)S(1)}, f32[2,32,128]{2,1,0:T(8,128)S(1)}, u32[]{:S(2)}, u32[]{:S(2)}) collective-permute-start(f32[2,32,128]{2,1,0:T(8,128)S(1)} %get-tuple-element.40), channel_id=1, source_target_pairs={{40,0},{41,1},{42,2},{43,3},{44,4},{45,5},{46,6},{47,7},{48,8},{49... | collective-permute-start | bytes 98312 | tf_op jit(solution)/shard_map/ppermute | solution.py:24
  96.2 2.8 %collective-permute-start.12 = (f32[2,32,128]{2,1,0:T(8,128)S(1)}, f32[2,32,128]{2,1,0:T(8,128)S(1)}, u32[]{:S(2)}, u32[]{:S(2)}) collective-permute-start(f32[2,32,128]{2,1,0:T(8,128)S(1)} %get-tuple-element.41), channel_id=1, source_target_pairs={{48,0},{49,1},{50,2},{51,3},{52,4},{53,5},{54,6},{55,7},{56,8},{57... | collective-permute-start | bytes 98312 | tf_op jit(solution)/shard_map/ppermute | solution.py:24
  99.1 1.9 %collective-permute-done.10.refs_4_ = f32[2,32,128]{2,1,0:T(8,128)S(1)} collective-permute-done((f32[2,32,128]{2,1,0:T(8,128)S(1)}, f32[2,32,128]{2,1,0:T(8,128)S(1)}, u32[]{:S(2)}, u32[]{:S(2)}) %collective-permute-start.10) | collective-permute-done | bytes 32800 | tf_op jit(solution)/shard_map/ppermute | solution.py:24
  102.2 1.6 %collective-permute-done.12.refs_6_ = f32[2,32,128]{2,1,0:T(8,128)S(1)} collective-permute-done((f32[2,32,128]{2,1,0:T(8,128)S(1)}, f32[2,32,128]{2,1,0:T(8,128)S(1)}, u32[]{:S(2)}, u32[]{:S(2)}) %collective-permute-start.12) | collective-permute-done | bytes 32800 | tf_op jit(solution)/shard_map/ppermute | solution.py:24
  108.8 3.6 %collective-permute-start.15 = (f32[72,128]{1,0:T(8,128)}, f32[72,128]{1,0:T(8,128)S(1)}, u32[]{:S(2)}, u32[]{:S(2)}) collective-permute-start(f32[72,128]{1,0:T(8,128)} %sum_third.1.v0), channel_id=1, source_target_pairs={{128,0},{129,1},{130,2},{131,3},{132,4},{133,5},{134,6},{135,7},{1... | collective-permute-start | bytes 110600 | tf_op jit(solution)/shard_map/ppermute | solution.py:24
  114.6 2.0 %collective-permute-done.14.v1 = f32[72,128]{1,0:T(8,128)S(1)} collective-permute-done((f32[72,128]{1,0:T(8,128)}, f32[72,128]{1,0:T(8,128)S(1)}, u32[]{:S(2)}, u32[]{:S(2)}) %collective-permute-start.14) | collective-permute-done | bytes 36896 | tf_op jit(solution)/shard_map/ppermute | solution.py:24
  117.3 1.6 %finish.1 = f32[2,128,128]{2,1,0:T(8,128)} custom-call(s32[5]{0:T(128)} %copy-done.3, f32[72,128]{1,0:T(8,128)} %sum_third.1.v0, f32[72,128]{1,0:T(8,128)} %copy-done.7, f32[72,128]{1,0:T(8,128)} %copy-done.6, f32[72,128]{1,0:T(8,128)} %copy-done.5), custom_call_target="tpu_custom_call" | custom-call | tf_op jit(solution)/shard_map/finish/pallas_call | solution.py:212
  118.9 20.1 %products.1 = (bf16[352,512]{1,0:T(8,128)(2,1)}, bf16[352,8192]{1,0:T(8,128)(2,1)}) custom-call(s32[256]{0:T(256)} %select_reduce_fusion.inverse, s32[5]{0:T(128)} %copy-done.3, bf16[352,8192]{1,0:T(8,128)(2,1)} %x_ref.5, bf16[352,512]{1,0:T(8,128)(2,1)} %cot_ref.3, bf16[64,192,512]{2,1,0:T(8,128)(2,1)} %bitcast.5, bf16[64,192,512]{2,1,0:T(8,128)(2,1)} %bitcast.6), custom_call_target="tpu_custom_call" | custom-call | flops 6000000000 | bytes 25000000 | tf_op jit(solution)/shard_map/products/pallas_call | solution.py:285
  (58 shorter events, 16.6 us)
Async XLA Ops:
  7.2 111.7 %all-gather.3.cloned.1.call-start = ((), (), s32[]{:S(2)}) async-start(), calls=%async_computation | async-start | bytes 12779520 | tf_op jit(solution)/shard_map/all_gather | solution.py:316
  10.5 74.7 %copy-start.3 = (s32[5]{0:T(128)}, s32[5]{0:T(128)S(1)}, u32[]{:S(2)}) copy-start(s32[5]{0:T(128)S(1)} %stack.19.pos) | copy-start | bytes 64
  36.7 62.3 %copy-start.4 = (s32[256]{0:T(256)}, s32[256]{0:T(256)S(1)}, u32[]{:S(2)}) copy-start(s32[256]{0:T(256)S(1)} %psum.7.ids) | copy-start | bytes 3076
  42.8 4.2 %collective-permute-start = (bf16[64,128,128]{2,1,0:T(8,128)(2,1)S(1)}, bf16[64,128,128]{2,1,0:T(8,128)(2,1)S(1)}, u32[]{:S(2)}, u32[]{:S(2)}) collective-permute-start(bf16[64,128,128]{2,1,0:T(8,128)(2,1)S(1)} %get-tuple-element.26), channel_id=1, source_target_pairs={{1,0},{0,1},{3,2},{2,3},{5,4},{4,5},{7,6},{6,7},{9,8},{8,9},{11,10... | collective-permute-start | bytes 6291464 | tf_op jit(solution)/shard_map/ppermute | solution.py:24
  53.3 9.3 %collective-permute-start.1 = (bf16[64,32,128]{2,1,0:T(8,128)(2,1)S(1)}, bf16[64,32,128]{2,1,0:T(8,128)(2,1)S(1)}, u32[]{:S(2)}, u32[]{:S(2)}) collective-permute-start(bf16[64,32,128]{2,1,0:T(8,128)(2,1)S(1)} %get-tuple-element.28), channel_id=1, source_target_pairs={{64,0},{3,1},{66,2},{5,3},{68,4},{7,5},{70,6},{1,7},{72,8},{11,9},... | collective-permute-start | bytes 1572872 | tf_op jit(solution)/shard_map/ppermute | solution.py:24
  53.8 15.4 %collective-permute-start.2 = (bf16[64,32,128]{2,1,0:T(8,128)(2,1)S(1)}, bf16[64,32,128]{2,1,0:T(8,128)(2,1)S(1)}, u32[]{:S(2)}, u32[]{:S(2)}) collective-permute-start(bf16[64,32,128]{2,1,0:T(8,128)(2,1)S(1)} %get-tuple-element.29), channel_id=1, source_target_pairs={{128,0},{5,1},{130,2},{7,3},{132,4},{1,5},{134,6},{3,7},{136,8},{1... | collective-permute-start | bytes 1572872 | tf_op jit(solution)/shard_map/ppermute | solution.py:24
  56.4 13.9 %collective-permute-start.3 = (bf16[64,32,128]{2,1,0:T(8,128)(2,1)S(1)}, bf16[64,32,128]{2,1,0:T(8,128)(2,1)S(1)}, u32[]{:S(2)}, u32[]{:S(2)}) collective-permute-start(bf16[64,32,128]{2,1,0:T(8,128)(2,1)S(1)} %get-tuple-element.30), channel_id=1, source_target_pairs={{192,0},{7,1},{194,2},{1,3},{196,4},{3,5},{198,6},{5,7},{200,8},{1... | collective-permute-start | bytes 1572872 | tf_op jit(solution)/shard_map/ppermute | solution.py:24
  71.1 7.8 %collective-permute-start.4 = (bf16[16,32,128]{2,1,0:T(8,128)(2,1)S(1)}, bf16[16,32,128]{2,1,0:T(8,128)(2,1)S(1)}, u32[]{:S(2)}, u32[]{:S(2)}) collective-permute-start(bf16[16,32,128]{2,1,0:T(8,128)(2,1)S(1)} %get-tuple-element.32), channel_id=1, source_target_pairs={{2,0},{65,1},{4,2},{67,3},{6,4},{69,5},{0,6},{71,7},{10,8},{73,9},... | collective-permute-start | bytes 393224 | tf_op jit(solution)/shard_map/ppermute | solution.py:24
  72.9 10.3 %collective-permute-start.5 = (bf16[16,32,128]{2,1,0:T(8,128)(2,1)S(1)}, bf16[16,32,128]{2,1,0:T(8,128)(2,1)S(1)}, u32[]{:S(2)}, u32[]{:S(2)}) collective-permute-start(bf16[16,32,128]{2,1,0:T(8,128)(2,1)S(1)} %get-tuple-element.33), channel_id=1, source_target_pairs={{4,0},{129,1},{6,2},{131,3},{0,4},{133,5},{2,6},{135,7},{12,8},{13... | collective-permute-start | bytes 393224 | tf_op jit(solution)/shard_map/ppermute | solution.py:24
  73.2 12.0 %collective-permute-start.6 = (bf16[16,32,128]{2,1,0:T(8,128)(2,1)S(1)}, bf16[16,32,128]{2,1,0:T(8,128)(2,1)S(1)}, u32[]{:S(2)}, u32[]{:S(2)}) collective-permute-start(bf16[16,32,128]{2,1,0:T(8,128)(2,1)S(1)} %get-tuple-element.34), channel_id=1, source_target_pairs={{6,0},{193,1},{0,2},{195,3},{2,4},{197,5},{4,6},{199,7},{14,8},{20... | collective-permute-start | bytes 393224 | tf_op jit(solution)/shard_map/ppermute | solution.py:24
  86.5 9.8 %collective-permute-start.7 = (f32[2,32,128]{2,1,0:T(8,128)S(1)}, f32[2,32,128]{2,1,0:T(8,128)S(1)}, u32[]{:S(2)}, u32[]{:S(2)}) collective-permute-start(f32[2,32,128]{2,1,0:T(8,128)S(1)} %get-tuple-element.36), channel_id=1, source_target_pairs={{8,0},{9,1},{10,2},{11,3},{12,4},{13,5},{14,6},{15,7},{16,8},{17,9... | collective-permute-start | bytes 98312 | tf_op jit(solution)/shard_map/ppermute | solution.py:24
  86.5 12.6 %collective-permute-start.8 = (f32[2,32,128]{2,1,0:T(8,128)S(1)}, f32[2,32,128]{2,1,0:T(8,128)S(1)}, u32[]{:S(2)}, u32[]{:S(2)}) collective-permute-start(f32[2,32,128]{2,1,0:T(8,128)S(1)} %get-tuple-element.37), channel_id=1, source_target_pairs={{16,0},{17,1},{18,2},{19,3},{20,4},{21,5},{22,6},{23,7},{24,8},{25... | collective-permute-start | bytes 98312 | tf_op jit(solution)/shard_map/ppermute | solution.py:24
  87.0 12.1 %collective-permute-start.9 = (f32[2,32,128]{2,1,0:T(8,128)S(1)}, f32[2,32,128]{2,1,0:T(8,128)S(1)}, u32[]{:S(2)}, u32[]{:S(2)}) collective-permute-start(f32[2,32,128]{2,1,0:T(8,128)S(1)} %get-tuple-element.38), channel_id=1, source_target_pairs={{24,0},{25,1},{26,2},{27,3},{28,4},{29,5},{30,6},{31,7},{32,8},{33... | collective-permute-start | bytes 98312 | tf_op jit(solution)/shard_map/ppermute | solution.py:24
  92.0 9.0 %collective-permute-start.10 = (f32[2,32,128]{2,1,0:T(8,128)S(1)}, f32[2,32,128]{2,1,0:T(8,128)S(1)}, u32[]{:S(2)}, u32[]{:S(2)}) collective-permute-start(f32[2,32,128]{2,1,0:T(8,128)S(1)} %get-tuple-element.39), channel_id=1, source_target_pairs={{32,0},{33,1},{34,2},{35,3},{36,4},{37,5},{38,6},{39,7},{40,8},{41... | collective-permute-start | bytes 98312 | tf_op jit(solution)/shard_map/ppermute | solution.py:24
  93.0 9.2 %collective-permute-start.11 = (f32[2,32,128]{2,1,0:T(8,128)S(1)}, f32[2,32,128]{2,1,0:T(8,128)S(1)}, u32[]{:S(2)}, u32[]{:S(2)}) collective-permute-start(f32[2,32,128]{2,1,0:T(8,128)S(1)} %get-tuple-element.40), channel_id=1, source_target_pairs={{40,0},{41,1},{42,2},{43,3},{44,4},{45,5},{46,6},{47,7},{48,8},{49... | collective-permute-start | bytes 98312 | tf_op jit(solution)/shard_map/ppermute | solution.py:24
  96.2 9.0 %copy-start.8 = (f32[2,32,128]{2,1,0:T(8,128)}, f32[2,32,128]{2,1,0:T(8,128)S(1)}, u32[]{:S(2)}) copy-start(f32[2,32,128]{2,1,0:T(8,128)S(1)} %collective-permute-done.7.refs_1_) | copy-start | bytes 98308
  96.2 7.6 %collective-permute-start.12 = (f32[2,32,128]{2,1,0:T(8,128)S(1)}, f32[2,32,128]{2,1,0:T(8,128)S(1)}, u32[]{:S(2)}, u32[]{:S(2)}) collective-permute-start(f32[2,32,128]{2,1,0:T(8,128)S(1)} %get-tuple-element.41), channel_id=1, source_target_pairs={{48,0},{49,1},{50,2},{51,3},{52,4},{53,5},{54,6},{55,7},{56,8},{57... | collective-permute-start | bytes 98312 | tf_op jit(solution)/shard_map/ppermute | solution.py:24
  99.0 6.2 %copy-start.9 = (f32[2,32,128]{2,1,0:T(8,128)}, f32[2,32,128]{2,1,0:T(8,128)S(1)}, u32[]{:S(2)}) copy-start(f32[2,32,128]{2,1,0:T(8,128)S(1)} %collective-permute-done.8.refs_2_) | copy-start | bytes 98308
  99.0 6.1 %collective-permute-start.13 = (f32[2,32,128]{2,1,0:T(8,128)S(1)}, f32[2,32,128]{2,1,0:T(8,128)S(1)}, u32[]{:S(2)}, u32[]{:S(2)}) collective-permute-start(f32[2,32,128]{2,1,0:T(8,128)S(1)} %get-tuple-element.42), channel_id=1, source_target_pairs={{56,0},{57,1},{58,2},{59,3},{60,4},{61,5},{62,6},{63,7},{0,8},{1,9... | collective-permute-start | bytes 98312 | tf_op jit(solution)/shard_map/ppermute | solution.py:24
  99.1 6.1 %copy-start.10 = (f32[2,32,128]{2,1,0:T(8,128)}, f32[2,32,128]{2,1,0:T(8,128)S(1)}, u32[]{:S(2)}) copy-start(f32[2,32,128]{2,1,0:T(8,128)S(1)} %collective-permute-done.9.refs_3_) | copy-start | bytes 98308
  101.0 4.2 %copy-start.11 = (f32[2,32,128]{2,1,0:T(8,128)}, f32[2,32,128]{2,1,0:T(8,128)S(1)}, u32[]{:S(2)}) copy-start(f32[2,32,128]{2,1,0:T(8,128)S(1)} %collective-permute-done.10.refs_4_) | copy-start | bytes 98308
  107.3 5.8 %collective-permute-start.16 = (f32[72,128]{1,0:T(8,128)}, f32[72,128]{1,0:T(8,128)S(1)}, u32[]{:S(2)}, u32[]{:S(2)}) collective-permute-start(f32[72,128]{1,0:T(8,128)} %sum_third.1.v0), channel_id=1, source_target_pairs={{192,0},{193,1},{194,2},{195,3},{196,4},{197,5},{198,6},{199,7},{2... | collective-permute-start | bytes 110600 | tf_op jit(solution)/shard_map/ppermute | solution.py:24
  108.8 5.8 %collective-permute-start.15 = (f32[72,128]{1,0:T(8,128)}, f32[72,128]{1,0:T(8,128)S(1)}, u32[]{:S(2)}, u32[]{:S(2)}) collective-permute-start(f32[72,128]{1,0:T(8,128)} %sum_third.1.v0), channel_id=1, source_target_pairs={{128,0},{129,1},{130,2},{131,3},{132,4},{133,5},{134,6},{135,7},{1... | collective-permute-start | bytes 110600 | tf_op jit(solution)/shard_map/ppermute | solution.py:24
  112.5 4.2 %collective-permute-start.14 = (f32[72,128]{1,0:T(8,128)}, f32[72,128]{1,0:T(8,128)S(1)}, u32[]{:S(2)}, u32[]{:S(2)}) collective-permute-start(f32[72,128]{1,0:T(8,128)} %sum_third.1.v0), channel_id=1, source_target_pairs={{64,0},{65,1},{66,2},{67,3},{68,4},{69,5},{70,6},{71,7},{72,8},{73... | collective-permute-start | bytes 110600 | tf_op jit(solution)/shard_map/ppermute | solution.py:24
  (9 other events, 15.4 us)
Sparse Core Ops, SparseCore 0:
  11.3 100.4 all-gather.2

commit v3 on v2

--- a/solution.py
+++ b/solution.py
@@ -198,7 +198,7 @@
     )(ids, *parts)
 
 
-def finish_kernel(pos, v0, v1, v2, v3, out, t_ref):
+def finish_kernel(pos, v0, v1, v2, v3, after, out, t_ref):
     total = (v0[64:65, :] + v1[64:65, :]) + (v2[64:65, :] + v3[64:65, :])
     for j, v in enumerate((v0, v1, v2, v3)):
         q = (pos[0] + j) % NY
@@ -208,15 +208,15 @@
         out[k] = t_ref[k].T
 
 
-def finish(pos, *parts):
+def finish(pos, parts, after):
     return pl.pallas_call(
         finish_kernel,
         out_shape=jax.ShapeDtypeStruct((2, 128, 128), F32),
-        in_specs=smem(1) + vmem(4),
+        in_specs=smem(1) + vmem(4) + [pl.BlockSpec(memory_space=pl.ANY)],
         out_specs=vmem(1)[0],
         scratch_shapes=[pltpu.VMEM((2, 128, 128), F32)],
         name="finish",
-    )(pos, *parts)
+    )(pos, *parts, after)
 
 
 def pack_kernel(frozen_ref, delta_ref, out):
@@ -237,42 +237,70 @@
     )(frozen, delta_slots)
 
 
-TILES_A_STEP = 4
-
-
-def products_kernel(inverse, pos, x_ref, cot_ref, w_ref, all_ref, proj_ref, grad_ref, d_ref, m_ref, acc_ref, e_ref, sem):
-    step = pl.program_id(0)
-    block = 128
+CHUNK = 8
+
+
+def build(inverse, w_ref, d_ref, e_ref, chunk):
+    for j in range(CHUNK):
+        tile = chunk * CHUNK + j
+        for col in range(4):
+            slot = inverse[tile * 4 + col]
+            safe = jnp.maximum(slot, 0)
+            lanes = slice(col * 128, col * 128 + 128)
+            for half in range(2):
+                at = pl.ds(pl.multiple_of((safe % 2 * 2 + half) * 128, 128), 128)
+                d = d_ref[safe // 2, :, at].astype(F32)
+                d = jnp.where(slot >= 0, d, jnp.zeros_like(d))
+                rows = slice(half * 64, half * 64 + 64)
+                e_ref[j, rows, lanes] = (w_ref[tile, rows, lanes].astype(F32) + d).astype(BF16)
+
+
+def products_kernel(inverse, pos, x_ref, cot_ref, all_ref, proj_ref, grad_ref, w_ref, d_ref, m_ref, acc_ref, e0, e1, wsem, dsem):
+    step, steps = pl.program_id(0), pl.num_programs(0)
+    width = CHUNK * 128
     rows = lax.broadcasted_iota(jnp.int32, acc_ref.shape, 0)
 
+    def weights(n):
+        tiles = pl.ds(n * 2 * CHUNK, 2 * CHUNK)
+        return pltpu.make_async_copy(all_ref.at[tiles, 0:128, :], w_ref.at[tiles], wsem.at[n])
+
     @pl.when(step == 0)
     def _():
-        copy = pltpu.make_async_copy(all_ref.at[:, 128:192, :], d_ref, sem)
-        copy.start()
+        deltas = pltpu.make_async_copy(all_ref.at[:, 128:192, :], d_ref, dsem)
+        deltas.start()
+        weights(0).start()
         g = cot_ref[...]
         m_ref[...] = jnp.where(rows < pos[4], g, jnp.zeros_like(g))
         acc_ref[...] = jnp.zeros_like(acc_ref)
-        copy.wait()
-
-    for j in range(TILES_A_STEP):
-        for col in range(4):
-            slot = inverse[(step * TILES_A_STEP + j) * 4 + col]
-            safe = jnp.maximum(slot, 0)
-            for half in range(2):
-                lanes = pl.ds(pl.multiple_of((safe % 2 * 2 + half) * block, block), block)
-                d = d_ref[safe // 2, :, lanes].astype(F32)
-                d = jnp.where(slot >= 0, d, jnp.zeros_like(d))
-                at = slice(half * 64, half * 64 + 64), slice(col * block, col * block + block)
-                w = w_ref[j, at[0], at[1]].astype(F32)
-                e_ref[j * block + half * 64 : j * block + half * 64 + 64, at[1]] = (w + d).astype(BF16)
-
-    w = e_ref[...]
-    acc_ref[...] += jnp.dot(x_ref[...], w, preferred_element_type=F32)
-    grad_ref[...] = lax.dot_general(
-        m_ref[...], w, (((1,), (1,)), ((), ())), preferred_element_type=F32
-    ).astype(BF16)
-
-    @pl.when(step == pl.num_programs(0) - 1)
+        deltas.wait()
+        weights(1).start()
+        weights(2).start()
+        weights(0).wait()
+        build(inverse, w_ref, d_ref, e0, 0)
+
+    def multiply(e_ref, part):
+        w = e_ref[...].reshape(width, acc_ref.shape[1])
+        lanes = slice(part * width, part * width + width)
+        acc_ref[...] += jnp.dot(x_ref[:, lanes], w, preferred_element_type=F32)
+        grad_ref[:, lanes] = lax.dot_general(
+            m_ref[...], w, (((1,), (1,)), ((), ())), preferred_element_type=F32
+        ).astype(BF16)
+
+    build(inverse, w_ref, d_ref, e1, step * 2 + 1)
+    multiply(e0, 0)
+
+    @pl.when(step < steps - 1)
+    def _():
+        @pl.when(step < steps - 3)
+        def _():
+            weights(step + 3).start()
+
+        weights(step + 1).wait()
+
+    build(inverse, w_ref, d_ref, e0, jnp.minimum(step * 2 + 2, 2 * steps - 1))
+    multiply(e1, 1)
+
+    @pl.when(step == steps - 1)
     def _():
         acc = acc_ref[...]
         proj_ref[...] = jnp.where(rows < pos[4], acc, jnp.zeros_like(acc)).astype(BF16)
@@ -281,33 +309,35 @@
 def products(inverse, pos, x, cot, gathered):
     tokens, width = x.shape
     heads = cot.shape[1]
-    chunk = TILES_A_STEP * 128
+    wide = 2 * CHUNK * 128
     return pl.pallas_call(
         products_kernel,
-        grid=(width // chunk,),
+        grid=(width // wide,),
         out_shape=[jax.ShapeDtypeStruct((tokens, heads), BF16), jax.ShapeDtypeStruct((tokens, width), BF16)],
         in_specs=smem(2)
         + [
-            pl.BlockSpec((tokens, chunk), lambda i: (0, i)),
+            pl.BlockSpec((tokens, wide), lambda i: (0, i)),
             pl.BlockSpec((tokens, heads), lambda i: (0, 0)),
-            pl.BlockSpec((TILES_A_STEP, 128, heads), lambda i: (i, 0, 0)),
             pl.BlockSpec(memory_space=pl.ANY),
         ],
         out_specs=[
             pl.BlockSpec((tokens, heads), lambda i: (0, 0)),
-            pl.BlockSpec((tokens, chunk), lambda i: (0, i)),
+            pl.BlockSpec((tokens, wide), lambda i: (0, i)),
         ],
         scratch_shapes=[
+            pltpu.VMEM((64, 128, heads), BF16),
             pltpu.VMEM((64, 64, heads), BF16),
             pltpu.VMEM((tokens, heads), BF16),
             pltpu.VMEM((tokens, heads), F32),
-            pltpu.VMEM((chunk, heads), BF16),
+            pltpu.VMEM((CHUNK, 128, heads), BF16),
+            pltpu.VMEM((CHUNK, 128, heads), BF16),
+            pltpu.SemaphoreType.DMA((64 // (2 * CHUNK),)),
             pltpu.SemaphoreType.DMA,
         ],
         compiler_params=params(60),
         cost_estimate=pl.CostEstimate(flops=6_000_000_000, bytes_accessed=25_000_000, transcendentals=0),
         name="products",
-    )(inverse, pos, x, cot, gathered, gathered)
+    )(inverse, pos, x, cot, gathered)
 
 
 def per_device(inputs, frozen, cotangent, delta_slots, slot_tile, token_count):
@@ -325,12 +355,13 @@
     j = sum_first(pos, h[0], *exchange(h, y_or_x))
     t = sum_second(pos, j[0], *exchange(j, x_or_y))
     q = sum_third(ids, t[0], *exchange(t, along_z))
-    owned = finish(pos, q, *[fetch(q, lambda c, d=d: (d, 0, 0, 0)) for d in (1, 2, 3)])
+    last = [fetch(q, lambda c, d=d: (d, 0, 0, 0)) for d in (1, 2, 3)]
 
     slots = jnp.arange(128, dtype=jnp.int32)
     tiles = jnp.arange(256, dtype=jnp.int32)
     inverse = jnp.max(jnp.where(ids[None, :128] == tiles[:, None], slots[None, :], -1), axis=1)
     projected, grad_in = products(inverse, pos, inputs, cotangent, gathered)
+    owned = finish(pos, [q, *last], projected)
     return projected, grad_in, owned
 
 

time: 147 us -> 140 us (0.952)
  Pallas kernels: 38.6 us -> 34.4 us
  waiting for transfers between devices: 35.7 us -> 31.5 us
    pallas_call x1, Pallas kernels: 20.1 us -> 15.9 us  [products(): pl.pallas_call(products_kernel, grid=(width // wide,), out_shape=[jax.Sha...]
    ppermute x17, waiting for transfers between devices: 35.7 us -> 31.5 us  [fetch(): return lax.ppermute(v, ('dp', 'fsdp'), pairs)]
  transfers between devices with their start and end apart: 18 -> 18, of which waited for: 13 -> 11; matrix products, arithmetic and copies ran while one was open for 1% -> 1% of each run, Pallas kernels for 12% -> 23%
where the time goes in v3:
time: 140 us; the launch traced here: 137 us
  Pallas kernels  34.4 us (25%)
  waiting for transfers between devices  31.5 us (22%)
  starting transfers between devices  27 us (19%)
  blocking collectives  22.6 us (16%)
  between operations  14.9 us (11%)
  local copies, waits for them, and re-layouts  6.4 us (5%)
    ppermute x17, waiting for transfers between devices, fetch(): return lax.ppermute(v, ('dp', 'fsdp'), pairs)  31.5 us
    ppermute x17, starting transfers between devices, fetch(): return lax.ppermute(v, ('dp', 'fsdp'), pairs)  26.9 us
    psum x1, blocking collectives, per_device(): ids = lax.psum(here, 'fsdp')  22.6 us
    pallas_call x1, Pallas kernels, products(): pl.pallas_call(products_kernel, grid=(width // wide,), out_shape=[jax.Sha...  15.9 us
    pallas_call x1, Pallas kernels, grads_home(): pl.pallas_call(grads_home_kernel, out_shape=[jax.ShapeDtypeStruct((OWNERS...  6.17 us
    pallas_call x1, Pallas kernels, grads_away(): pl.pallas_call(grads_away_kernel, out_shape=[jax.ShapeDtypeStruct((OWNERS...  6.08 us
    unnamed x30, local copies, waits for them, and re-layouts  5.43 us
  transfers between devices with their start and end apart: 18, of which 11 were waited for; matrix products, arithmetic and copies ran while one was open for 1% of the time, Pallas kernels for 23%

profile of v3, /device:TPU:10, one launch (start us, length us, event | category | flops | bytes accessed | tf_op | source)
XLA Modules:
  0.0 137.4 jit_solution(1311876367002991971)
XLA Ops:
  7.2 1.6 %pack.1 = bf16[192,512]{1,0:T(8,128)(2,1)} custom-call(bf16[128,512]{1,0:T(8,128)(2,1)} %frozen_ref.1, bf16[2,128,128]{2,1,0:T(8,128)(2,1)} %delta_ref.1), custom_call_target="tpu_custom_call" | custom-call | tf_op jit(solution)/shard_map/pack/pallas_call | solution.py:231
  10.5 22.6 %psum.7.ids = s32[256]{0:T(256)S(1)} all-reduce(s32[256]{0:T(256)S(1)} %constant_dynamic-update-slice_fusion), channel_id=1, replica_groups=mesh['dp'=4,'fsdp'=64] {'fsdp'}, use_global_device_ids=true, to_apply=%region_0.0 | all-reduce | flops 256 | bytes 2048 | tf_op jit(solution)/shard_map/psum | solution.py:350
  33.1 2.6 %copy-done.3 = bf16[352,8192]{1,0:T(8,128)(2,1)S(1)} copy-done((bf16[352,8192]{1,0:T(8,128)(2,1)S(1)}, bf16[352,8192]{1,0:T(8,128)(2,1)}, u32[]{:S(2)}) %copy-start.3) | copy-done | bytes 5767192
  36.7 6.1 %grads_away.1 = (bf16[64,128,128]{2,1,0:T(8,128)(2,1)S(1)}, bf16[512,352]{1,0:T(8,128)(2,1)S(1)}) custom-call(s32[256]{0:T(256)S(1)} %psum.7.ids, s32[5]{0:T(128)S(1)} %stack.19.pos, bf16[352,8192]{1,0:T(8,128)(2,1)S(1)} %copy-done.3, bf16[352,512]{1,0:T(8,128)(2,1)S(1)} %copy-done.4), custom_call_target="tpu_custom_call" | custom-call | flops 3000000000 | bytes 8000000 | tf_op jit(solution)/shard_map/grads_away/pallas_call | solution.py:106
  42.9 4.1 %collective-permute-done.r_ref = bf16[64,128,128]{2,1,0:T(8,128)(2,1)S(1)} collective-permute-done((bf16[64,128,128]{2,1,0:T(8,128)(2,1)S(1)}, bf16[64,128,128]{2,1,0:T(8,128)(2,1)S(1)}, u32[]{:S(2)}, u32[]{:S(2)}) %collective-permute-start) | collective-permute-done | bytes 2097184 | tf_op jit(solution)/shard_map/ppermute | solution.py:24
  47.1 6.2 %grads_home.1 = (f32[64,32,128]{2,1,0:T(8,128)S(1)}, bf16[64,32,128]{2,1,0:T(8,128)(2,1)S(1)}, bf16[64,32,128]{2,1,0:T(8,128)(2,1)S(1)}, bf16[64,32,128]{2,1,0:T(8,128)(2,1)S(1)}) custom-call(s32[256]{0:T(256)S(1)} %psum.7.ids, s32[5]{0:T(128)S(1)} %stack.19.pos, bf16[352,8192]{1,0:T(8,128)(2,1)S(1)} %copy-done.3, ...), custom_call_target="tpu_custom_call" | custom-call | flops 3000000000 | bytes 10000000 | tf_op jit(solution)/shard_map/grads_home/pallas_call | solution.py:121
  53.8 2.6 %collective-permute-start.2 = (bf16[64,32,128]{2,1,0:T(8,128)(2,1)S(1)}, bf16[64,32,128]{2,1,0:T(8,128)(2,1)S(1)}, u32[]{:S(2)}, u32[]{:S(2)}) collective-permute-start(bf16[64,32,128]{2,1,0:T(8,128)(2,1)S(1)} %get-tuple-element.29), channel_id=1, source_target_pairs={{128,0},{5,1},{130,2},{7,3},{132,4},{1,5},{134,6},{3,7},{136,8},{1... | collective-permute-start | bytes 1572872 | tf_op jit(solution)/shard_map/ppermute | solution.py:24
  56.4 1.9 %collective-permute-start.3 = (bf16[64,32,128]{2,1,0:T(8,128)(2,1)S(1)}, bf16[64,32,128]{2,1,0:T(8,128)(2,1)S(1)}, u32[]{:S(2)}, u32[]{:S(2)}) collective-permute-start(bf16[64,32,128]{2,1,0:T(8,128)(2,1)S(1)} %get-tuple-element.30), channel_id=1, source_target_pairs={{192,0},{7,1},{194,2},{1,3},{196,4},{3,5},{198,6},{5,7},{200,8},{1... | collective-permute-start | bytes 1572872 | tf_op jit(solution)/shard_map/ppermute | solution.py:24
  58.2 4.3 %collective-permute-done.1.b = bf16[64,32,128]{2,1,0:T(8,128)(2,1)S(1)} collective-permute-done((bf16[64,32,128]{2,1,0:T(8,128)(2,1)S(1)}, bf16[64,32,128]{2,1,0:T(8,128)(2,1)S(1)}, u32[]{:S(2)}, u32[]{:S(2)}) %collective-permute-start.1) | collective-permute-done | bytes 524320 | tf_op jit(solution)/shard_map/ppermute | solution.py:24
  62.5 6.6 %collective-permute-done.2.c = bf16[64,32,128]{2,1,0:T(8,128)(2,1)S(1)} collective-permute-done((bf16[64,32,128]{2,1,0:T(8,128)(2,1)S(1)}, bf16[64,32,128]{2,1,0:T(8,128)(2,1)S(1)}, u32[]{:S(2)}, u32[]{:S(2)}) %collective-permute-start.2) | collective-permute-done | bytes 524320 | tf_op jit(solution)/shard_map/ppermute | solution.py:24
  71.0 1.8 %collective-permute-start.4 = (bf16[16,32,128]{2,1,0:T(8,128)(2,1)S(1)}, bf16[16,32,128]{2,1,0:T(8,128)(2,1)S(1)}, u32[]{:S(2)}, u32[]{:S(2)}) collective-permute-start(bf16[16,32,128]{2,1,0:T(8,128)(2,1)S(1)} %get-tuple-element.32), channel_id=1, source_target_pairs={{2,0},{65,1},{4,2},{67,3},{6,4},{69,5},{0,6},{71,7},{10,8},{73,9},... | collective-permute-start | bytes 393224 | tf_op jit(solution)/shard_map/ppermute | solution.py:24
  73.1 2.1 %collective-permute-start.6 = (bf16[16,32,128]{2,1,0:T(8,128)(2,1)S(1)}, bf16[16,32,128]{2,1,0:T(8,128)(2,1)S(1)}, u32[]{:S(2)}, u32[]{:S(2)}) collective-permute-start(bf16[16,32,128]{2,1,0:T(8,128)(2,1)S(1)} %get-tuple-element.34), channel_id=1, source_target_pairs={{6,0},{193,1},{0,2},{195,3},{2,4},{197,5},{4,6},{199,7},{14,8},{20... | collective-permute-start | bytes 393224 | tf_op jit(solution)/shard_map/ppermute | solution.py:24
  75.2 3.7 %collective-permute-done.4.b = bf16[16,32,128]{2,1,0:T(8,128)(2,1)S(1)} collective-permute-done((bf16[16,32,128]{2,1,0:T(8,128)(2,1)S(1)}, bf16[16,32,128]{2,1,0:T(8,128)(2,1)S(1)}, u32[]{:S(2)}, u32[]{:S(2)}) %collective-permute-start.4) | collective-permute-done | bytes 131104 | tf_op jit(solution)/shard_map/ppermute | solution.py:24
  78.9 4.2 %collective-permute-done.5.c = bf16[16,32,128]{2,1,0:T(8,128)(2,1)S(1)} collective-permute-done((bf16[16,32,128]{2,1,0:T(8,128)(2,1)S(1)}, bf16[16,32,128]{2,1,0:T(8,128)(2,1)S(1)}, u32[]{:S(2)}, u32[]{:S(2)}) %collective-permute-start.5) | collective-permute-done | bytes 131104 | tf_op jit(solution)/shard_map/ppermute | solution.py:24
  83.1 2.1 %collective-permute-done.6.d = bf16[16,32,128]{2,1,0:T(8,128)(2,1)S(1)} collective-permute-done((bf16[16,32,128]{2,1,0:T(8,128)(2,1)S(1)}, bf16[16,32,128]{2,1,0:T(8,128)(2,1)S(1)}, u32[]{:S(2)}, u32[]{:S(2)}) %collective-permute-start.6) | collective-permute-done | bytes 131104 | tf_op jit(solution)/shard_map/ppermute | solution.py:24
  87.0 5.0 %collective-permute-start.9 = (f32[2,32,128]{2,1,0:T(8,128)S(1)}, f32[2,32,128]{2,1,0:T(8,128)S(1)}, u32[]{:S(2)}, u32[]{:S(2)}) collective-permute-start(f32[2,32,128]{2,1,0:T(8,128)S(1)} %get-tuple-element.38), channel_id=1, source_target_pairs={{24,0},{25,1},{26,2},{27,3},{28,4},{29,5},{30,6},{31,7},{32,8},{33... | collective-permute-start | bytes 98312 | tf_op jit(solution)/shard_map/ppermute | solution.py:24
  93.0 3.2 %collective-permute-start.11 = (f32[2,32,128]{2,1,0:T(8,128)S(1)}, f32[2,32,128]{2,1,0:T(8,128)S(1)}, u32[]{:S(2)}, u32[]{:S(2)}) collective-permute-start(f32[2,32,128]{2,1,0:T(8,128)S(1)} %get-tuple-element.40), channel_id=1, source_target_pairs={{40,0},{41,1},{42,2},{43,3},{44,4},{45,5},{46,6},{47,7},{48,8},{49... | collective-permute-start | bytes 98312 | tf_op jit(solution)/shard_map/ppermute | solution.py:24
  96.2 2.8 %collective-permute-start.12 = (f32[2,32,128]{2,1,0:T(8,128)S(1)}, f32[2,32,128]{2,1,0:T(8,128)S(1)}, u32[]{:S(2)}, u32[]{:S(2)}) collective-permute-start(f32[2,32,128]{2,1,0:T(8,128)S(1)} %get-tuple-element.41), channel_id=1, source_target_pairs={{48,0},{49,1},{50,2},{51,3},{52,4},{53,5},{54,6},{55,7},{56,8},{57... | collective-permute-start | bytes 98312 | tf_op jit(solution)/shard_map/ppermute | solution.py:24
  102.2 1.5 %collective-permute-done.12.refs_6_ = f32[2,32,128]{2,1,0:T(8,128)S(1)} collective-permute-done((f32[2,32,128]{2,1,0:T(8,128)S(1)}, f32[2,32,128]{2,1,0:T(8,128)S(1)}, u32[]{:S(2)}, u32[]{:S(2)}) %collective-permute-start.12) | collective-permute-done | bytes 32800 | tf_op jit(solution)/shard_map/ppermute | solution.py:24
  103.7 1.5 %collective-permute-done.13.refs_7_ = f32[2,32,128]{2,1,0:T(8,128)S(1)} collective-permute-done((f32[2,32,128]{2,1,0:T(8,128)S(1)}, f32[2,32,128]{2,1,0:T(8,128)S(1)}, u32[]{:S(2)}, u32[]{:S(2)}) %collective-permute-start.13) | collective-permute-done | bytes 32800 | tf_op jit(solution)/shard_map/ppermute | solution.py:24
  105.7 1.5 %sum_third.1.v0 = f32[72,128]{1,0:T(8,128)} custom-call(s32[256]{0:T(256)} %copy-done.2, f32[2,32,128]{2,1,0:T(8,128)} %copy-done, f32[2,32,128]{2,1,0:T(8,128)} %copy-done.8, f32[2,32,128]{2,1,0:T(8,128)} %copy-done.9, f32[2,32,128]{2,1,0:T(8,128)} %copy-done.10, f32[2,32,128]{2,1,0:T(8,128)} %copy-done.11, f32[2,32,128]{2,1,0:T(8,128)} %copy-done.12, ...), custom_call_target="tpu_custom_call" | custom-call | tf_op jit(solution)/shard_map/sum_third/pallas_call | solution.py:192
  108.7 3.6 %collective-permute-start.15 = (f32[72,128]{1,0:T(8,128)}, f32[72,128]{1,0:T(8,128)S(1)}, u32[]{:S(2)}, u32[]{:S(2)}) collective-permute-start(f32[72,128]{1,0:T(8,128)} %sum_third.1.v0), channel_id=1, source_target_pairs={{128,0},{129,1},{130,2},{131,3},{132,4},{133,5},{134,6},{135,7},{1... | collective-permute-start | bytes 110600 | tf_op jit(solution)/shard_map/ppermute | solution.py:24
  112.4 15.9 %products.1 = (bf16[352,512]{1,0:T(8,128)(2,1)}, bf16[352,8192]{1,0:T(8,128)(2,1)}) custom-call(s32[256]{0:T(256)} %select_reduce_fusion.inverse, s32[5]{0:T(128)} %copy-done.1, bf16[352,8192]{1,0:T(8,128)(2,1)} %x_ref.5, bf16[352,512]{1,0:T(8,128)(2,1)} %cot_ref.3, bf16[64,192,512]{2,1,0:T(8,128)(2,1)} %bitcast.5), custom_call_target="tpu_custom_call" | custom-call | flops 6000000000 | bytes 25000000 | tf_op jit(solution)/shard_map/products/pallas_call | solution.py:313
  129.0 1.6 %finish.1 = f32[2,128,128]{2,1,0:T(8,128)} custom-call(s32[5]{0:T(128)} %copy-done.1, f32[72,128]{1,0:T(8,128)} %sum_third.1.v0, f32[72,128]{1,0:T(8,128)} %copy-done.7, f32[72,128]{1,0:T(8,128)} %copy-done.6, f32[72,128]{1,0:T(8,128)} %copy-done.5, bf16[352,512]{1,0:T(8,128)(2,1)} %get-tuple-element.20.after), custom_call_target="tpu_custom_call" | custom-call | tf_op jit(solution)/shard_map/finish/pallas_call | solution.py:212
  (58 shorter events, 13.5 us)
Async XLA Ops:
  7.2 105.2 %all-gather.3.cloned.1.call-start = ((), (), s32[]{:S(2)}) async-start(), calls=%async_computation | async-start | bytes 12779520 | tf_op jit(solution)/shard_map/all_gather | solution.py:346
  10.5 74.6 %copy-start.1 = (s32[5]{0:T(128)}, s32[5]{0:T(128)S(1)}, u32[]{:S(2)}) copy-start(s32[5]{0:T(128)S(1)} %stack.19.pos) | copy-start | bytes 64
  36.7 50.3 %copy-start.2 = (s32[256]{0:T(256)}, s32[256]{0:T(256)S(1)}, u32[]{:S(2)}) copy-start(s32[256]{0:T(256)S(1)} %psum.7.ids) | copy-start | bytes 3076
  42.8 4.2 %collective-permute-start = (bf16[64,128,128]{2,1,0:T(8,128)(2,1)S(1)}, bf16[64,128,128]{2,1,0:T(8,128)(2,1)S(1)}, u32[]{:S(2)}, u32[]{:S(2)}) collective-permute-start(bf16[64,128,128]{2,1,0:T(8,128)(2,1)S(1)} %get-tuple-element.26), channel_id=1, source_target_pairs={{1,0},{0,1},{3,2},{2,3},{5,4},{4,5},{7,6},{6,7},{9,8},{8,9},{11,10... | collective-permute-start | bytes 6291464 | tf_op jit(solution)/shard_map/ppermute | solution.py:24
  53.2 9.3 %collective-permute-start.1 = (bf16[64,32,128]{2,1,0:T(8,128)(2,1)S(1)}, bf16[64,32,128]{2,1,0:T(8,128)(2,1)S(1)}, u32[]{:S(2)}, u32[]{:S(2)}) collective-permute-start(bf16[64,32,128]{2,1,0:T(8,128)(2,1)S(1)} %get-tuple-element.28), channel_id=1, source_target_pairs={{64,0},{3,1},{66,2},{5,3},{68,4},{7,5},{70,6},{1,7},{72,8},{11,9},... | collective-permute-start | bytes 1572872 | tf_op jit(solution)/shard_map/ppermute | solution.py:24
  53.8 15.4 %collective-permute-start.2 = (bf16[64,32,128]{2,1,0:T(8,128)(2,1)S(1)}, bf16[64,32,128]{2,1,0:T(8,128)(2,1)S(1)}, u32[]{:S(2)}, u32[]{:S(2)}) collective-permute-start(bf16[64,32,128]{2,1,0:T(8,128)(2,1)S(1)} %get-tuple-element.29), channel_id=1, source_target_pairs={{128,0},{5,1},{130,2},{7,3},{132,4},{1,5},{134,6},{3,7},{136,8},{1... | collective-permute-start | bytes 1572872 | tf_op jit(solution)/shard_map/ppermute | solution.py:24
  56.4 13.9 %collective-permute-start.3 = (bf16[64,32,128]{2,1,0:T(8,128)(2,1)S(1)}, bf16[64,32,128]{2,1,0:T(8,128)(2,1)S(1)}, u32[]{:S(2)}, u32[]{:S(2)}) collective-permute-start(bf16[64,32,128]{2,1,0:T(8,128)(2,1)S(1)} %get-tuple-element.30), channel_id=1, source_target_pairs={{192,0},{7,1},{194,2},{1,3},{196,4},{3,5},{198,6},{5,7},{200,8},{1... | collective-permute-start | bytes 1572872 | tf_op jit(solution)/shard_map/ppermute | solution.py:24
  71.0 7.8 %collective-permute-start.4 = (bf16[16,32,128]{2,1,0:T(8,128)(2,1)S(1)}, bf16[16,32,128]{2,1,0:T(8,128)(2,1)S(1)}, u32[]{:S(2)}, u32[]{:S(2)}) collective-permute-start(bf16[16,32,128]{2,1,0:T(8,128)(2,1)S(1)} %get-tuple-element.32), channel_id=1, source_target_pairs={{2,0},{65,1},{4,2},{67,3},{6,4},{69,5},{0,6},{71,7},{10,8},{73,9},... | collective-permute-start | bytes 393224 | tf_op jit(solution)/shard_map/ppermute | solution.py:24
  72.8 10.3 %collective-permute-start.5 = (bf16[16,32,128]{2,1,0:T(8,128)(2,1)S(1)}, bf16[16,32,128]{2,1,0:T(8,128)(2,1)S(1)}, u32[]{:S(2)}, u32[]{:S(2)}) collective-permute-start(bf16[16,32,128]{2,1,0:T(8,128)(2,1)S(1)} %get-tuple-element.33), channel_id=1, source_target_pairs={{4,0},{129,1},{6,2},{131,3},{0,4},{133,5},{2,6},{135,7},{12,8},{13... | collective-permute-start | bytes 393224 | tf_op jit(solution)/shard_map/ppermute | solution.py:24
  73.1 12.0 %collective-permute-start.6 = (bf16[16,32,128]{2,1,0:T(8,128)(2,1)S(1)}, bf16[16,32,128]{2,1,0:T(8,128)(2,1)S(1)}, u32[]{:S(2)}, u32[]{:S(2)}) collective-permute-start(bf16[16,32,128]{2,1,0:T(8,128)(2,1)S(1)} %get-tuple-element.34), channel_id=1, source_target_pairs={{6,0},{193,1},{0,2},{195,3},{2,4},{197,5},{4,6},{199,7},{14,8},{20... | collective-permute-start | bytes 393224 | tf_op jit(solution)/shard_map/ppermute | solution.py:24
  86.4 9.8 %collective-permute-start.7 = (f32[2,32,128]{2,1,0:T(8,128)S(1)}, f32[2,32,128]{2,1,0:T(8,128)S(1)}, u32[]{:S(2)}, u32[]{:S(2)}) collective-permute-start(f32[2,32,128]{2,1,0:T(8,128)S(1)} %get-tuple-element.36), channel_id=1, source_target_pairs={{8,0},{9,1},{10,2},{11,3},{12,4},{13,5},{14,6},{15,7},{16,8},{17,9... | collective-permute-start | bytes 98312 | tf_op jit(solution)/shard_map/ppermute | solution.py:24
  86.4 12.6 %collective-permute-start.8 = (f32[2,32,128]{2,1,0:T(8,128)S(1)}, f32[2,32,128]{2,1,0:T(8,128)S(1)}, u32[]{:S(2)}, u32[]{:S(2)}) collective-permute-start(f32[2,32,128]{2,1,0:T(8,128)S(1)} %get-tuple-element.37), channel_id=1, source_target_pairs={{16,0},{17,1},{18,2},{19,3},{20,4},{21,5},{22,6},{23,7},{24,8},{25... | collective-permute-start | bytes 98312 | tf_op jit(solution)/shard_map/ppermute | solution.py:24
  87.0 12.7 %collective-permute-start.9 = (f32[2,32,128]{2,1,0:T(8,128)S(1)}, f32[2,32,128]{2,1,0:T(8,128)S(1)}, u32[]{:S(2)}, u32[]{:S(2)}) collective-permute-start(f32[2,32,128]{2,1,0:T(8,128)S(1)} %get-tuple-element.38), channel_id=1, source_target_pairs={{24,0},{25,1},{26,2},{27,3},{28,4},{29,5},{30,6},{31,7},{32,8},{33... | collective-permute-start | bytes 98312 | tf_op jit(solution)/shard_map/ppermute | solution.py:24
  92.0 9.0 %collective-permute-start.10 = (f32[2,32,128]{2,1,0:T(8,128)S(1)}, f32[2,32,128]{2,1,0:T(8,128)S(1)}, u32[]{:S(2)}, u32[]{:S(2)}) collective-permute-start(f32[2,32,128]{2,1,0:T(8,128)S(1)} %get-tuple-element.39), channel_id=1, source_target_pairs={{32,0},{33,1},{34,2},{35,3},{36,4},{37,5},{38,6},{39,7},{40,8},{41... | collective-permute-start | bytes 98312 | tf_op jit(solution)/shard_map/ppermute | solution.py:24
  93.0 9.2 %collective-permute-start.11 = (f32[2,32,128]{2,1,0:T(8,128)S(1)}, f32[2,32,128]{2,1,0:T(8,128)S(1)}, u32[]{:S(2)}, u32[]{:S(2)}) collective-permute-start(f32[2,32,128]{2,1,0:T(8,128)S(1)} %get-tuple-element.40), channel_id=1, source_target_pairs={{40,0},{41,1},{42,2},{43,3},{44,4},{45,5},{46,6},{47,7},{48,8},{49... | collective-permute-start | bytes 98312 | tf_op jit(solution)/shard_map/ppermute | solution.py:24
  96.2 9.0 %copy-start.8 = (f32[2,32,128]{2,1,0:T(8,128)}, f32[2,32,128]{2,1,0:T(8,128)S(1)}, u32[]{:S(2)}) copy-start(f32[2,32,128]{2,1,0:T(8,128)S(1)} %collective-permute-done.7.refs_1_) | copy-start | bytes 98308
  96.2 7.5 %collective-permute-start.12 = (f32[2,32,128]{2,1,0:T(8,128)S(1)}, f32[2,32,128]{2,1,0:T(8,128)S(1)}, u32[]{:S(2)}, u32[]{:S(2)}) collective-permute-start(f32[2,32,128]{2,1,0:T(8,128)S(1)} %get-tuple-element.41), channel_id=1, source_target_pairs={{48,0},{49,1},{50,2},{51,3},{52,4},{53,5},{54,6},{55,7},{56,8},{57... | collective-permute-start | bytes 98312 | tf_op jit(solution)/shard_map/ppermute | solution.py:24
  99.0 6.1 %copy-start.9 = (f32[2,32,128]{2,1,0:T(8,128)}, f32[2,32,128]{2,1,0:T(8,128)S(1)}, u32[]{:S(2)}) copy-start(f32[2,32,128]{2,1,0:T(8,128)S(1)} %collective-permute-done.8.refs_2_) | copy-start | bytes 98308
  99.0 6.1 %collective-permute-start.13 = (f32[2,32,128]{2,1,0:T(8,128)S(1)}, f32[2,32,128]{2,1,0:T(8,128)S(1)}, u32[]{:S(2)}, u32[]{:S(2)}) collective-permute-start(f32[2,32,128]{2,1,0:T(8,128)S(1)} %get-tuple-element.42), channel_id=1, source_target_pairs={{56,0},{57,1},{58,2},{59,3},{60,4},{61,5},{62,6},{63,7},{0,8},{1,9... | collective-permute-start | bytes 98312 | tf_op jit(solution)/shard_map/ppermute | solution.py:24
  99.7 5.4 %copy-start.10 = (f32[2,32,128]{2,1,0:T(8,128)}, f32[2,32,128]{2,1,0:T(8,128)S(1)}, u32[]{:S(2)}) copy-start(f32[2,32,128]{2,1,0:T(8,128)S(1)} %collective-permute-done.9.refs_3_) | copy-start | bytes 98308
  101.0 4.2 %copy-start.11 = (f32[2,32,128]{2,1,0:T(8,128)}, f32[2,32,128]{2,1,0:T(8,128)S(1)}, u32[]{:S(2)}) copy-start(f32[2,32,128]{2,1,0:T(8,128)S(1)} %collective-permute-done.10.refs_4_) | copy-start | bytes 98308
  107.3 21.0 %collective-permute-start.16 = (f32[72,128]{1,0:T(8,128)}, f32[72,128]{1,0:T(8,128)S(1)}, u32[]{:S(2)}, u32[]{:S(2)}) collective-permute-start(f32[72,128]{1,0:T(8,128)} %sum_third.1.v0), channel_id=1, source_target_pairs={{192,0},{193,1},{194,2},{195,3},{196,4},{197,5},{198,6},{199,7},{2... | collective-permute-start | bytes 110600 | tf_op jit(solution)/shard_map/ppermute | solution.py:24
  108.7 19.6 %collective-permute-start.15 = (f32[72,128]{1,0:T(8,128)}, f32[72,128]{1,0:T(8,128)S(1)}, u32[]{:S(2)}, u32[]{:S(2)}) collective-permute-start(f32[72,128]{1,0:T(8,128)} %sum_third.1.v0), channel_id=1, source_target_pairs={{128,0},{129,1},{130,2},{131,3},{132,4},{133,5},{134,6},{135,7},{1... | collective-permute-start | bytes 110600 | tf_op jit(solution)/shard_map/ppermute | solution.py:24
  112.4 16.0 %collective-permute-start.14 = (f32[72,128]{1,0:T(8,128)}, f32[72,128]{1,0:T(8,128)S(1)}, u32[]{:S(2)}, u32[]{:S(2)}) collective-permute-start(f32[72,128]{1,0:T(8,128)} %sum_third.1.v0), channel_id=1, source_target_pairs={{64,0},{65,1},{66,2},{67,3},{68,4},{69,5},{70,6},{71,7},{72,8},{73... | collective-permute-start | bytes 110600 | tf_op jit(solution)/shard_map/ppermute | solution.py:24
  (9 other events, 11.2 us)
Sparse Core Ops, SparseCore 0:
  11.3 100.4 all-gather.2

commit v4 on v3

--- a/solution.py
+++ b/solution.py
@@ -58,37 +58,51 @@
     return [pl.BlockSpec(memory_space=pltpu.SMEM)] * n
 
 
-def grad_blocks(ids, core, x_ref, mt_ref, emit):
-    block = 128
-
-    def one(i, carry):
-        tile = ids[((i // 2 % NZ * NX + i // (2 * NZ)) * NC + core) * 2 + i % 2]
-        safe = jnp.maximum(tile, 0)
-        xt = x_ref[:, pl.ds(pl.multiple_of(safe // 4 * block, block), block)]
-        mt = mt_ref[pl.ds(pl.multiple_of(safe % 4 * block, block), block), :]
-        part = jnp.dot(mt, xt, preferred_element_type=F32)
-        emit(i, jnp.where(tile >= 0, part, jnp.zeros_like(part)))
+def grad_blocks(ids, core, x_ref, mt_ref, live_ref, emit):
+    block, unroll = 128, 4
+
+    def tile_of(i):
+        return ids[((i // 2 % NZ * NX + i // (2 * NZ)) * NC + core) * 2 + i % 2]
+
+    def note(i, n):
+        live_ref[n] = i
+        return n + (tile_of(i) >= 0).astype(jnp.int32)
+
+    n = lax.fori_loop(0, OWNERS * 2, note, 0, unroll=8)
+    for p in range(unroll):
+        live_ref[n + p] = live_ref[0]
+
+    def one(r, carry):
+        for p in range(unroll):
+            i = live_ref[r * unroll + p]
+            tile = tile_of(i)
+            xt = x_ref[:, pl.ds(pl.multiple_of(tile // 4 * block, block), block)]
+            mt = mt_ref[pl.ds(pl.multiple_of(tile % 4 * block, block), block), :]
+            emit(i, jnp.dot(mt, xt, preferred_element_type=F32))
         return carry
 
-    lax.fori_loop(0, OWNERS * 2, one, 0, unroll=4)
-
-
-def grads_away_kernel(ids, pos, x_ref, cot_ref, out_ref, mt_ref):
+    lax.fori_loop(0, (n + unroll - 1) // unroll, one, 0)
+
+
+def grads_away_kernel(ids, pos, x_ref, cot_ref, out_ref, mt_ref, live_ref):
     rows = lax.broadcasted_iota(jnp.int32, cot_ref.shape, 0)
     g = cot_ref[...]
     mt_ref[...] = jnp.where(rows < pos[4], g, jnp.zeros_like(g)).T
+    out_ref[...] = jnp.zeros_like(out_ref)
 
     def emit(i, v):
         out_ref[i] = v.astype(BF16)
 
-    grad_blocks(ids, 1 - pos[3], x_ref, mt_ref, emit)
-
-
-def grads_home_kernel(ids, pos, x_ref, mt_ref, r_ref, h0, h1, h2, h3, t_ref):
+    grad_blocks(ids, 1 - pos[3], x_ref, mt_ref, live_ref, emit)
+
+
+def grads_home_kernel(ids, pos, x_ref, mt_ref, r_ref, h0, h1, h2, h3, t_ref, live_ref):
+    t_ref[...] = r_ref[...].astype(F32)
+
     def emit(i, v):
         t_ref[i] = v + r_ref[i].astype(F32)
 
-    grad_blocks(ids, pos[3], x_ref, mt_ref, emit)
+    grad_blocks(ids, pos[3], x_ref, mt_ref, live_ref, emit)
     @pl.when(pos[3] == 0)
     def _():
         for j, h in enumerate((h0, h1, h2, h3)):
@@ -111,6 +125,7 @@
         ],
         in_specs=smem(2) + vmem(2),
         out_specs=vmem(2),
+        scratch_shapes=[pltpu.SMEM((OWNERS * 2 + 8,), jnp.int32)],
         compiler_params=params(32),
         cost_estimate=pl.CostEstimate(flops=3_000_000_000, bytes_accessed=8_000_000, transcendentals=0),
         name="grads_away",
@@ -123,7 +138,7 @@
         out_shape=[jax.ShapeDtypeStruct((OWNERS * 2, 32, 128), d) for d in (F32, BF16, BF16, BF16)],
         in_specs=smem(2) + vmem(3),
         out_specs=vmem(4),
-        scratch_shapes=[pltpu.VMEM((OWNERS * 2, 128, 128), F32)],
+        scratch_shapes=[pltpu.VMEM((OWNERS * 2, 128, 128), F32), pltpu.SMEM((OWNERS * 2 + 8,), jnp.int32)],
         compiler_params=params(32),
         cost_estimate=pl.CostEstimate(flops=3_000_000_000, bytes_accessed=10_000_000, transcendentals=0),
         name="grads_home",
@@ -164,13 +179,13 @@
     t_ref[...] = a[...] + b[...].astype(F32) + c[...].astype(F32) + d[...].astype(F32)
     for j, o in enumerate(outs):
         z = (pos[1] + j) % NZ
-        o[...] = t_ref[pl.ds(z * 2, 2)]
+        o[...] = t_ref[pl.ds(z * 2, 2)].astype(o.dtype)
 
 
 def sum_second(pos, *parts):
     return pl.pallas_call(
         sum_second_kernel,
-        out_shape=[jax.ShapeDtypeStruct((2, 32, 128), F32)] * NZ,
+        out_shape=[jax.ShapeDtypeStruct((2, 32, 128), BF16 if j else F32) for j in range(NZ)],
         in_specs=smem(1) + vmem(4),
         out_specs=vmem(NZ),
         scratch_shapes=[pltpu.VMEM(parts[0].shape, F32)],
@@ -183,7 +198,7 @@
     out = refs[-1]
     total = refs[0][...]
     for r in refs[1:-1]:
-        total = total + r[...]
+        total = total + r[...].astype(F32)
     out[0:64, :] = total.reshape(64, 128)
     out[64:72, :] = jnp.full((8, 128), ids[128].astype(F32), F32)
 
@@ -198,7 +213,7 @@
     )(ids, *parts)
 
 
-def finish_kernel(pos, v0, v1, v2, v3, after, out, t_ref):
+def finish_kernel(pos, v0, v1, v2, v3, out, t_ref):
     total = (v0[64:65, :] + v1[64:65, :]) + (v2[64:65, :] + v3[64:65, :])
     for j, v in enumerate((v0, v1, v2, v3)):
         q = (pos[0] + j) % NY
@@ -208,15 +223,15 @@
         out[k] = t_ref[k].T
 
 
-def finish(pos, parts, after):
+def finish(pos, *parts):
     return pl.pallas_call(
         finish_kernel,
         out_shape=jax.ShapeDtypeStruct((2, 128, 128), F32),
-        in_specs=smem(1) + vmem(4) + [pl.BlockSpec(memory_space=pl.ANY)],
+        in_specs=smem(1) + vmem(4),
         out_specs=vmem(1)[0],
         scratch_shapes=[pltpu.VMEM((2, 128, 128), F32)],
         name="finish",
-    )(pos, *parts, after)
+    )(pos, *parts)
 
 
 def pack_kernel(frozen_ref, delta_ref, out):
@@ -355,13 +370,12 @@
     j = sum_first(pos, h[0], *exchange(h, y_or_x))
     t = sum_second(pos, j[0], *exchange(j, x_or_y))
     q = sum_third(ids, t[0], *exchange(t, along_z))
-    last = [fetch(q, lambda c, d=d: (d, 0, 0, 0)) for d in (1, 2, 3)]
+    owned = finish(pos, q, *[fetch(q, lambda c, d=d: (d, 0, 0, 0)) for d in (1, 2, 3)])
 
     slots = jnp.arange(128, dtype=jnp.int32)
     tiles = jnp.arange(256, dtype=jnp.int32)
     inverse = jnp.max(jnp.where(ids[None, :128] == tiles[:, None], slots[None, :], -1), axis=1)
     projected, grad_in = products(inverse, pos, inputs, cotangent, gathered)
-    owned = finish(pos, [q, *last], projected)
     return projected, grad_in, owned
 
 

time: 140 us -> 138 us (0.986); the launches traced: 137 us -> 138 us
  waiting for transfers between devices: 31.5 us -> 34.8 us
  Pallas kernels: 34.4 us -> 32 us
    ppermute x17, waiting for transfers between devices: 31.5 us -> 34.8 us  [fetch(): return lax.ppermute(v, ('dp', 'fsdp'), pairs)]
  transfers between devices with their start and end apart: 18 -> 18, of which waited for: 11 -> 13; matrix products, arithmetic and copies ran while one was open for 1% -> 1% of each run, Pallas kernels for 23% -> 10%
where the time goes in v4:
time: 138 us
  waiting for transfers between devices  34.8 us (25%)
  Pallas kernels  32 us (23%)
  starting transfers between devices  26.8 us (19%)
  blocking collectives  22.6 us (16%)
  between operations  14.9 us (11%)
  local copies, waits for them, and re-layouts  6.42 us (5%)
    ppermute x17, waiting for transfers between devices, fetch(): return lax.ppermute(v, ('dp', 'fsdp'), pairs)  34.8 us
    ppermute x17, starting transfers between devices, fetch(): return lax.ppermute(v, ('dp', 'fsdp'), pairs)  26.8 us
    psum x1, blocking collectives, per_device(): ids = lax.psum(here, 'fsdp')  22.6 us
    pallas_call x1, Pallas kernels, products(): pl.pallas_call(products_kernel, grid=(width // wide,), out_shape=[jax.Sha...  15.9 us
    unnamed x30, local copies, waits for them, and re-layouts  5.45 us
    pallas_call x1, Pallas kernels, grads_home(): pl.pallas_call(grads_home_kernel, out_shape=[jax.ShapeDtypeStruct((OWNERS...  5.03 us
    pallas_call x1, Pallas kernels, grads_away(): pl.pallas_call(grads_away_kernel, out_shape=[jax.ShapeDtypeStruct((OWNERS...  4.88 us
  transfers between devices with their start and end apart: 18, of which 13 were waited for; matrix products, arithmetic and copies ran while one was open for 1% of the time, Pallas kernels for 10%

profile of v4, /device:TPU:10, one launch (start us, length us, event | category | flops | bytes accessed | tf_op | source)
XLA Modules:
  0.0 138.1 jit_solution(1351973361335877976)
XLA Ops:
  7.2 1.6 %pack.1 = bf16[192,512]{1,0:T(8,128)(2,1)} custom-call(bf16[128,512]{1,0:T(8,128)(2,1)} %frozen_ref.1, bf16[2,128,128]{2,1,0:T(8,128)(2,1)} %delta_ref.1), custom_call_target="tpu_custom_call" | custom-call | tf_op jit(solution)/shard_map/pack/pallas_call | solution.py:246
  10.5 22.6 %psum.7.ids = s32[256]{0:T(256)S(1)} all-reduce(s32[256]{0:T(256)S(1)} %constant_dynamic-update-slice_fusion), channel_id=1, replica_groups=mesh['dp'=4,'fsdp'=64] {'fsdp'}, use_global_device_ids=true, to_apply=%region_0.0 | all-reduce | flops 256 | bytes 2048 | tf_op jit(solution)/shard_map/psum | solution.py:365
  33.1 2.6 %copy-done.3 = bf16[352,8192]{1,0:T(8,128)(2,1)S(1)} copy-done((bf16[352,8192]{1,0:T(8,128)(2,1)S(1)}, bf16[352,8192]{1,0:T(8,128)(2,1)}, u32[]{:S(2)}) %copy-start.3) | copy-done | bytes 5767192
  36.7 4.9 %grads_away.1 = (bf16[64,128,128]{2,1,0:T(8,128)(2,1)S(1)}, bf16[512,352]{1,0:T(8,128)(2,1)S(1)}) custom-call(s32[256]{0:T(256)S(1)} %psum.7.ids, s32[5]{0:T(128)S(1)} %stack.19.pos, bf16[352,8192]{1,0:T(8,128)(2,1)S(1)} %copy-done.3, bf16[352,512]{1,0:T(8,128)(2,1)S(1)} %copy-done.4), custom_call_target="tpu_custom_call" | custom-call | flops 3000000000 | bytes 8000000 | tf_op jit(solution)/shard_map/grads_away/pallas_call | solution.py:120
  41.7 4.1 %collective-permute-done.r_ref = bf16[64,128,128]{2,1,0:T(8,128)(2,1)S(1)} collective-permute-done((bf16[64,128,128]{2,1,0:T(8,128)(2,1)S(1)}, bf16[64,128,128]{2,1,0:T(8,128)(2,1)S(1)}, u32[]{:S(2)}, u32[]{:S(2)}) %collective-permute-start) | collective-permute-done | bytes 2097184 | tf_op jit(solution)/shard_map/ppermute | solution.py:24
  45.9 5.0 %grads_home.1 = (f32[64,32,128]{2,1,0:T(8,128)S(1)}, bf16[64,32,128]{2,1,0:T(8,128)(2,1)S(1)}, bf16[64,32,128]{2,1,0:T(8,128)(2,1)S(1)}, bf16[64,32,128]{2,1,0:T(8,128)(2,1)S(1)}) custom-call(s32[256]{0:T(256)S(1)} %psum.7.ids, s32[5]{0:T(128)S(1)} %stack.19.pos, bf16[352,8192]{1,0:T(8,128)(2,1)S(1)} %copy-done.3, ...), custom_call_target="tpu_custom_call" | custom-call | flops 3000000000 | bytes 10000000 | tf_op jit(solution)/shard_map/grads_home/pallas_call | solution.py:136
  51.4 2.6 %collective-permute-start.2 = (bf16[64,32,128]{2,1,0:T(8,128)(2,1)S(1)}, bf16[64,32,128]{2,1,0:T(8,128)(2,1)S(1)}, u32[]{:S(2)}, u32[]{:S(2)}) collective-permute-start(bf16[64,32,128]{2,1,0:T(8,128)(2,1)S(1)} %get-tuple-element.29), channel_id=1, source_target_pairs={{128,0},{5,1},{130,2},{7,3},{132,4},{1,5},{134,6},{3,7},{136,8},{1... | collective-permute-start | bytes 1572872 | tf_op jit(solution)/shard_map/ppermute | solution.py:24
  54.0 1.9 %collective-permute-start.3 = (bf16[64,32,128]{2,1,0:T(8,128)(2,1)S(1)}, bf16[64,32,128]{2,1,0:T(8,128)(2,1)S(1)}, u32[]{:S(2)}, u32[]{:S(2)}) collective-permute-start(bf16[64,32,128]{2,1,0:T(8,128)(2,1)S(1)} %get-tuple-element.30), channel_id=1, source_target_pairs={{192,0},{7,1},{194,2},{1,3},{196,4},{3,5},{198,6},{5,7},{200,8},{1... | collective-permute-start | bytes 1572872 | tf_op jit(solution)/shard_map/ppermute | solution.py:24
  55.9 4.3 %collective-permute-done.1.b = bf16[64,32,128]{2,1,0:T(8,128)(2,1)S(1)} collective-permute-done((bf16[64,32,128]{2,1,0:T(8,128)(2,1)S(1)}, bf16[64,32,128]{2,1,0:T(8,128)(2,1)S(1)}, u32[]{:S(2)}, u32[]{:S(2)}) %collective-permute-start.1) | collective-permute-done | bytes 524320 | tf_op jit(solution)/shard_map/ppermute | solution.py:24
  60.1 6.6 %collective-permute-done.2.c = bf16[64,32,128]{2,1,0:T(8,128)(2,1)S(1)} collective-permute-done((bf16[64,32,128]{2,1,0:T(8,128)(2,1)S(1)}, bf16[64,32,128]{2,1,0:T(8,128)(2,1)S(1)}, u32[]{:S(2)}, u32[]{:S(2)}) %collective-permute-start.2) | collective-permute-done | bytes 524320 | tf_op jit(solution)/shard_map/ppermute | solution.py:24
  68.7 1.8 %collective-permute-start.4 = (bf16[16,32,128]{2,1,0:T(8,128)(2,1)S(1)}, bf16[16,32,128]{2,1,0:T(8,128)(2,1)S(1)}, u32[]{:S(2)}, u32[]{:S(2)}) collective-permute-start(bf16[16,32,128]{2,1,0:T(8,128)(2,1)S(1)} %get-tuple-element.32), channel_id=1, source_target_pairs={{2,0},{65,1},{4,2},{67,3},{6,4},{69,5},{0,6},{71,7},{10,8},{73,9},... | collective-permute-start | bytes 393224 | tf_op jit(solution)/shard_map/ppermute | solution.py:24
  70.8 2.1 %collective-permute-start.6 = (bf16[16,32,128]{2,1,0:T(8,128)(2,1)S(1)}, bf16[16,32,128]{2,1,0:T(8,128)(2,1)S(1)}, u32[]{:S(2)}, u32[]{:S(2)}) collective-permute-start(bf16[16,32,128]{2,1,0:T(8,128)(2,1)S(1)} %get-tuple-element.34), channel_id=1, source_target_pairs={{6,0},{193,1},{0,2},{195,3},{2,4},{197,5},{4,6},{199,7},{14,8},{20... | collective-permute-start | bytes 393224 | tf_op jit(solution)/shard_map/ppermute | solution.py:24
  72.8 3.7 %collective-permute-done.4.b = bf16[16,32,128]{2,1,0:T(8,128)(2,1)S(1)} collective-permute-done((bf16[16,32,128]{2,1,0:T(8,128)(2,1)S(1)}, bf16[16,32,128]{2,1,0:T(8,128)(2,1)S(1)}, u32[]{:S(2)}, u32[]{:S(2)}) %collective-permute-start.4) | collective-permute-done | bytes 131104 | tf_op jit(solution)/shard_map/ppermute | solution.py:24
  76.5 4.2 %collective-permute-done.5.c = bf16[16,32,128]{2,1,0:T(8,128)(2,1)S(1)} collective-permute-done((bf16[16,32,128]{2,1,0:T(8,128)(2,1)S(1)}, bf16[16,32,128]{2,1,0:T(8,128)(2,1)S(1)}, u32[]{:S(2)}, u32[]{:S(2)}) %collective-permute-start.5) | collective-permute-done | bytes 131104 | tf_op jit(solution)/shard_map/ppermute | solution.py:24
  80.7 2.1 %collective-permute-done.6.d = bf16[16,32,128]{2,1,0:T(8,128)(2,1)S(1)} collective-permute-done((bf16[16,32,128]{2,1,0:T(8,128)(2,1)S(1)}, bf16[16,32,128]{2,1,0:T(8,128)(2,1)S(1)}, u32[]{:S(2)}, u32[]{:S(2)}) %collective-permute-start.6) | collective-permute-done | bytes 131104 | tf_op jit(solution)/shard_map/ppermute | solution.py:24
  84.6 5.0 %collective-permute-start.9 = (bf16[2,32,128]{2,1,0:T(8,128)(2,1)S(1)}, bf16[2,32,128]{2,1,0:T(8,128)(2,1)S(1)}, u32[]{:S(2)}, u32[]{:S(2)}) collective-permute-start(bf16[2,32,128]{2,1,0:T(8,128)(2,1)S(1)} %get-tuple-element.38), channel_id=1, source_target_pairs={{24,0},{25,1},{26,2},{27,3},{28,4},{29,5},{30,6},{31,7},{32,8},{33... | collective-permute-start | bytes 49160 | tf_op jit(solution)/shard_map/ppermute | solution.py:24
  90.5 3.3 %collective-permute-start.11 = (bf16[2,32,128]{2,1,0:T(8,128)(2,1)S(1)}, bf16[2,32,128]{2,1,0:T(8,128)(2,1)S(1)}, u32[]{:S(2)}, u32[]{:S(2)}) collective-permute-start(bf16[2,32,128]{2,1,0:T(8,128)(2,1)S(1)} %get-tuple-element.40), channel_id=1, source_target_pairs={{40,0},{41,1},{42,2},{43,3},{44,4},{45,5},{46,6},{47,7},{48,8},{49... | collective-permute-start | bytes 49160 | tf_op jit(solution)/shard_map/ppermute | solution.py:24
  93.8 2.8 %collective-permute-start.12 = (bf16[2,32,128]{2,1,0:T(8,128)(2,1)S(1)}, bf16[2,32,128]{2,1,0:T(8,128)(2,1)S(1)}, u32[]{:S(2)}, u32[]{:S(2)}) collective-permute-start(bf16[2,32,128]{2,1,0:T(8,128)(2,1)S(1)} %get-tuple-element.41), channel_id=1, source_target_pairs={{48,0},{49,1},{50,2},{51,3},{52,4},{53,5},{54,6},{55,7},{56,8},{57... | collective-permute-start | bytes 49160 | tf_op jit(solution)/shard_map/ppermute | solution.py:24
  97.9 2.1 %collective-permute-done.12.refs_6_ = bf16[2,32,128]{2,1,0:T(8,128)(2,1)S(1)} collective-permute-done((bf16[2,32,128]{2,1,0:T(8,128)(2,1)S(1)}, bf16[2,32,128]{2,1,0:T(8,128)(2,1)S(1)}, u32[]{:S(2)}, u32[]{:S(2)}) %collective-permute-start.12) | collective-permute-done | bytes 16416 | tf_op jit(solution)/shard_map/ppermute | solution.py:24
  100.0 1.9 %collective-permute-done.13.refs_7_ = bf16[2,32,128]{2,1,0:T(8,128)(2,1)S(1)} collective-permute-done((bf16[2,32,128]{2,1,0:T(8,128)(2,1)S(1)}, bf16[2,32,128]{2,1,0:T(8,128)(2,1)S(1)}, u32[]{:S(2)}, u32[]{:S(2)}) %collective-permute-start.13) | collective-permute-done | bytes 16416 | tf_op jit(solution)/shard_map/ppermute | solution.py:24
  105.4 3.5 %collective-permute-start.15 = (f32[72,128]{1,0:T(8,128)}, f32[72,128]{1,0:T(8,128)S(1)}, u32[]{:S(2)}, u32[]{:S(2)}) collective-permute-start(f32[72,128]{1,0:T(8,128)} %sum_third.1.v0), channel_id=1, source_target_pairs={{128,0},{129,1},{130,2},{131,3},{132,4},{133,5},{134,6},{135,7},{1... | collective-permute-start | bytes 110600 | tf_op jit(solution)/shard_map/ppermute | solution.py:24
  111.1 2.0 %collective-permute-done.14.v1 = f32[72,128]{1,0:T(8,128)S(1)} collective-permute-done((f32[72,128]{1,0:T(8,128)}, f32[72,128]{1,0:T(8,128)S(1)}, u32[]{:S(2)}, u32[]{:S(2)}) %collective-permute-start.14) | collective-permute-done | bytes 36896 | tf_op jit(solution)/shard_map/ppermute | solution.py:24
  113.7 1.6 %finish.1 = f32[2,128,128]{2,1,0:T(8,128)} custom-call(s32[5]{0:T(128)} %copy-done.1, f32[72,128]{1,0:T(8,128)} %sum_third.1.v0, f32[72,128]{1,0:T(8,128)} %copy-done.7, f32[72,128]{1,0:T(8,128)} %copy-done.6, f32[72,128]{1,0:T(8,128)} %copy-done.5), custom_call_target="tpu_custom_call" | custom-call | tf_op jit(solution)/shard_map/finish/pallas_call | solution.py:227
  115.3 15.9 %products.1 = (bf16[352,512]{1,0:T(8,128)(2,1)}, bf16[352,8192]{1,0:T(8,128)(2,1)}) custom-call(s32[256]{0:T(256)} %select_reduce_fusion.inverse, s32[5]{0:T(128)} %copy-done.1, bf16[352,8192]{1,0:T(8,128)(2,1)} %x_ref.5, bf16[352,512]{1,0:T(8,128)(2,1)} %cot_ref.3, bf16[64,192,512]{2,1,0:T(8,128)(2,1)} %bitcast.5), custom_call_target="tpu_custom_call" | custom-call | flops 6000000000 | bytes 25000000 | tf_op jit(solution)/shard_map/products/pallas_call | solution.py:328
  (58 shorter events, 15.1 us)
Async XLA Ops:
  7.2 108.2 %all-gather.3.cloned.1.call-start = ((), (), s32[]{:S(2)}) async-start(), calls=%async_computation | async-start | bytes 12779520 | tf_op jit(solution)/shard_map/all_gather | solution.py:361
  10.5 72.3 %copy-start.1 = (s32[5]{0:T(128)}, s32[5]{0:T(128)S(1)}, u32[]{:S(2)}) copy-start(s32[5]{0:T(128)S(1)} %stack.19.pos) | copy-start | bytes 64
  36.7 59.9 %copy-start.2 = (s32[256]{0:T(256)}, s32[256]{0:T(256)S(1)}, u32[]{:S(2)}) copy-start(s32[256]{0:T(256)S(1)} %psum.7.ids) | copy-start | bytes 3076
  41.6 4.2 %collective-permute-start = (bf16[64,128,128]{2,1,0:T(8,128)(2,1)S(1)}, bf16[64,128,128]{2,1,0:T(8,128)(2,1)S(1)}, u32[]{:S(2)}, u32[]{:S(2)}) collective-permute-start(bf16[64,128,128]{2,1,0:T(8,128)(2,1)S(1)} %get-tuple-element.26), channel_id=1, source_target_pairs={{1,0},{0,1},{3,2},{2,3},{5,4},{4,5},{7,6},{6,7},{9,8},{8,9},{11,10... | collective-permute-start | bytes 6291464 | tf_op jit(solution)/shard_map/ppermute | solution.py:24
  50.9 9.3 %collective-permute-start.1 = (bf16[64,32,128]{2,1,0:T(8,128)(2,1)S(1)}, bf16[64,32,128]{2,1,0:T(8,128)(2,1)S(1)}, u32[]{:S(2)}, u32[]{:S(2)}) collective-permute-start(bf16[64,32,128]{2,1,0:T(8,128)(2,1)S(1)} %get-tuple-element.28), channel_id=1, source_target_pairs={{64,0},{3,1},{66,2},{5,3},{68,4},{7,5},{70,6},{1,7},{72,8},{11,9},... | collective-permute-start | bytes 1572872 | tf_op jit(solution)/shard_map/ppermute | solution.py:24
  51.4 15.4 %collective-permute-start.2 = (bf16[64,32,128]{2,1,0:T(8,128)(2,1)S(1)}, bf16[64,32,128]{2,1,0:T(8,128)(2,1)S(1)}, u32[]{:S(2)}, u32[]{:S(2)}) collective-permute-start(bf16[64,32,128]{2,1,0:T(8,128)(2,1)S(1)} %get-tuple-element.29), channel_id=1, source_target_pairs={{128,0},{5,1},{130,2},{7,3},{132,4},{1,5},{134,6},{3,7},{136,8},{1... | collective-permute-start | bytes 1572872 | tf_op jit(solution)/shard_map/ppermute | solution.py:24
  54.0 13.9 %collective-permute-start.3 = (bf16[64,32,128]{2,1,0:T(8,128)(2,1)S(1)}, bf16[64,32,128]{2,1,0:T(8,128)(2,1)S(1)}, u32[]{:S(2)}, u32[]{:S(2)}) collective-permute-start(bf16[64,32,128]{2,1,0:T(8,128)(2,1)S(1)} %get-tuple-element.30), channel_id=1, source_target_pairs={{192,0},{7,1},{194,2},{1,3},{196,4},{3,5},{198,6},{5,7},{200,8},{1... | collective-permute-start | bytes 1572872 | tf_op jit(solution)/shard_map/ppermute | solution.py:24
  68.7 7.8 %collective-permute-start.4 = (bf16[16,32,128]{2,1,0:T(8,128)(2,1)S(1)}, bf16[16,32,128]{2,1,0:T(8,128)(2,1)S(1)}, u32[]{:S(2)}, u32[]{:S(2)}) collective-permute-start(bf16[16,32,128]{2,1,0:T(8,128)(2,1)S(1)} %get-tuple-element.32), channel_id=1, source_target_pairs={{2,0},{65,1},{4,2},{67,3},{6,4},{69,5},{0,6},{71,7},{10,8},{73,9},... | collective-permute-start | bytes 393224 | tf_op jit(solution)/shard_map/ppermute | solution.py:24
  70.5 10.3 %collective-permute-start.5 = (bf16[16,32,128]{2,1,0:T(8,128)(2,1)S(1)}, bf16[16,32,128]{2,1,0:T(8,128)(2,1)S(1)}, u32[]{:S(2)}, u32[]{:S(2)}) collective-permute-start(bf16[16,32,128]{2,1,0:T(8,128)(2,1)S(1)} %get-tuple-element.33), channel_id=1, source_target_pairs={{4,0},{129,1},{6,2},{131,3},{0,4},{133,5},{2,6},{135,7},{12,8},{13... | collective-permute-start | bytes 393224 | tf_op jit(solution)/shard_map/ppermute | solution.py:24
  70.8 12.0 %collective-permute-start.6 = (bf16[16,32,128]{2,1,0:T(8,128)(2,1)S(1)}, bf16[16,32,128]{2,1,0:T(8,128)(2,1)S(1)}, u32[]{:S(2)}, u32[]{:S(2)}) collective-permute-start(bf16[16,32,128]{2,1,0:T(8,128)(2,1)S(1)} %get-tuple-element.34), channel_id=1, source_target_pairs={{6,0},{193,1},{0,2},{195,3},{2,4},{197,5},{4,6},{199,7},{14,8},{20... | collective-permute-start | bytes 393224 | tf_op jit(solution)/shard_map/ppermute | solution.py:24
  84.0 9.8 %collective-permute-start.7 = (bf16[2,32,128]{2,1,0:T(8,128)(2,1)S(1)}, bf16[2,32,128]{2,1,0:T(8,128)(2,1)S(1)}, u32[]{:S(2)}, u32[]{:S(2)}) collective-permute-start(bf16[2,32,128]{2,1,0:T(8,128)(2,1)S(1)} %get-tuple-element.36), channel_id=1, source_target_pairs={{8,0},{9,1},{10,2},{11,3},{12,4},{13,5},{14,6},{15,7},{16,8},{17,9... | collective-permute-start | bytes 49160 | tf_op jit(solution)/shard_map/ppermute | solution.py:24
  84.0 12.6 %collective-permute-start.8 = (bf16[2,32,128]{2,1,0:T(8,128)(2,1)S(1)}, bf16[2,32,128]{2,1,0:T(8,128)(2,1)S(1)}, u32[]{:S(2)}, u32[]{:S(2)}) collective-permute-start(bf16[2,32,128]{2,1,0:T(8,128)(2,1)S(1)} %get-tuple-element.37), channel_id=1, source_target_pairs={{16,0},{17,1},{18,2},{19,3},{20,4},{21,5},{22,6},{23,7},{24,8},{25... | collective-permute-start | bytes 49160 | tf_op jit(solution)/shard_map/ppermute | solution.py:24
  84.6 12.1 %collective-permute-start.9 = (bf16[2,32,128]{2,1,0:T(8,128)(2,1)S(1)}, bf16[2,32,128]{2,1,0:T(8,128)(2,1)S(1)}, u32[]{:S(2)}, u32[]{:S(2)}) collective-permute-start(bf16[2,32,128]{2,1,0:T(8,128)(2,1)S(1)} %get-tuple-element.38), channel_id=1, source_target_pairs={{24,0},{25,1},{26,2},{27,3},{28,4},{29,5},{30,6},{31,7},{32,8},{33... | collective-permute-start | bytes 49160 | tf_op jit(solution)/shard_map/ppermute | solution.py:24
  89.6 8.0 %collective-permute-start.10 = (bf16[2,32,128]{2,1,0:T(8,128)(2,1)S(1)}, bf16[2,32,128]{2,1,0:T(8,128)(2,1)S(1)}, u32[]{:S(2)}, u32[]{:S(2)}) collective-permute-start(bf16[2,32,128]{2,1,0:T(8,128)(2,1)S(1)} %get-tuple-element.39), channel_id=1, source_target_pairs={{32,0},{33,1},{34,2},{35,3},{36,4},{37,5},{38,6},{39,7},{40,8},{41... | collective-permute-start | bytes 49160 | tf_op jit(solution)/shard_map/ppermute | solution.py:24
  90.5 7.3 %collective-permute-start.11 = (bf16[2,32,128]{2,1,0:T(8,128)(2,1)S(1)}, bf16[2,32,128]{2,1,0:T(8,128)(2,1)S(1)}, u32[]{:S(2)}, u32[]{:S(2)}) collective-permute-start(bf16[2,32,128]{2,1,0:T(8,128)(2,1)S(1)} %get-tuple-element.40), channel_id=1, source_target_pairs={{40,0},{41,1},{42,2},{43,3},{44,4},{45,5},{46,6},{47,7},{48,8},{49... | collective-permute-start | bytes 49160 | tf_op jit(solution)/shard_map/ppermute | solution.py:24
  93.8 8.1 %copy-start.8 = (bf16[2,32,128]{2,1,0:T(8,128)(2,1)}, bf16[2,32,128]{2,1,0:T(8,128)(2,1)S(1)}, u32[]{:S(2)}) copy-start(bf16[2,32,128]{2,1,0:T(8,128)(2,1)S(1)} %collective-permute-done.7.refs_1_) | copy-start | bytes 49156
  93.8 6.2 %collective-permute-start.12 = (bf16[2,32,128]{2,1,0:T(8,128)(2,1)S(1)}, bf16[2,32,128]{2,1,0:T(8,128)(2,1)S(1)}, u32[]{:S(2)}, u32[]{:S(2)}) collective-permute-start(bf16[2,32,128]{2,1,0:T(8,128)(2,1)S(1)} %get-tuple-element.41), channel_id=1, source_target_pairs={{48,0},{49,1},{50,2},{51,3},{52,4},{53,5},{54,6},{55,7},{56,8},{57... | collective-permute-start | bytes 49160 | tf_op jit(solution)/shard_map/ppermute | solution.py:24
  96.6 5.3 %copy-start.9 = (bf16[2,32,128]{2,1,0:T(8,128)(2,1)}, bf16[2,32,128]{2,1,0:T(8,128)(2,1)S(1)}, u32[]{:S(2)}) copy-start(bf16[2,32,128]{2,1,0:T(8,128)(2,1)S(1)} %collective-permute-done.8.refs_2_) | copy-start | bytes 49156
  96.6 5.3 %collective-permute-start.13 = (bf16[2,32,128]{2,1,0:T(8,128)(2,1)S(1)}, bf16[2,32,128]{2,1,0:T(8,128)(2,1)S(1)}, u32[]{:S(2)}, u32[]{:S(2)}) collective-permute-start(bf16[2,32,128]{2,1,0:T(8,128)(2,1)S(1)} %get-tuple-element.42), channel_id=1, source_target_pairs={{56,0},{57,1},{58,2},{59,3},{60,4},{61,5},{62,6},{63,7},{0,8},{1,9... | collective-permute-start | bytes 49160 | tf_op jit(solution)/shard_map/ppermute | solution.py:24
  96.7 5.2 %copy-start.10 = (bf16[2,32,128]{2,1,0:T(8,128)(2,1)}, bf16[2,32,128]{2,1,0:T(8,128)(2,1)S(1)}, u32[]{:S(2)}) copy-start(bf16[2,32,128]{2,1,0:T(8,128)(2,1)S(1)} %collective-permute-done.9.refs_3_) | copy-start | bytes 49156
  97.6 4.3 %copy-start.11 = (bf16[2,32,128]{2,1,0:T(8,128)(2,1)}, bf16[2,32,128]{2,1,0:T(8,128)(2,1)S(1)}, u32[]{:S(2)}) copy-start(bf16[2,32,128]{2,1,0:T(8,128)(2,1)S(1)} %collective-permute-done.10.refs_4_) | copy-start | bytes 49156
  104.0 5.6 %collective-permute-start.16 = (f32[72,128]{1,0:T(8,128)}, f32[72,128]{1,0:T(8,128)S(1)}, u32[]{:S(2)}, u32[]{:S(2)}) collective-permute-start(f32[72,128]{1,0:T(8,128)} %sum_third.1.v0), channel_id=1, source_target_pairs={{192,0},{193,1},{194,2},{195,3},{196,4},{197,5},{198,6},{199,7},{2... | collective-permute-start | bytes 110600 | tf_op jit(solution)/shard_map/ppermute | solution.py:24
  105.4 5.7 %collective-permute-start.15 = (f32[72,128]{1,0:T(8,128)}, f32[72,128]{1,0:T(8,128)S(1)}, u32[]{:S(2)}, u32[]{:S(2)}) collective-permute-start(f32[72,128]{1,0:T(8,128)} %sum_third.1.v0), channel_id=1, source_target_pairs={{128,0},{129,1},{130,2},{131,3},{132,4},{133,5},{134,6},{135,7},{1... | collective-permute-start | bytes 110600 | tf_op jit(solution)/shard_map/ppermute | solution.py:24
  108.9 4.2 %collective-permute-start.14 = (f32[72,128]{1,0:T(8,128)}, f32[72,128]{1,0:T(8,128)S(1)}, u32[]{:S(2)}, u32[]{:S(2)}) collective-permute-start(f32[72,128]{1,0:T(8,128)} %sum_third.1.v0), channel_id=1, source_target_pairs={{64,0},{65,1},{66,2},{67,3},{68,4},{69,5},{70,6},{71,7},{72,8},{73... | collective-permute-start | bytes 110600 | tf_op jit(solution)/shard_map/ppermute | solution.py:24
  (9 other events, 17.0 us)
Sparse Core Ops, SparseCore 0:
  11.3 97.0 all-gather.2

commit v5 on v4

--- a/solution.py
+++ b/solution.py
@@ -264,10 +264,10 @@
             lanes = slice(col * 128, col * 128 + 128)
             for half in range(2):
                 at = pl.ds(pl.multiple_of((safe % 2 * 2 + half) * 128, 128), 128)
-                d = d_ref[safe // 2, :, at].astype(F32)
+                d = d_ref[safe // 2, :, at]
                 d = jnp.where(slot >= 0, d, jnp.zeros_like(d))
                 rows = slice(half * 64, half * 64 + 64)
-                e_ref[j, rows, lanes] = (w_ref[tile, rows, lanes].astype(F32) + d).astype(BF16)
+                e_ref[j, rows, lanes] = w_ref[tile, rows, lanes] + d
 
 
 def products_kernel(inverse, pos, x_ref, cot_ref, all_ref, proj_ref, grad_ref, w_ref, d_ref, m_ref, acc_ref, e0, e1, wsem, dsem):

time: 138 us -> 137 us (level)
  Pallas kernels: 32 us -> 30.4 us
  transfers between devices with their start and end apart: 18 -> 18, of which waited for: 13 -> 12; matrix products, arithmetic and copies ran while one was open for 1% -> 1% of each run, Pallas kernels for 10% -> 10%
where the time goes in v5:
time: 137 us
  waiting for transfers between devices  34.8 us (25%)
  Pallas kernels  30.4 us (22%)
  starting transfers between devices  26.8 us (20%)
  blocking collectives  22.6 us (16%)
  between operations  14.9 us (11%)
  local copies, waits for them, and re-layouts  6.42 us (5%)
    ppermute x17, waiting for transfers between devices, fetch(): return lax.ppermute(v, ('dp', 'fsdp'), pairs)  34.8 us
    ppermute x17, starting transfers between devices, fetch(): return lax.ppermute(v, ('dp', 'fsdp'), pairs)  26.8 us
    psum x1, blocking collectives, per_device(): ids = lax.psum(here, 'fsdp')  22.6 us
    pallas_call x1, Pallas kernels, products(): pl.pallas_call(products_kernel, grid=(width // wide,), out_shape=[jax.Sha...  15.7 us
    unnamed x30, local copies, waits for them, and re-layouts  5.45 us
    pallas_call x1, Pallas kernels, grads_away(): pl.pallas_call(grads_away_kernel, out_shape=[jax.ShapeDtypeStruct((OWNERS...  4.54 us
    pallas_call x1, Pallas kernels, grads_home(): pl.pallas_call(grads_home_kernel, out_shape=[jax.ShapeDtypeStruct((OWNERS...  4.01 us
  transfers between devices with their start and end apart: 18, of which 12 were waited for; matrix products, arithmetic and copies ran while one was open for 1% of the time, Pallas kernels for 10%

profile of v5, /device:TPU:10, one launch (start us, length us, event | category | flops | bytes accessed | tf_op | source)
XLA Modules:
  0.0 136.5 jit_solution(9805841468636470826)
XLA Ops:
  7.2 1.6 %pack.1 = bf16[192,512]{1,0:T(8,128)(2,1)} custom-call(bf16[128,512]{1,0:T(8,128)(2,1)} %frozen_ref.1, bf16[2,128,128]{2,1,0:T(8,128)(2,1)} %delta_ref.1), custom_call_target="tpu_custom_call" | custom-call | tf_op jit(solution)/shard_map/pack/pallas_call | solution.py:246
  10.5 22.6 %psum.7.ids = s32[256]{0:T(256)S(1)} all-reduce(s32[256]{0:T(256)S(1)} %constant_dynamic-update-slice_fusion), channel_id=1, replica_groups=mesh['dp'=4,'fsdp'=64] {'fsdp'}, use_global_device_ids=true, to_apply=%region_0.0 | all-reduce | flops 256 | bytes 2048 | tf_op jit(solution)/shard_map/psum | solution.py:365
  33.1 2.6 %copy-done.3 = bf16[352,8192]{1,0:T(8,128)(2,1)S(1)} copy-done((bf16[352,8192]{1,0:T(8,128)(2,1)S(1)}, bf16[352,8192]{1,0:T(8,128)(2,1)}, u32[]{:S(2)}) %copy-start.3) | copy-done | bytes 5767192
  36.7 4.5 %grads_away.1 = (bf16[64,128,128]{2,1,0:T(8,128)(2,1)S(1)}, bf16[512,352]{1,0:T(8,128)(2,1)S(1)}) custom-call(s32[256]{0:T(256)S(1)} %psum.7.ids, s32[5]{0:T(128)S(1)} %stack.19.pos, bf16[352,8192]{1,0:T(8,128)(2,1)S(1)} %copy-done.3, bf16[352,512]{1,0:T(8,128)(2,1)S(1)} %copy-done.4), custom_call_target="tpu_custom_call" | custom-call | flops 3000000000 | bytes 8000000 | tf_op jit(solution)/shard_map/grads_away/pallas_call | solution.py:120
  41.4 4.1 %collective-permute-done.r_ref = bf16[64,128,128]{2,1,0:T(8,128)(2,1)S(1)} collective-permute-done((bf16[64,128,128]{2,1,0:T(8,128)(2,1)S(1)}, bf16[64,128,128]{2,1,0:T(8,128)(2,1)S(1)}, u32[]{:S(2)}, u32[]{:S(2)}) %collective-permute-start) | collective-permute-done | bytes 2097184 | tf_op jit(solution)/shard_map/ppermute | solution.py:24
  45.5 4.0 %grads_home.1 = (f32[64,32,128]{2,1,0:T(8,128)S(1)}, bf16[64,32,128]{2,1,0:T(8,128)(2,1)S(1)}, bf16[64,32,128]{2,1,0:T(8,128)(2,1)S(1)}, bf16[64,32,128]{2,1,0:T(8,128)(2,1)S(1)}) custom-call(s32[256]{0:T(256)S(1)} %psum.7.ids, s32[5]{0:T(128)S(1)} %stack.19.pos, bf16[352,8192]{1,0:T(8,128)(2,1)S(1)} %copy-done.3, ...), custom_call_target="tpu_custom_call" | custom-call | flops 3000000000 | bytes 10000000 | tf_op jit(solution)/shard_map/grads_home/pallas_call | solution.py:136
  50.0 2.6 %collective-permute-start.2 = (bf16[64,32,128]{2,1,0:T(8,128)(2,1)S(1)}, bf16[64,32,128]{2,1,0:T(8,128)(2,1)S(1)}, u32[]{:S(2)}, u32[]{:S(2)}) collective-permute-start(bf16[64,32,128]{2,1,0:T(8,128)(2,1)S(1)} %get-tuple-element.29), channel_id=1, source_target_pairs={{128,0},{5,1},{130,2},{7,3},{132,4},{1,5},{134,6},{3,7},{136,8},{1... | collective-permute-start | bytes 1572872 | tf_op jit(solution)/shard_map/ppermute | solution.py:24
  52.6 1.9 %collective-permute-start.3 = (bf16[64,32,128]{2,1,0:T(8,128)(2,1)S(1)}, bf16[64,32,128]{2,1,0:T(8,128)(2,1)S(1)}, u32[]{:S(2)}, u32[]{:S(2)}) collective-permute-start(bf16[64,32,128]{2,1,0:T(8,128)(2,1)S(1)} %get-tuple-element.30), channel_id=1, source_target_pairs={{192,0},{7,1},{194,2},{1,3},{196,4},{3,5},{198,6},{5,7},{200,8},{1... | collective-permute-start | bytes 1572872 | tf_op jit(solution)/shard_map/ppermute | solution.py:24
  54.5 4.3 %collective-permute-done.1.b = bf16[64,32,128]{2,1,0:T(8,128)(2,1)S(1)} collective-permute-done((bf16[64,32,128]{2,1,0:T(8,128)(2,1)S(1)}, bf16[64,32,128]{2,1,0:T(8,128)(2,1)S(1)}, u32[]{:S(2)}, u32[]{:S(2)}) %collective-permute-start.1) | collective-permute-done | bytes 524320 | tf_op jit(solution)/shard_map/ppermute | solution.py:24
  58.8 6.6 %collective-permute-done.2.c = bf16[64,32,128]{2,1,0:T(8,128)(2,1)S(1)} collective-permute-done((bf16[64,32,128]{2,1,0:T(8,128)(2,1)S(1)}, bf16[64,32,128]{2,1,0:T(8,128)(2,1)S(1)}, u32[]{:S(2)}, u32[]{:S(2)}) %collective-permute-start.2) | collective-permute-done | bytes 524320 | tf_op jit(solution)/shard_map/ppermute | solution.py:24
  67.3 1.8 %collective-permute-start.4 = (bf16[16,32,128]{2,1,0:T(8,128)(2,1)S(1)}, bf16[16,32,128]{2,1,0:T(8,128)(2,1)S(1)}, u32[]{:S(2)}, u32[]{:S(2)}) collective-permute-start(bf16[16,32,128]{2,1,0:T(8,128)(2,1)S(1)} %get-tuple-element.32), channel_id=1, source_target_pairs={{2,0},{65,1},{4,2},{67,3},{6,4},{69,5},{0,6},{71,7},{10,8},{73,9},... | collective-permute-start | bytes 393224 | tf_op jit(solution)/shard_map/ppermute | solution.py:24
  69.4 2.1 %collective-permute-start.6 = (bf16[16,32,128]{2,1,0:T(8,128)(2,1)S(1)}, bf16[16,32,128]{2,1,0:T(8,128)(2,1)S(1)}, u32[]{:S(2)}, u32[]{:S(2)}) collective-permute-start(bf16[16,32,128]{2,1,0:T(8,128)(2,1)S(1)} %get-tuple-element.34), channel_id=1, source_target_pairs={{6,0},{193,1},{0,2},{195,3},{2,4},{197,5},{4,6},{199,7},{14,8},{20... | collective-permute-start | bytes 393224 | tf_op jit(solution)/shard_map/ppermute | solution.py:24
  71.5 3.7 %collective-permute-done.4.b = bf16[16,32,128]{2,1,0:T(8,128)(2,1)S(1)} collective-permute-done((bf16[16,32,128]{2,1,0:T(8,128)(2,1)S(1)}, bf16[16,32,128]{2,1,0:T(8,128)(2,1)S(1)}, u32[]{:S(2)}, u32[]{:S(2)}) %collective-permute-start.4) | collective-permute-done | bytes 131104 | tf_op jit(solution)/shard_map/ppermute | solution.py:24
  75.2 4.2 %collective-permute-done.5.c = bf16[16,32,128]{2,1,0:T(8,128)(2,1)S(1)} collective-permute-done((bf16[16,32,128]{2,1,0:T(8,128)(2,1)S(1)}, bf16[16,32,128]{2,1,0:T(8,128)(2,1)S(1)}, u32[]{:S(2)}, u32[]{:S(2)}) %collective-permute-start.5) | collective-permute-done | bytes 131104 | tf_op jit(solution)/shard_map/ppermute | solution.py:24
  79.4 2.1 %collective-permute-done.6.d = bf16[16,32,128]{2,1,0:T(8,128)(2,1)S(1)} collective-permute-done((bf16[16,32,128]{2,1,0:T(8,128)(2,1)S(1)}, bf16[16,32,128]{2,1,0:T(8,128)(2,1)S(1)}, u32[]{:S(2)}, u32[]{:S(2)}) %collective-permute-start.6) | collective-permute-done | bytes 131104 | tf_op jit(solution)/shard_map/ppermute | solution.py:24
  83.2 5.0 %collective-permute-start.9 = (bf16[2,32,128]{2,1,0:T(8,128)(2,1)S(1)}, bf16[2,32,128]{2,1,0:T(8,128)(2,1)S(1)}, u32[]{:S(2)}, u32[]{:S(2)}) collective-permute-start(bf16[2,32,128]{2,1,0:T(8,128)(2,1)S(1)} %get-tuple-element.38), channel_id=1, source_target_pairs={{24,0},{25,1},{26,2},{27,3},{28,4},{29,5},{30,6},{31,7},{32,8},{33... | collective-permute-start | bytes 49160 | tf_op jit(solution)/shard_map/ppermute | solution.py:24
  89.2 3.3 %collective-permute-start.11 = (bf16[2,32,128]{2,1,0:T(8,128)(2,1)S(1)}, bf16[2,32,128]{2,1,0:T(8,128)(2,1)S(1)}, u32[]{:S(2)}, u32[]{:S(2)}) collective-permute-start(bf16[2,32,128]{2,1,0:T(8,128)(2,1)S(1)} %get-tuple-element.40), channel_id=1, source_target_pairs={{40,0},{41,1},{42,2},{43,3},{44,4},{45,5},{46,6},{47,7},{48,8},{49... | collective-permute-start | bytes 49160 | tf_op jit(solution)/shard_map/ppermute | solution.py:24
  92.5 2.8 %collective-permute-start.12 = (bf16[2,32,128]{2,1,0:T(8,128)(2,1)S(1)}, bf16[2,32,128]{2,1,0:T(8,128)(2,1)S(1)}, u32[]{:S(2)}, u32[]{:S(2)}) collective-permute-start(bf16[2,32,128]{2,1,0:T(8,128)(2,1)S(1)} %get-tuple-element.41), channel_id=1, source_target_pairs={{48,0},{49,1},{50,2},{51,3},{52,4},{53,5},{54,6},{55,7},{56,8},{57... | collective-permute-start | bytes 49160 | tf_op jit(solution)/shard_map/ppermute | solution.py:24
  96.3 2.3 %collective-permute-done.12.refs_6_ = bf16[2,32,128]{2,1,0:T(8,128)(2,1)S(1)} collective-permute-done((bf16[2,32,128]{2,1,0:T(8,128)(2,1)S(1)}, bf16[2,32,128]{2,1,0:T(8,128)(2,1)S(1)}, u32[]{:S(2)}, u32[]{:S(2)}) %collective-permute-start.12) | collective-permute-done | bytes 16416 | tf_op jit(solution)/shard_map/ppermute | solution.py:24
  98.6 1.9 %collective-permute-done.13.refs_7_ = bf16[2,32,128]{2,1,0:T(8,128)(2,1)S(1)} collective-permute-done((bf16[2,32,128]{2,1,0:T(8,128)(2,1)S(1)}, bf16[2,32,128]{2,1,0:T(8,128)(2,1)S(1)}, u32[]{:S(2)}, u32[]{:S(2)}) %collective-permute-start.13) | collective-permute-done | bytes 16416 | tf_op jit(solution)/shard_map/ppermute | solution.py:24
  104.1 3.5 %collective-permute-start.15 = (f32[72,128]{1,0:T(8,128)}, f32[72,128]{1,0:T(8,128)S(1)}, u32[]{:S(2)}, u32[]{:S(2)}) collective-permute-start(f32[72,128]{1,0:T(8,128)} %sum_third.1.v0), channel_id=1, source_target_pairs={{128,0},{129,1},{130,2},{131,3},{132,4},{133,5},{134,6},{135,7},{1... | collective-permute-start | bytes 110600 | tf_op jit(solution)/shard_map/ppermute | solution.py:24
  109.7 2.0 %collective-permute-done.14.v1 = f32[72,128]{1,0:T(8,128)S(1)} collective-permute-done((f32[72,128]{1,0:T(8,128)}, f32[72,128]{1,0:T(8,128)S(1)}, u32[]{:S(2)}, u32[]{:S(2)}) %collective-permute-start.14) | collective-permute-done | bytes 36896 | tf_op jit(solution)/shard_map/ppermute | solution.py:24
  112.4 1.6 %finish.1 = f32[2,128,128]{2,1,0:T(8,128)} custom-call(s32[5]{0:T(128)} %copy-done.1, f32[72,128]{1,0:T(8,128)} %sum_third.1.v0, f32[72,128]{1,0:T(8,128)} %copy-done.7, f32[72,128]{1,0:T(8,128)} %copy-done.6, f32[72,128]{1,0:T(8,128)} %copy-done.5), custom_call_target="tpu_custom_call" | custom-call | tf_op jit(solution)/shard_map/finish/pallas_call | solution.py:227
  114.0 15.7 %products.1 = (bf16[352,512]{1,0:T(8,128)(2,1)}, bf16[352,8192]{1,0:T(8,128)(2,1)}) custom-call(s32[256]{0:T(256)} %select_reduce_fusion.inverse, s32[5]{0:T(128)} %copy-done.1, bf16[352,8192]{1,0:T(8,128)(2,1)} %x_ref.5, bf16[352,512]{1,0:T(8,128)(2,1)} %cot_ref.3, bf16[64,192,512]{2,1,0:T(8,128)(2,1)} %bitcast.5), custom_call_target="tpu_custom_call" | custom-call | flops 6000000000 | bytes 25000000 | tf_op jit(solution)/shard_map/products/pallas_call | solution.py:328
  (58 shorter events, 14.8 us)
Async XLA Ops:
  7.2 106.8 %all-gather.3.cloned.1.call-start = ((), (), s32[]{:S(2)}) async-start(), calls=%async_computation | async-start | bytes 12779520 | tf_op jit(solution)/shard_map/all_gather | solution.py:361
  10.5 70.9 %copy-start.1 = (s32[5]{0:T(128)}, s32[5]{0:T(128)S(1)}, u32[]{:S(2)}) copy-start(s32[5]{0:T(128)S(1)} %stack.19.pos) | copy-start | bytes 64
  36.7 58.6 %copy-start.2 = (s32[256]{0:T(256)}, s32[256]{0:T(256)S(1)}, u32[]{:S(2)}) copy-start(s32[256]{0:T(256)S(1)} %psum.7.ids) | copy-start | bytes 3076
  41.3 4.2 %collective-permute-start = (bf16[64,128,128]{2,1,0:T(8,128)(2,1)S(1)}, bf16[64,128,128]{2,1,0:T(8,128)(2,1)S(1)}, u32[]{:S(2)}, u32[]{:S(2)}) collective-permute-start(bf16[64,128,128]{2,1,0:T(8,128)(2,1)S(1)} %get-tuple-element.26), channel_id=1, source_target_pairs={{1,0},{0,1},{3,2},{2,3},{5,4},{4,5},{7,6},{6,7},{9,8},{8,9},{11,10... | collective-permute-start | bytes 6291464 | tf_op jit(solution)/shard_map/ppermute | solution.py:24
  49.5 9.3 %collective-permute-start.1 = (bf16[64,32,128]{2,1,0:T(8,128)(2,1)S(1)}, bf16[64,32,128]{2,1,0:T(8,128)(2,1)S(1)}, u32[]{:S(2)}, u32[]{:S(2)}) collective-permute-start(bf16[64,32,128]{2,1,0:T(8,128)(2,1)S(1)} %get-tuple-element.28), channel_id=1, source_target_pairs={{64,0},{3,1},{66,2},{5,3},{68,4},{7,5},{70,6},{1,7},{72,8},{11,9},... | collective-permute-start | bytes 1572872 | tf_op jit(solution)/shard_map/ppermute | solution.py:24
  50.0 15.4 %collective-permute-start.2 = (bf16[64,32,128]{2,1,0:T(8,128)(2,1)S(1)}, bf16[64,32,128]{2,1,0:T(8,128)(2,1)S(1)}, u32[]{:S(2)}, u32[]{:S(2)}) collective-permute-start(bf16[64,32,128]{2,1,0:T(8,128)(2,1)S(1)} %get-tuple-element.29), channel_id=1, source_target_pairs={{128,0},{5,1},{130,2},{7,3},{132,4},{1,5},{134,6},{3,7},{136,8},{1... | collective-permute-start | bytes 1572872 | tf_op jit(solution)/shard_map/ppermute | solution.py:24
  52.6 13.9 %collective-permute-start.3 = (bf16[64,32,128]{2,1,0:T(8,128)(2,1)S(1)}, bf16[64,32,128]{2,1,0:T(8,128)(2,1)S(1)}, u32[]{:S(2)}, u32[]{:S(2)}) collective-permute-start(bf16[64,32,128]{2,1,0:T(8,128)(2,1)S(1)} %get-tuple-element.30), channel_id=1, source_target_pairs={{192,0},{7,1},{194,2},{1,3},{196,4},{3,5},{198,6},{5,7},{200,8},{1... | collective-permute-start | bytes 1572872 | tf_op jit(solution)/shard_map/ppermute | solution.py:24
  67.3 7.8 %collective-permute-start.4 = (bf16[16,32,128]{2,1,0:T(8,128)(2,1)S(1)}, bf16[16,32,128]{2,1,0:T(8,128)(2,1)S(1)}, u32[]{:S(2)}, u32[]{:S(2)}) collective-permute-start(bf16[16,32,128]{2,1,0:T(8,128)(2,1)S(1)} %get-tuple-element.32), channel_id=1, source_target_pairs={{2,0},{65,1},{4,2},{67,3},{6,4},{69,5},{0,6},{71,7},{10,8},{73,9},... | collective-permute-start | bytes 393224 | tf_op jit(solution)/shard_map/ppermute | solution.py:24
  69.1 10.3 %collective-permute-start.5 = (bf16[16,32,128]{2,1,0:T(8,128)(2,1)S(1)}, bf16[16,32,128]{2,1,0:T(8,128)(2,1)S(1)}, u32[]{:S(2)}, u32[]{:S(2)}) collective-permute-start(bf16[16,32,128]{2,1,0:T(8,128)(2,1)S(1)} %get-tuple-element.33), channel_id=1, source_target_pairs={{4,0},{129,1},{6,2},{131,3},{0,4},{133,5},{2,6},{135,7},{12,8},{13... | collective-permute-start | bytes 393224 | tf_op jit(solution)/shard_map/ppermute | solution.py:24
  69.4 12.0 %collective-permute-start.6 = (bf16[16,32,128]{2,1,0:T(8,128)(2,1)S(1)}, bf16[16,32,128]{2,1,0:T(8,128)(2,1)S(1)}, u32[]{:S(2)}, u32[]{:S(2)}) collective-permute-start(bf16[16,32,128]{2,1,0:T(8,128)(2,1)S(1)} %get-tuple-element.34), channel_id=1, source_target_pairs={{6,0},{193,1},{0,2},{195,3},{2,4},{197,5},{4,6},{199,7},{14,8},{20... | collective-permute-start | bytes 393224 | tf_op jit(solution)/shard_map/ppermute | solution.py:24
  82.7 9.8 %collective-permute-start.7 = (bf16[2,32,128]{2,1,0:T(8,128)(2,1)S(1)}, bf16[2,32,128]{2,1,0:T(8,128)(2,1)S(1)}, u32[]{:S(2)}, u32[]{:S(2)}) collective-permute-start(bf16[2,32,128]{2,1,0:T(8,128)(2,1)S(1)} %get-tuple-element.36), channel_id=1, source_target_pairs={{8,0},{9,1},{10,2},{11,3},{12,4},{13,5},{14,6},{15,7},{16,8},{17,9... | collective-permute-start | bytes 49160 | tf_op jit(solution)/shard_map/ppermute | solution.py:24
  82.7 12.6 %collective-permute-start.8 = (bf16[2,32,128]{2,1,0:T(8,128)(2,1)S(1)}, bf16[2,32,128]{2,1,0:T(8,128)(2,1)S(1)}, u32[]{:S(2)}, u32[]{:S(2)}) collective-permute-start(bf16[2,32,128]{2,1,0:T(8,128)(2,1)S(1)} %get-tuple-element.37), channel_id=1, source_target_pairs={{16,0},{17,1},{18,2},{19,3},{20,4},{21,5},{22,6},{23,7},{24,8},{25... | collective-permute-start | bytes 49160 | tf_op jit(solution)/shard_map/ppermute | solution.py:24
  83.2 12.1 %collective-permute-start.9 = (bf16[2,32,128]{2,1,0:T(8,128)(2,1)S(1)}, bf16[2,32,128]{2,1,0:T(8,128)(2,1)S(1)}, u32[]{:S(2)}, u32[]{:S(2)}) collective-permute-start(bf16[2,32,128]{2,1,0:T(8,128)(2,1)S(1)} %get-tuple-element.38), channel_id=1, source_target_pairs={{24,0},{25,1},{26,2},{27,3},{28,4},{29,5},{30,6},{31,7},{32,8},{33... | collective-permute-start | bytes 49160 | tf_op jit(solution)/shard_map/ppermute | solution.py:24
  88.3 8.0 %collective-permute-start.10 = (bf16[2,32,128]{2,1,0:T(8,128)(2,1)S(1)}, bf16[2,32,128]{2,1,0:T(8,128)(2,1)S(1)}, u32[]{:S(2)}, u32[]{:S(2)}) collective-permute-start(bf16[2,32,128]{2,1,0:T(8,128)(2,1)S(1)} %get-tuple-element.39), channel_id=1, source_target_pairs={{32,0},{33,1},{34,2},{35,3},{36,4},{37,5},{38,6},{39,7},{40,8},{41... | collective-permute-start | bytes 49160 | tf_op jit(solution)/shard_map/ppermute | solution.py:24
  89.2 7.1 %collective-permute-start.11 = (bf16[2,32,128]{2,1,0:T(8,128)(2,1)S(1)}, bf16[2,32,128]{2,1,0:T(8,128)(2,1)S(1)}, u32[]{:S(2)}, u32[]{:S(2)}) collective-permute-start(bf16[2,32,128]{2,1,0:T(8,128)(2,1)S(1)} %get-tuple-element.40), channel_id=1, source_target_pairs={{40,0},{41,1},{42,2},{43,3},{44,4},{45,5},{46,6},{47,7},{48,8},{49... | collective-permute-start | bytes 49160 | tf_op jit(solution)/shard_map/ppermute | solution.py:24
  92.5 8.1 %copy-start.8 = (bf16[2,32,128]{2,1,0:T(8,128)(2,1)}, bf16[2,32,128]{2,1,0:T(8,128)(2,1)S(1)}, u32[]{:S(2)}) copy-start(bf16[2,32,128]{2,1,0:T(8,128)(2,1)S(1)} %collective-permute-done.7.refs_1_) | copy-start | bytes 49156
  92.5 6.2 %collective-permute-start.12 = (bf16[2,32,128]{2,1,0:T(8,128)(2,1)S(1)}, bf16[2,32,128]{2,1,0:T(8,128)(2,1)S(1)}, u32[]{:S(2)}, u32[]{:S(2)}) collective-permute-start(bf16[2,32,128]{2,1,0:T(8,128)(2,1)S(1)} %get-tuple-element.41), channel_id=1, source_target_pairs={{48,0},{49,1},{50,2},{51,3},{52,4},{53,5},{54,6},{55,7},{56,8},{57... | collective-permute-start | bytes 49160 | tf_op jit(solution)/shard_map/ppermute | solution.py:24
  95.3 5.3 %copy-start.9 = (bf16[2,32,128]{2,1,0:T(8,128)(2,1)}, bf16[2,32,128]{2,1,0:T(8,128)(2,1)S(1)}, u32[]{:S(2)}) copy-start(bf16[2,32,128]{2,1,0:T(8,128)(2,1)S(1)} %collective-permute-done.8.refs_2_) | copy-start | bytes 49156
  95.3 5.3 %collective-permute-start.13 = (bf16[2,32,128]{2,1,0:T(8,128)(2,1)S(1)}, bf16[2,32,128]{2,1,0:T(8,128)(2,1)S(1)}, u32[]{:S(2)}, u32[]{:S(2)}) collective-permute-start(bf16[2,32,128]{2,1,0:T(8,128)(2,1)S(1)} %get-tuple-element.42), channel_id=1, source_target_pairs={{56,0},{57,1},{58,2},{59,3},{60,4},{61,5},{62,6},{63,7},{0,8},{1,9... | collective-permute-start | bytes 49160 | tf_op jit(solution)/shard_map/ppermute | solution.py:24
  95.3 5.2 %copy-start.10 = (bf16[2,32,128]{2,1,0:T(8,128)(2,1)}, bf16[2,32,128]{2,1,0:T(8,128)(2,1)S(1)}, u32[]{:S(2)}) copy-start(bf16[2,32,128]{2,1,0:T(8,128)(2,1)S(1)} %collective-permute-done.9.refs_3_) | copy-start | bytes 49156
  96.3 4.3 %copy-start.12 = (bf16[2,32,128]{2,1,0:T(8,128)(2,1)}, bf16[2,32,128]{2,1,0:T(8,128)(2,1)S(1)}, u32[]{:S(2)}) copy-start(bf16[2,32,128]{2,1,0:T(8,128)(2,1)S(1)} %collective-permute-done.11.refs_5_) | copy-start | bytes 49156
  102.6 5.6 %collective-permute-start.16 = (f32[72,128]{1,0:T(8,128)}, f32[72,128]{1,0:T(8,128)S(1)}, u32[]{:S(2)}, u32[]{:S(2)}) collective-permute-start(f32[72,128]{1,0:T(8,128)} %sum_third.1.v0), channel_id=1, source_target_pairs={{192,0},{193,1},{194,2},{195,3},{196,4},{197,5},{198,6},{199,7},{2... | collective-permute-start | bytes 110600 | tf_op jit(solution)/shard_map/ppermute | solution.py:24
  104.1 5.7 %collective-permute-start.15 = (f32[72,128]{1,0:T(8,128)}, f32[72,128]{1,0:T(8,128)S(1)}, u32[]{:S(2)}, u32[]{:S(2)}) collective-permute-start(f32[72,128]{1,0:T(8,128)} %sum_third.1.v0), channel_id=1, source_target_pairs={{128,0},{129,1},{130,2},{131,3},{132,4},{133,5},{134,6},{135,7},{1... | collective-permute-start | bytes 110600 | tf_op jit(solution)/shard_map/ppermute | solution.py:24
  107.6 4.2 %collective-permute-start.14 = (f32[72,128]{1,0:T(8,128)}, f32[72,128]{1,0:T(8,128)S(1)}, u32[]{:S(2)}, u32[]{:S(2)}) collective-permute-start(f32[72,128]{1,0:T(8,128)} %sum_third.1.v0), channel_id=1, source_target_pairs={{64,0},{65,1},{66,2},{67,3},{68,4},{69,5},{70,6},{71,7},{72,8},{73... | collective-permute-start | bytes 110600 | tf_op jit(solution)/shard_map/ppermute | solution.py:24
  (9 other events, 17.2 us)
Sparse Core Ops, SparseCore 0:
  11.3 96.7 all-gather.2
